TPU v7x, 32 devices: a whole 2x2x4 slice. The times are simulated.
32 devices in a mesh: dp: 4 (over x, core), ctx: 8 (over z, y).
Axes of the slice: x: 2, y: 2, z: 4, core: 2. Of those that a mesh axis runs over, the one named last changes fastest.
Arguments:
- tokens: bfloat16 [4, 8, 2, 64, 2048], P('dp', 'ctx'), may hold values from -6 to 6
- cotangent: bfloat16 [4, 8, 2, 64, 2048], P('dp', 'ctx'), may hold values from -6 to 6
- w_qkv: bfloat16 [2048, 6144], P('dp'), may hold values from -0.125 to 0.125
- b_qkv: bfloat16 [6144], P('dp'), may hold values from -0.119628906 to 0.119628906
- w_out: bfloat16 [2048, 2048], P('dp'), may hold values from -3 to 3
- w_gate: bfloat16 [2048, 5632], P('dp'), may hold values from -0.125 to 0.125
- w_up: bfloat16 [2048, 5632], P('dp'), may hold values from -0.125 to 0.125
- w_down: bfloat16 [5632, 2048], P('dp'), may hold values from -0.078125 to 0.078125
- norms: bfloat16 [4, 2048], P(None, 'dp'), may hold values from -1 to 2, as said below
Outputs:
- output: bfloat16 [4, 8, 2, 64, 2048], P('dp', 'ctx')
- tokens_grad: float32 [4, 8, 2, 64, 2048], P('dp', 'ctx')
- w_qkv_grad: float32 [2048, 6144], P(('dp', 'ctx'))
- b_qkv_grad: float32 [6144], P(('dp', 'ctx'))
- w_out_grad: float32 [2048, 2048], P(('dp', 'ctx'))
- w_gate_grad: float32 [2048, 5632], P(('dp', 'ctx'))
- w_up_grad: float32 [2048, 5632], P(('dp', 'ctx'))
- w_down_grad: float32 [5632, 2048], P(('dp', 'ctx'))
- norms_grad: float32 [4, 2048], P(None, ('dp', 'ctx'))
Inputs may be any that keep to these rules, and one draw needn't show every extreme that they name: `norms`: rows 0 and 2 lie near one, rows 1 and 3 near zero.
All inputs are finite; a program needn't handle non-finite values.
Results may differ from a plain program's by a relative error of at most 0.014.
Values may be sent and summed in bfloat16 or wider, within the bound.
A program may use at most 448 MiB of HBM per device.

v0:
```python
import math

import jax
import jax.numpy as jnp
from jax import lax
from jax.sharding import PartitionSpec as P

HEADS = 32
HDIM = 64
ROT = 16


def normalize_rows(field):
    centre = field - jnp.mean(field, axis=-1, keepdims=True)
    inverse_deviation = lax.rsqrt(jnp.mean(centre * centre, axis=-1, keepdims=True) + 1e-05)
    return (centre * inverse_deviation, inverse_deviation)


def layer_norm_reverse(incoming_gradient, norm_gain, centered_scaled, inverse_deviation):
    inner_product = incoming_gradient * norm_gain
    return inverse_deviation * (
        inner_product
        - jnp.mean(inner_product, axis=-1, keepdims=True)
        - centered_scaled * jnp.mean(inner_product * centered_scaled, axis=-1, keepdims=True)
    )


def place_of(device, parts, half, offset):
    return jnp.where(
        offset < half, device * half + offset, (2 * parts - 1 - device) * half + offset - half
    )


def rotary_table(positions):
    pairs = ROT // 2
    inverse = jnp.power(10000.0, -jnp.arange(pairs, dtype=jnp.float32) / pairs)
    angle = positions.astype(jnp.float32)[:, None] * inverse[None, :]
    return (jnp.cos(angle)[:, None, :], jnp.sin(angle)[:, None, :])


def rotate(field, cosine, sine):
    pairs = ROT // 2
    first = field[..., :pairs]
    second = field[..., pairs:ROT]
    return jnp.concatenate(
        [first * cosine - second * sine, second * cosine + first * sine, field[..., ROT:]], axis=-1
    )


def unrotate(incoming_gradient, cosine, sine):
    pairs = ROT // 2
    first = incoming_gradient[..., :pairs]
    second = incoming_gradient[..., pairs:ROT]
    return jnp.concatenate(
        [
            first * cosine + second * sine,
            second * cosine - first * sine,
            incoming_gradient[..., ROT:],
        ],
        axis=-1,
    )


def shards(tokens, cotangent, w_qkv, b_qkv, w_out, w_gate, w_up, w_down, norms):
    width = tokens.shape[-1]
    half = tokens.shape[3]
    rows = 2 * half
    parts = lax.axis_size("ctx")
    place = lax.axis_index("ctx")
    f32 = jnp.float32
    brain_float_sixteen = jnp.bfloat16
    input_rows = tokens.reshape(rows, width).astype(f32)
    output_gradient_rows = cotangent.reshape(rows, width).astype(f32)
    offsets = jnp.arange(rows, dtype=jnp.int32)
    own_pos = place_of(place, parts, half, offsets)
    full = (
        lax.all_gather(w_qkv, "dp", axis=0, tiled=True),
        lax.all_gather(b_qkv, "dp", axis=0, tiled=True),
        lax.all_gather(w_out, "dp", axis=0, tiled=True),
        lax.all_gather(norms, "dp", axis=1, tiled=True),
        lax.all_gather(w_gate, "dp", axis=0, tiled=True),
        lax.all_gather(w_up, "dp", axis=0, tiled=True),
        lax.all_gather(w_down, "dp", axis=0, tiled=True),
    )
    full_bias = full[1]
    norm_gains = full[3].astype(f32)
    first_centered_scaled, first_inverse_deviation = normalize_rows(input_rows)
    first_hidden_narrow = (first_centered_scaled * norm_gains[0] + norm_gains[1]).astype(
        brain_float_sixteen
    )
    qkv = jnp.dot(first_hidden_narrow, full[0], preferred_element_type=f32) + full_bias.astype(f32)
    cosine, sine = rotary_table(own_pos)
    query = (
        rotate(qkv[:, :width].reshape(rows, HEADS, HDIM), cosine, sine)
        .astype(brain_float_sixteen)
        .reshape(rows, width)
    )
    key_own = (
        rotate(qkv[:, width : 2 * width].reshape(rows, HEADS, HDIM), cosine, sine)
        .astype(brain_float_sixteen)
        .reshape(rows, width)
    )
    value_own = qkv[:, 2 * width :].astype(brain_float_sixteen)
    keys_all, values_all = (
        lax.all_gather(key_own, "ctx", axis=0, tiled=True),
        lax.all_gather(value_own, "ctx", axis=0, tiled=True),
    )
    count = keys_all.shape[0]
    gathered = jnp.arange(count, dtype=jnp.int32)
    key_pos = place_of(gathered // rows, parts, half, gathered % rows)
    allowed = (key_pos[None, :] <= own_pos[:, None])[None]
    groups = math.gcd(HEADS, 8)
    per_group = HEADS // groups
    span = per_group * HDIM

    def group_scores(start):
        q_part = lax.dynamic_slice_in_dim(query, start, span, 1).reshape(rows, per_group, HDIM)
        k_part = lax.dynamic_slice_in_dim(keys_all, start, span, 1).reshape(count, per_group, HDIM)
        v_part = lax.dynamic_slice_in_dim(values_all, start, span, 1).reshape(
            count, per_group, HDIM
        )
        scores = jnp.einsum("qhd,khd->hqk", q_part, k_part, preferred_element_type=f32) * 0.125
        return (q_part, k_part, v_part, jnp.where(allowed, scores, -1e30))

    def forward_group(index, carry):
        mixed_acc, lse_acc = carry
        start = index * span
        q_part, k_part, v_part, scores = group_scores(start)
        top = jnp.max(scores, axis=-1)
        expo = jnp.exp(scores - top[..., None])
        total = jnp.sum(expo, axis=-1)
        probs = (expo / total[..., None]).astype(brain_float_sixteen)
        mixed = jnp.einsum("hqk,khd->qhd", probs, v_part, preferred_element_type=f32).reshape(
            rows, span
        )
        mixed_acc = lax.dynamic_update_slice_in_dim(mixed_acc, mixed, start, 1)
        lse_acc = lax.dynamic_update_slice_in_dim(
            lse_acc, top + jnp.log(total), index * per_group, 0
        )
        return (mixed_acc, lse_acc)

    mixed, lse = lax.fori_loop(
        0, groups, forward_group, (jnp.zeros((rows, width), f32), jnp.zeros((HEADS, rows), f32))
    )
    mixed_b = mixed.astype(brain_float_sixteen)
    first_residual = input_rows + jnp.dot(mixed_b, full[2], preferred_element_type=f32)
    second_centered_scaled, second_inverse_deviation = normalize_rows(first_residual)
    second_hidden_narrow = (second_centered_scaled * norm_gains[2] + norm_gains[3]).astype(
        brain_float_sixteen
    )
    gate = jnp.dot(second_hidden_narrow, full[4], preferred_element_type=f32)
    up = jnp.dot(second_hidden_narrow, full[5], preferred_element_type=f32)
    sig = jax.nn.sigmoid(gate)
    hidden_b = (gate * sig * up).astype(brain_float_sixteen)
    result = first_residual + jnp.dot(hidden_b, full[6], preferred_element_type=f32)
    dyb = output_gradient_rows.astype(brain_float_sixteen)
    back = (
        lax.all_gather(w_qkv, "dp", axis=0, tiled=True),
        lax.all_gather(w_out, "dp", axis=0, tiled=True),
        lax.all_gather(w_gate, "dp", axis=0, tiled=True),
        lax.all_gather(w_up, "dp", axis=0, tiled=True),
        lax.all_gather(w_down, "dp", axis=0, tiled=True),
    )
    grad_down = jnp.einsum("rf,rd->fd", hidden_b, dyb, preferred_element_type=f32)
    d_hidden = jnp.einsum("rd,fd->rf", dyb, back[4], preferred_element_type=f32)
    d_gate = (d_hidden * up * sig * (1.0 + gate * (1.0 - sig))).astype(brain_float_sixteen)
    d_up = (d_hidden * gate * sig).astype(brain_float_sixteen)
    grad_gate = jnp.einsum("rd,rf->df", second_hidden_narrow, d_gate, preferred_element_type=f32)
    grad_up = jnp.einsum("rd,rf->df", second_hidden_narrow, d_up, preferred_element_type=f32)
    second_hidden_gradient = jnp.einsum("rf,df->rd", d_gate, back[2], preferred_element_type=f32)
    second_hidden_gradient = second_hidden_gradient + jnp.einsum(
        "rf,df->rd", d_up, back[3], preferred_element_type=f32
    )
    second_gain_gradient = jnp.sum(second_hidden_gradient * second_centered_scaled, axis=0)
    shift2_grad = jnp.sum(second_hidden_gradient, axis=0)
    first_residual_gradient = output_gradient_rows + layer_norm_reverse(
        second_hidden_gradient, norm_gains[2], second_centered_scaled, second_inverse_deviation
    )
    d_attn = first_residual_gradient.astype(brain_float_sixteen)
    grad_out = jnp.einsum("rd,re->de", mixed_b, d_attn, preferred_element_type=f32)
    d_mixed = jnp.einsum("re,de->rd", d_attn, back[1], preferred_element_type=f32).astype(
        brain_float_sixteen
    )

    def backward_group(index, carry):
        dq_acc, dk_acc, dv_acc = carry
        start = index * span
        q_part, k_part, v_part, scores = group_scores(start)
        lse_part = lax.dynamic_slice_in_dim(lse, index * per_group, per_group, 0)
        probs = jnp.exp(scores - lse_part[..., None])
        dout = lax.dynamic_slice_in_dim(d_mixed, start, span, 1).reshape(rows, per_group, HDIM)
        d_probs = jnp.einsum("qhd,khd->hqk", dout, v_part, preferred_element_type=f32)
        centre = jnp.sum(probs * d_probs, axis=-1, keepdims=True)
        d_scores = (probs * (d_probs - centre)).astype(brain_float_sixteen)
        dq = jnp.einsum("hqk,khd->qhd", d_scores, k_part, preferred_element_type=f32) * 0.125
        dk = jnp.einsum("hqk,qhd->khd", d_scores, q_part, preferred_element_type=f32) * 0.125
        dv = jnp.einsum(
            "hqk,qhd->khd", probs.astype(brain_float_sixteen), dout, preferred_element_type=f32
        )
        dq_acc = lax.dynamic_update_slice_in_dim(dq_acc, dq.reshape(rows, span), start, 1)
        dk_acc = lax.dynamic_update_slice_in_dim(dk_acc, dk.reshape(count, span), start, 1)
        dv_acc = lax.dynamic_update_slice_in_dim(dv_acc, dv.reshape(count, span), start, 1)
        return (dq_acc, dk_acc, dv_acc)

    empty_keys = jnp.zeros((count, width), f32)
    d_query, d_keys, d_values = lax.fori_loop(
        0, groups, backward_group, (jnp.zeros((rows, width), f32), empty_keys, empty_keys)
    )
    d_key_own, d_value_own = (
        lax.psum_scatter(
            d_keys.astype(jnp.bfloat16), "ctx", scatter_dimension=0, tiled=True
        ).astype(jnp.float32),
        lax.psum_scatter(
            d_values.astype(jnp.bfloat16), "ctx", scatter_dimension=0, tiled=True
        ).astype(jnp.float32),
    )
    d_query = unrotate(d_query.reshape(rows, HEADS, HDIM), cosine, sine).reshape(rows, width)
    d_key_own = unrotate(d_key_own.reshape(rows, HEADS, HDIM), cosine, sine).reshape(rows, width)
    d_qkv = jnp.concatenate([d_query, d_key_own, d_value_own], axis=1).astype(brain_float_sixteen)
    grad_bias = jnp.sum(d_qkv.astype(f32), axis=0)
    grad_qkv = jnp.einsum("rd,re->de", first_hidden_narrow, d_qkv, preferred_element_type=f32)
    first_hidden_gradient = jnp.einsum("re,de->rd", d_qkv, back[0], preferred_element_type=f32)
    first_gain_gradient = jnp.sum(first_hidden_gradient * first_centered_scaled, axis=0)
    shift1_grad = jnp.sum(first_hidden_gradient, axis=0)
    input_gradient = first_residual_gradient + layer_norm_reverse(
        first_hidden_gradient, norm_gains[0], first_centered_scaled, first_inverse_deviation
    )
    norm_grads = jnp.stack(
        [first_gain_gradient, shift1_grad, second_gain_gradient, shift2_grad], axis=0
    )
    owned = (
        lax.psum_scatter(grad_qkv, ("dp", "ctx"), scatter_dimension=0, tiled=True),
        lax.psum_scatter(grad_bias, ("dp", "ctx"), scatter_dimension=0, tiled=True),
        lax.psum_scatter(grad_out, ("dp", "ctx"), scatter_dimension=0, tiled=True),
        lax.psum_scatter(grad_gate, ("dp", "ctx"), scatter_dimension=0, tiled=True),
        lax.psum_scatter(grad_up, ("dp", "ctx"), scatter_dimension=0, tiled=True),
        lax.psum_scatter(grad_down, ("dp", "ctx"), scatter_dimension=0, tiled=True),
        lax.psum_scatter(norm_grads, ("dp", "ctx"), scatter_dimension=1, tiled=True),
    )
    qkv_owned, bias_owned, out_owned, gate_owned, up_owned, down_owned, norms_owned = owned
    output = result.astype(brain_float_sixteen).reshape(tokens.shape)
    tokens_grad = input_gradient.reshape(tokens.shape)
    return (
        output,
        tokens_grad,
        qkv_owned,
        bias_owned,
        out_owned,
        gate_owned,
        up_owned,
        down_owned,
        norms_owned,
    )


def solution(mesh):
    placed = (
        P("dp", "ctx", None, None, None),
        P("dp", "ctx", None, None, None),
        P("dp", None),
        P("dp"),
        P("dp", None),
        P("dp", None),
        P("dp", None),
        P("dp", None),
        P(None, "dp"),
    )
    return jax.shard_map(
        shards,
        mesh=mesh,
        in_specs=placed,
        out_specs=(
            P("dp", "ctx", None, None, None),
            P("dp", "ctx", None, None, None),
            P(("dp", "ctx"), None),
            P(("dp", "ctx")),
            P(("dp", "ctx"), None),
            P(("dp", "ctx"), None),
            P(("dp", "ctx"), None),
            P(("dp", "ctx"), None),
            P(None, ("dp", "ctx")),
        ),
        check_vma=False,
    )
```

profile of v0, /device:TPU:0, one launch (start us, length us, event | category | flops | bytes accessed | tf_op | source)
XLA Modules:
  0.0 5006.2 jit_solution(16834388638528498729)
XLA Ops:
  8.9 6.2 all-gather
  15.1 5.4 all_gather.32
  21.0 146.2 %all-gather.9.cloned.1.call-done = bf16[2048,6144]{1,0:T(8,128)(2,1)} async-done(((bf16[512,6144]{1,0:T(8,128)(2,1)}), bf16[2048,6144]{1,0:T(8,128)(2,1)}) %all-gather.9.cloned.1.call-update) | async-done | bytes 25165840 | tf_op jit(solution)/shard_map/all_gather | solution.py:77
  167.2 10.0 convolution_add_fusion
  177.2 1.7 copy-done.6
  180.0 1.7 fusion.36
  192.3 61.1 %all-gather.11.cloned.1.call-done = bf16[1024,2048]{1,0:T(8,128)(2,1)} async-done(((bf16[128,2048]{1,0:T(8,128)(2,1)}), bf16[1024,2048]{1,0:T(8,128)(2,1)}) %all-gather.11.cloned.1.call-update) | async-done | bytes 4194320 | tf_op jit(solution)/shard_map/all_gather | solution.py:106
  253.3 6.4 copy.41
  259.7 69.5 %all-gather.13.cloned.1.call-done = bf16[1024,2048]{0,1:T(8,128)(2,1)} async-done(((bf16[128,2048]{0,1:T(8,128)(2,1)}), bf16[1024,2048]{0,1:T(8,128)(2,1)}) %all-gather.13.cloned.1.call-update) | async-done | bytes 4194320 | tf_op jit(solution)/shard_map/all_gather | solution.py:105
  329.3 39.4 while.34
  334.1 1.4 constant_dynamic-slice_fusion.15
  339.1 1.6 constant_dynamic-slice_fusion.15
  368.7 18.5 all-gather.15.cloned.1.call-done
  387.2 4.9 fusion.38
  392.7 139.2 %all-gather.17.cloned.1.call-done = bf16[2048,5632]{1,0:T(8,128)(2,1)} async-done(((bf16[512,5632]{1,0:T(8,128)(2,1)}), bf16[2048,5632]{1,0:T(8,128)(2,1)}) %all-gather.17.cloned.1.call-update) | async-done | bytes 23068688 | tf_op jit(solution)/shard_map/all_gather | solution.py:81
  531.9 12.7 fusion.40
  544.6 131.9 %all-gather.19.cloned.1.call-done = bf16[2048,5632]{1,0:T(8,128)(2,1)} async-done(((bf16[512,5632]{1,0:T(8,128)(2,1)}), bf16[2048,5632]{1,0:T(8,128)(2,1)}) %all-gather.19.cloned.1.call-update) | async-done | bytes 23068688 | tf_op jit(solution)/shard_map/all_gather | solution.py:82
  676.5 12.7 fusion.41
  689.2 132.1 %all-gather.21.cloned.1.call-done = bf16[5632,2048]{1,0:T(8,128)(2,1)} async-done(((bf16[1408,2048]{1,0:T(8,128)(2,1)}), bf16[5632,2048]{1,0:T(8,128)(2,1)}) %all-gather.21.cloned.1.call-update) | async-done | bytes 23068688 | tf_op jit(solution)/shard_map/all_gather | solution.py:83
  821.3 15.4 multiply_convert_fusion.1
  836.7 13.5 fusion.42
  850.2 12.7 multiply_reduce_fusion.1
  863.5 7.5 convolution_convert_fusion
  871.0 2.5 broadcast_in_dim.87
  873.5 2.5 broadcast_in_dim.87.clone
  877.0 70.7 %while.35 = (s32[]{:T(128)}, f32[128,2048]{0,1:T(8,128)}, bf16[1024,2048]{0,1:T(8,128)(2,1)}, bf16[1024,2048]{0,1:T(8,128)(2,1)}, bf16[1024,2048]{0,1:T(8,128)(2...) while((s32[]{:T(128)}, f32[128,2048]{0,1:T(8,128)}, ...), condition=%wide.region_12.13_spmd.clone, body=%wide.region_10.12_spmd.clone.sunk | while | flops 340950528 | bytes 23870228 | solution.py:206
  947.7 6.6 copy.44
  954.4 6.5 copy.46
  961.0 1.4 copy-done.17
  962.4 79.9 %reduce-scatter.25.cloned.1.call-done = bf16[128,2048]{1,0:T(8,128)(2,1)} async-done(((bf16[1024,2048]{1,0:T(8,128)(2,1)}), bf16[128,2048]{1,0:T(8,128)(2,1)}) %reduce-scatter.25.cloned.1.call-update) | async-done | bytes 524304
  1042.4 1.3 copy.45
  1044.1 90.0 %reduce-scatter.27.cloned.1.call-done = bf16[128,2048]{1,0:T(8,128)(2,1)} async-done(((bf16[1024,2048]{1,0:T(8,128)(2,1)}), bf16[128,2048]{1,0:T(8,128)(2,1)}) %reduce-scatter.27.cloned.1.call-update) | async-done | bytes 524304
  1136.3 20.7 multiply_reduce_fusion.2
  1157.0 1.4 copy.48
  1158.8 9.2 fusion.13
  1169.1 20.7 fusion.33
  1189.8 19.2 fusion.43
  1209.1 19.2 fusion.44
  1229.4 19.2 fusion.45
  1249.8 12.1 fusion.11
  1262.5 40.7 all-reduce
  1303.8 2.6 multiply_add_fusion
  1306.4 1.4 copy.49
  1307.8 343.2 %reduce-scatter.17.cloned.1.call-done = f32[64,2048]{1,0:T(8,128)} async-done(((f32[2048,2048]{1,0:T(8,128)}), f32[64,2048]{1,0:T(8,128)}) %reduce-scatter.17.cloned.1.call-update) | async-done | bytes 524304 | tf_op jit(solution)/shard_map/reduce_scatter | solution.py:234
  1651.0 438.7 %reduce-scatter.15.cloned.1.call-done = f32[64,6144]{1,0:T(8,128)} async-done(((f32[2048,6144]{1,0:T(8,128)}), f32[64,6144]{1,0:T(8,128)}) %reduce-scatter.15.cloned.1.call-update) | async-done | bytes 1572880 | tf_op jit(solution)/shard_map/reduce_scatter | solution.py:232
  2089.7 969.4 %reduce-scatter.19.cloned.1.call-done = f32[64,5632]{1,0:T(8,128)} async-done(((f32[2048,5632]{1,0:T(8,128)}), f32[64,5632]{1,0:T(8,128)}) %reduce-scatter.19.cloned.1.call-update) | async-done | bytes 1441808 | tf_op jit(solution)/shard_map/reduce_scatter | solution.py:235
  3059.1 970.2 %reduce-scatter.21.cloned.1.call-done = f32[64,5632]{1,0:T(8,128)} async-done(((f32[2048,5632]{1,0:T(8,128)}), f32[64,5632]{1,0:T(8,128)}) %reduce-scatter.21.cloned.1.call-update) | async-done | bytes 1441808 | tf_op jit(solution)/shard_map/reduce_scatter | solution.py:236
  4029.3 970.2 %reduce-scatter.23.cloned.1.call-done = f32[176,2048]{1,0:T(8,128)} async-done(((f32[5632,2048]{1,0:T(8,128)}), f32[176,2048]{1,0:T(8,128)}) %reduce-scatter.23.cloned.1.call-update) | async-done | bytes 1441808 | tf_op jit(solution)/shard_map/reduce_scatter | solution.py:237
  (310 shorter events, 129.7 us)
Async XLA Ops:
  7.2 1.0 copy-start.4
  7.2 1.7 copy-start.23
  7.2 7.9 copy-start.22
  7.2 159.9 %all-gather.9.cloned.1.call-start = ((), (), s32[]{:S(2)}) async-start(), calls=%async_computation.8 | async-start | bytes 31457280 | tf_op jit(solution)/shard_map/all_gather | solution.py:77
  7.9 245.4 %all-gather.11.cloned.1.call-start = ((), (), s32[]{:S(2)}) async-start(), calls=%async_computation.9 | async-start | bytes 4718592 | tf_op jit(solution)/shard_map/all_gather | solution.py:106
  8.5 168.7 %copy-start.24 = (f32[128]{0:T(128)}, f32[128]{0:T(128)S(1)}, u32[]{:S(2)}) copy-start(f32[128]{0:T(128)S(1)} %div.61) | copy-start | bytes 1540
  8.9 168.3 %copy-start.26 = (f32[128]{0:T(128)}, f32[128]{0:T(128)S(1)}, u32[]{:S(2)}) copy-start(f32[128]{0:T(128)S(1)} %rsqrt.20) | copy-start | bytes 1540
  20.5 156.6 %copy-start.20 = (f32[1,2048]{1,0:T(1,128)}, f32[1,2048]{1,0:T(1,128)S(1)}, u32[]{:S(2)}) copy-start(f32[1,2048]{1,0:T(1,128)S(1)} %get-tuple-element.484) | copy-start | bytes 24580
  20.9 156.2 %copy-start.8 = (bf16[128,2048]{1,0:T(8,128)(2,1)}, bf16[128,2048]{1,0:T(8,128)(2,1)S(1)}, u32[]{:S(2)}) copy-start(bf16[128,2048]{1,0:T(8,128)(2,1)S(1)} %add_convert_fusion.1) | copy-start | bytes 1572868
  177.2 1.7 copy-start.6
  179.8 149.5 %all-gather.13.cloned.1.call-start = ((), (), s32[]{:S(2)}) async-start(), calls=%async_computation.10 | async-start | bytes 4718592 | tf_op jit(solution)/shard_map/all_gather | solution.py:105
  183.0 2.5 copy-start.16
  187.4 199.8 %all-gather.15.cloned.1.call-start = ((), (), s32[]{:S(2)}) async-start(), calls=%async_computation.11 | async-start | bytes 10485760 | tf_op jit(solution)/shard_map/all_gather | solution.py:79
  188.0 343.9 %all-gather.17.cloned.1.call-start = ((), (), s32[]{:S(2)}) async-start(), calls=%async_computation.12 | async-start | bytes 28835840 | tf_op jit(solution)/shard_map/all_gather | solution.py:81
  188.6 487.9 %all-gather.19.cloned.1.call-start = ((), (), s32[]{:S(2)}) async-start(), calls=%async_computation.13 | async-start | bytes 28835840 | tf_op jit(solution)/shard_map/all_gather | solution.py:82
  189.2 632.2 %all-gather.21.cloned.1.call-start = ((), (), s32[]{:S(2)}) async-start(), calls=%async_computation.14 | async-start | bytes 28835840 | tf_op jit(solution)/shard_map/all_gather | solution.py:83
  189.9 852.4 %reduce-scatter.25.cloned.1.call-start = ((), (), s32[]{:S(2)}) async-start(), calls=%async_computation.20 | async-start | bytes 4718592
  392.1 470.8 %copy-start = (f32[128,2048]{1,0:T(8,128)}, f32[128,2048]{1,0:T(8,128)S(1)}, u32[]{:S(2)}) copy-start(f32[128,2048]{1,0:T(8,128)S(1)} %get-tuple-element.493) | copy-start | bytes 3145732
  836.7 13.5 copy-start.7
  850.2 12.7 copy-start.18
  863.5 7.5 copy-start.2
  954.3 179.8 %reduce-scatter.27.cloned.1.call-start = ((), (), s32[]{:S(2)}) async-start(), calls=%async_computation.21 | async-start | bytes 4718592
  960.9 1.5 copy-start.17
  960.9 345.5 %reduce-scatter.29.cloned.1.call-start = ((), (), s32[]{:S(2)}) async-start(), calls=%async_computation.22 | async-start | bytes 1081344
  1043.7 92.6 %copy-start.5 = (bf16[1,1,2,64,2048]{4,3,2,1,0:T(8,128)(2,1)S(1)}, bf16[1,1,2,64,2048]{4,3,2,1,0:T(8,128)(2,1)}, u32[]{:S(2)}) copy-start(bf16[1,1,2,64,2048]{4,3,2,1,0:T(8,128)(2,1)} %param.13) | copy-start | bytes 1572868
  1043.7 92.6 %copy-start.21 = (f32[1,2048]{1,0:T(1,128)S(1)}, f32[1,2048]{1,0:T(1,128)}, u32[]{:S(2)}) copy-start(f32[1,2048]{1,0:T(1,128)} %copy-done.20) | copy-start | bytes 24580
  1043.7 92.6 %copy-start.25 = (f32[128]{0:T(128)S(1)}, f32[128]{0:T(128)}, u32[]{:S(2)}) copy-start(f32[128]{0:T(128)} %copy-done.24) | copy-start | bytes 1540
  1043.7 92.5 %copy-start.27 = (f32[128]{0:T(128)S(1)}, f32[128]{0:T(128)}, u32[]{:S(2)}) copy-start(f32[128]{0:T(128)} %copy-done.26) | copy-start | bytes 1540
  1044.0 124.1 %copy-start.10 = (bf16[128,32,64]{0,2,1:T(8,128)(2,1)}, bf16[128,32,64]{0,2,1:T(8,128)(2,1)S(1)}, u32[]{:S(2)}) copy-start(bf16[128,32,64]{0,2,1:T(8,128)(2,1)S(1)} %pad_maximum_fusion.3) | copy-start | bytes 1572868
  1044.1 112.8 %copy-start.12 = (bf16[128,32,64]{0,2,1:T(8,128)(2,1)}, bf16[128,32,64]{0,2,1:T(8,128)(2,1)S(1)}, u32[]{:S(2)}) copy-start(bf16[128,32,64]{0,2,1:T(8,128)(2,1)S(1)} %pad_maximum_fusion.4) | copy-start | bytes 1572868
  1135.4 0.8 copy-start.14
  1156.9 1.9 copy-start.3
  1158.4 492.6 %reduce-scatter.17.cloned.1.call-start = ((), (), s32[]{:S(2)}) async-start(), calls=%async_computation.16 | async-start | bytes 17301504 | tf_op jit(solution)/shard_map/reduce_scatter | solution.py:234
  1168.0 1.0 copy-start.9
  1168.0 921.7 %reduce-scatter.15.cloned.1.call-start = ((), (), s32[]{:S(2)}) async-start(), calls=%async_computation.15 | async-start | bytes 51904512 | tf_op jit(solution)/shard_map/reduce_scatter | solution.py:232
  1189.7 1869.4 %reduce-scatter.19.cloned.1.call-start = ((), (), s32[]{:S(2)}) async-start(), calls=%async_computation.17 | async-start | bytes 47579136 | tf_op jit(solution)/shard_map/reduce_scatter | solution.py:235
  1209.1 2820.3 %reduce-scatter.21.cloned.1.call-start = ((), (), s32[]{:S(2)}) async-start(), calls=%async_computation.18 | async-start | bytes 47579136 | tf_op jit(solution)/shard_map/reduce_scatter | solution.py:236
  1228.3 1.0 copy-start.19
  1228.4 3771.2 %reduce-scatter.23.cloned.1.call-start = ((), (), s32[]{:S(2)}) async-start(), calls=%async_computation.19 | async-start | bytes 47579136 | tf_op jit(solution)/shard_map/reduce_scatter | solution.py:237
  1248.6 1.2 copy-start.1
  1249.8 12.1 copy-start.11
  1249.8 12.1 copy-start.13
  1249.8 12.1 copy-start.15
Sparse Core Ops, SparseCore 0:
  9.6 157.4 all-gather.8
  179.9 73.3 all-gather.10
  256.0 73.2 all-gather.12
  330.7 56.4 all-gather.14
  388.6 143.2 all-gather.16
  533.3 143.2 all-gather.18
  678.1 143.2 all-gather.20
  954.4 87.8 reduce-scatter.24
  1046.4 87.6 reduce-scatter.26
  1158.5 134.7 reduce-scatter.28
  1296.3 354.6 reduce-scatter.16
  1659.0 430.6 reduce-scatter.14
  2092.7 966.3 reduce-scatter.18
  3062.0 967.3 reduce-scatter.20
  4032.2 967.3 reduce-scatter.22
where the time goes:
time: 5010 us
  waiting for transfers between devices  4560 us (91%)
  matrix products  240 us (5%)
  local copies, waits for them, and re-layouts  114 us (2%)
  blocking collectives  52.2 us (1%)
    reduce_scatter x1, waiting for transfers between devices, shards(): lax.psum_scatter(grad_up, ('dp', 'ctx'), scatter_dimension=0, tiled=True)  970 us
    reduce_scatter x1, waiting for transfers between devices, shards(): lax.psum_scatter(grad_down, ('dp', 'ctx'), scatter_dimension=0, tiled=True)  970 us
    reduce_scatter x1, waiting for transfers between devices, shards(): lax.psum_scatter(grad_gate, ('dp', 'ctx'), scatter_dimension=0, tiled=True)  969 us
    reduce_scatter x1, waiting for transfers between devices, shards(): lax.psum_scatter(grad_qkv, ('dp', 'ctx'), scatter_dimension=0, tiled=True)  439 us
    reduce_scatter x1, waiting for transfers between devices, shards(): lax.psum_scatter(grad_out, ('dp', 'ctx'), scatter_dimension=0, tiled=True)  343 us
    unnamed x18, waiting for transfers between devices  173 us
    all_gather x1, waiting for transfers between devices, shards(): lax.all_gather(w_qkv, 'dp', axis=0, tiled=True)  146 us
    all_gather x1, waiting for transfers between devices, shards(): lax.all_gather(w_gate, 'dp', axis=0, tiled=True)  139 us
  transfers between devices with their start and end apart: 15, of which 14 were waited for; matrix products, arithmetic and copies ran while one was open for 4% of the time, Pallas kernels for 0%

commit v1 on v0

v1 whole, which is shorter than its diff:
```python
import jax
import jax.numpy as jnp
from jax import lax
from jax.experimental import pallas as pl
from jax.experimental.pallas import tpu as pltpu
from jax.sharding import PartitionSpec as P

HEADS = 32
HDIM = 64
ROT = 16
MESH = pl.DeviceIdType.MESH
F32 = jnp.float32
BF16 = jnp.bfloat16
VMEM_BYTES = 56 * 1024 * 1024


def normalize_rows(field):
    centre = field - jnp.mean(field, axis=-1, keepdims=True)
    inverse = lax.rsqrt(jnp.mean(centre * centre, axis=-1, keepdims=True) + 1e-05)
    return (centre * inverse, inverse)


def norm_reverse(incoming, gain, scaled, inverse):
    inner = incoming * gain
    return inverse * (
        inner
        - jnp.mean(inner, axis=-1, keepdims=True)
        - scaled * jnp.mean(inner * scaled, axis=-1, keepdims=True)
    )


def rotary_factors(positions):
    pairs = ROT // 2
    inverse = jnp.power(10000.0, -jnp.arange(pairs, dtype=F32) / pairs)
    angle = positions.astype(F32)[:, None] * inverse[None, :]
    cosine, sine = jnp.cos(angle), jnp.sin(angle)
    rows = positions.shape[0]
    none = jnp.zeros((rows, HDIM - ROT), F32)
    blank = jnp.zeros((rows, pairs), F32)
    keep = jnp.concatenate([cosine, cosine, none + 1.0], axis=1)
    left = jnp.concatenate([-sine, blank, none], axis=1)
    right = jnp.concatenate([blank, sine, none], axis=1)
    return keep, left, right


def turn(field, factors, sign):
    keep, left, right = factors
    heads = field.shape[-1] // HDIM
    pairs = ROT // 2
    keep, left, right = (jnp.tile(t, (1, heads)) for t in (keep, left, right))
    return (
        field * keep
        + jnp.roll(field, -pairs, axis=-1) * (left * sign)
        + jnp.roll(field, pairs, axis=-1) * (right * sign)
    )


def exchange(axis, size, cid, items):
    counts = [len(plan(0, 0)) for _, _, plan in items]
    total = sum(counts)

    def body(*refs):
        ins = refs[: len(items)]
        outs = refs[len(items) : 2 * len(items)]
        send, recv, local = refs[2 * len(items) :]
        me = lax.axis_index(axis)
        barrier = pltpu.get_barrier_semaphore()
        for k in range(1, size):
            pl.semaphore_signal(
                barrier, inc=1, device_id={axis: lax.rem(me + k, size)}, device_id_type=MESH
            )
        pl.semaphore_wait(barrier, size - 1)
        copies = []
        for k in range(1, size):
            peer = lax.rem(me + k, size)
            at = 0
            for (_, _, plan), src, dst in zip(items, ins, outs):
                for a, b in plan(me, peer):
                    copy = pltpu.make_async_remote_copy(
                        src_ref=src.at[a],
                        dst_ref=dst.at[b],
                        send_sem=send.at[k - 1, at],
                        recv_sem=recv.at[k - 1, at],
                        device_id={axis: peer},
                        device_id_type=MESH,
                    )
                    copy.start()
                    copies.append(copy)
                    at += 1
        at = 0
        for (_, _, plan), src, dst in zip(items, ins, outs):
            for a, b in plan(me, me):
                copy = pltpu.make_async_copy(src.at[a], dst.at[b], local.at[at])
                copy.start()
                copies.append(copy)
                at += 1
        for copy in copies:
            copy.wait()

    anywhere = pl.BlockSpec(memory_space=pl.ANY)
    return pl.pallas_call(
        body,
        out_shape=[jax.ShapeDtypeStruct(shape, x.dtype) for x, shape, _ in items],
        in_specs=[anywhere] * len(items),
        out_specs=[anywhere] * len(items),
        scratch_shapes=[
            pltpu.SemaphoreType.DMA((size - 1, total)),
            pltpu.SemaphoreType.DMA((size - 1, total)),
            pltpu.SemaphoreType.DMA((total,)),
        ],
        compiler_params=pltpu.CompilerParams(collective_id=cid, has_side_effects=True),
    )(*[x for x, _, _ in items])


def gather(axis, size, cid, *arrays):
    return exchange(
        axis,
        size,
        cid,
        [(x, (size,) + x.shape, lambda me, peer: [(slice(None), me)]) for x in arrays],
    )


def swap_blocks(axis, size, cid, x):
    return exchange(axis, size, cid, [(x, x.shape, lambda me, peer: [(peer, me)])])[0]


def to_sequence(size, cid, x):
    half = x.shape[1] // 2

    def plan(me, peer):
        return [
            ((peer, pl.ds(0, half)), me),
            ((peer, pl.ds(half, half)), 2 * size - 1 - me),
        ]

    return exchange("ctx", size, cid, [(x, (2 * size, half, x.shape[2]), plan)])[0]


def from_sequence(size, cid, x):
    half = x.shape[1]

    def plan(me, peer):
        return [
            (peer, (me, pl.ds(0, half))),
            (2 * size - 1 - peer, (me, pl.ds(half, half))),
        ]

    return exchange("ctx", size, cid, [(x, (size, 2 * half, x.shape[2]), plan)])[0]


def last_dims(a, b):
    return lax.dot_general(a, b, (((1,), (1,)), ((), ())), preferred_element_type=F32)


def first_dims(a, b):
    return lax.dot_general(a, b, (((0,), (0,)), ((), ())), preferred_element_type=F32)


def plain(a, b):
    return lax.dot_general(a, b, (((1,), (0,)), ((), ())), preferred_element_type=F32)


def attention_shapes(length):
    block = min(256, length)
    segments = min(4, length // block)
    return block, segments, length // block // segments


def head_columns(heads, what, head):
    at = (what * heads + head) * HDIM
    return slice(at, at + HDIM)


def causal(scores, first_query):
    keys = lax.broadcasted_iota(jnp.int32, scores.shape, 0)
    queries = lax.broadcasted_iota(jnp.int32, scores.shape, 1) + first_query
    return jnp.where(keys <= queries, scores, -1e30)


def attention_forward(qkv, heads):
    length = qkv.shape[0]
    block, segments, inner = attention_shapes(length)

    def body(x_ref, o_ref, lse_ref):
        for head in range(heads):
            q_at, k_at, v_at = (head_columns(heads, i, head) for i in range(3))
            for segment in range(segments):
                count = (segment + 1) * inner * block
                keys = x_ref[:count, k_at]
                values = x_ref[:count, v_at]

                def step(i, _):
                    start = pl.multiple_of((segment * inner + i) * block, block)
                    query = x_ref[pl.ds(start, block), q_at] * 0.125
                    scores = causal(last_dims(keys, query), start)
                    top = jnp.max(scores, axis=0, keepdims=True)
                    expo = jnp.exp(scores - top)
                    total = jnp.sum(expo, axis=0, keepdims=True)
                    mixed = first_dims(values, expo.astype(BF16)) / total
                    o_ref[pl.ds(start, block), head * HDIM : (head + 1) * HDIM] = mixed.T.astype(
                        BF16
                    )
                    lse_ref[head : head + 1, pl.ds(start, block)] = top + jnp.log(total)
                    return 0

                if inner == 1:
                    step(0, 0)
                else:
                    lax.fori_loop(0, inner, step, 0)

    return pl.pallas_call(
        body,
        out_shape=[
            jax.ShapeDtypeStruct((length, heads * HDIM), BF16),
            jax.ShapeDtypeStruct((heads, length), F32),
        ],
        compiler_params=pltpu.CompilerParams(vmem_limit_bytes=VMEM_BYTES),
    )(qkv)


def attention_backward(qkv, lse, d_mixed, heads):
    length = qkv.shape[0]
    block, segments, inner = attention_shapes(length)

    def body(x_ref, lse_ref, do_ref, d_ref):
        d_ref[...] = jnp.zeros_like(d_ref)
        for head in range(heads):
            q_at, k_at, v_at = (head_columns(heads, i, head) for i in range(3))
            o_at = slice(head * HDIM, (head + 1) * HDIM)
            for segment in range(segments):
                count = (segment + 1) * inner * block
                keys = x_ref[:count, k_at]
                values = x_ref[:count, v_at]

                def step(i, _):
                    start = pl.multiple_of((segment * inner + i) * block, block)
                    query = x_ref[pl.ds(start, block), q_at] * 0.125
                    dout = do_ref[pl.ds(start, block), o_at]
                    scores = causal(last_dims(keys, query), start)
                    probs = jnp.exp(scores - lse_ref[head : head + 1, pl.ds(start, block)])
                    d_probs = last_dims(values, dout)
                    centre = jnp.sum(probs * d_probs, axis=0, keepdims=True)
                    d_scores = (probs * (d_probs - centre)).astype(BF16)
                    d_ref[:count, v_at] += plain(probs.astype(BF16), dout)
                    d_ref[:count, k_at] += plain(d_scores, query)
                    d_ref[pl.ds(start, block), q_at] = first_dims(keys, d_scores).T * 0.125
                    return 0

                if inner == 1:
                    step(0, 0)
                else:
                    lax.fori_loop(0, inner, step, 0)

    return pl.pallas_call(
        body,
        out_shape=jax.ShapeDtypeStruct(qkv.shape, F32),
        compiler_params=pltpu.CompilerParams(vmem_limit_bytes=VMEM_BYTES),
    )(qkv, lse, d_mixed)


def take(x, index):
    return lax.dynamic_index_in_dim(x, index, 0, keepdims=False)


def shards(tokens, cotangent, w_qkv, b_qkv, w_out, w_gate, w_up, w_down, norms):
    width = tokens.shape[-1]
    half = tokens.shape[3]
    rows = 2 * half
    nd, nc = lax.axis_size("dp"), lax.axis_size("ctx")
    dp, ctx = lax.axis_index("dp"), lax.axis_index("ctx")
    heads_here = HEADS // nd
    groups = nc // nd
    heads_mine = heads_here // groups
    span = heads_mine * HDIM
    many = nd * rows

    def flip(x, axis, bits):
        size = nd if axis == "dp" else nc
        return lax.ppermute(x, axis, [(i, i ^ bits) for i in range(size)])

    def columns_of(w):
        depth, cols = w.shape[1:]
        odd = ctx % 2
        other = jnp.stack([take(w, dp ^ 2), take(w, dp ^ 3)])
        there = other.reshape(2, 2, depth // 2, cols)
        mine = lax.dynamic_index_in_dim(there, odd, 1, keepdims=False)
        near = flip(mine, "dp", 2)
        far = flip(near, "ctx", 1)
        buffer = jnp.zeros((nd, 2, depth // 2, cols), w.dtype)
        place = lambda buf, block, a, b: lax.dynamic_update_slice(
            buf, block.reshape(1, -1, depth // 2, cols), (a, b, 0, 0)
        )
        buffer = place(buffer, take(w, dp), dp, 0)
        buffer = place(buffer, flip(take(w, dp ^ 1), "dp", 1), dp ^ 1, 0)
        buffer = place(buffer, near[0], dp ^ 2, odd)
        buffer = place(buffer, far[0], dp ^ 2, 1 - odd)
        swapped = flip(jnp.stack([near[1], far[1]]), "dp", 1)
        buffer = place(buffer, swapped[0], dp ^ 3, odd)
        buffer = place(buffer, swapped[1], dp ^ 3, 1 - odd)
        return buffer.reshape(nd * depth, cols)

    def sum_over_dp(partial):
        blocks = partial.astype(BF16).reshape(nd, rows, width)
        total = take(blocks, dp).astype(F32)
        for k in range(1, nd):
            total = total + flip(take(blocks, dp ^ k), "dp", k).astype(F32)
        return total

    def sum_over_ctx(left, right, outer):
        part = left.shape[1] // (outer * nc)
        split = left.reshape(many, outer, nc // 2, 2, part).transpose(3, 0, 2, 1, 4)
        odd, place = ctx % 2, ctx // 2
        size = (nc // 2, outer * part, right.shape[1])
        sent = first_dims(take(split, 1 - odd).reshape(many, -1), right).astype(BF16)
        got = flip(sent, "ctx", 1)
        kept = first_dims(take(split, odd).reshape(many, -1), right) + got.astype(F32)
        kept = kept.astype(BF16).reshape(size)
        total = take(kept, place).astype(F32)
        for k in range(1, nc // 2):
            block = take(kept, lax.rem(place + k, nc // 2))
            total = total + lax.ppermute(
                block, "ctx", [(i, (i + 2 * k) % nc) for i in range(nc)]
            ).astype(F32)
        return total

    def to_rows(total, outer):
        blocks = total.astype(BF16).reshape(nd, -1, total.shape[1])
        part, cols = blocks.shape[1:]
        out = jnp.zeros((part, nd, cols), BF16)
        for k in range(nd):
            block = take(blocks, dp ^ k)
            if k:
                block = flip(block, "dp", k)
            out = lax.dynamic_update_slice(out, block[:, None], (0, dp ^ k, 0))
        return out.astype(F32)

    wq = columns_of(w_qkv.reshape(-1, 3, nd, width // nd).transpose(2, 0, 1, 3).reshape(nd, -1, 3 * width // nd))
    hidden = w_gate.shape[1] // nd
    both = jnp.stack([w_gate.reshape(-1, nd, hidden), w_up.reshape(-1, nd, hidden)], axis=2)
    wgu = columns_of(both.transpose(1, 0, 2, 3).reshape(nd, -1, 2 * hidden))

    small = jnp.concatenate([norms.reshape(-1), b_qkv]).reshape(-1, 128)
    all_tokens, all_cotangents, all_small = gather(
        "dp", nd, 0, tokens.reshape(rows, width), cotangent.reshape(rows, width), small
    )
    all_small = all_small.reshape(nd, -1)
    gains = all_small[:, : 4 * (width // nd)].reshape(nd, 4, -1).transpose(1, 0, 2)
    gains = gains.reshape(4, width).astype(F32)
    bias = all_small[:, 4 * (width // nd) :].reshape(3, nd, width // nd)
    bias = lax.dynamic_index_in_dim(bias, dp, 1, keepdims=False).reshape(-1).astype(F32)

    x_all = all_tokens.reshape(many, width).astype(F32)
    dyb = all_cotangents.reshape(many, width)
    hat1_all, _ = normalize_rows(x_all)
    h1 = (hat1_all * gains[0] + gains[1]).astype(BF16)
    qkv = plain(h1, wq) + bias

    offsets = jnp.arange(rows, dtype=jnp.int32)
    positions = jnp.where(
        offsets < half, ctx * half + offsets, (2 * nc - 1 - ctx) * half + offsets - half
    )
    turned = turn(
        qkv[:, : 2 * heads_here * HDIM].reshape(nd, rows, -1), rotary_factors(positions), 1.0
    )
    qkv = jnp.concatenate(
        [turned.astype(BF16).reshape(many, -1), qkv[:, 2 * heads_here * HDIM :].astype(BF16)], axis=1
    )
    packed = qkv.reshape(nd, rows, 3, groups, span).transpose(0, 3, 1, 2, 4)
    seq = to_sequence(nc, 1, packed.reshape(nc, rows, 3 * span)).reshape(-1, 3 * span)
    mixed_seq, lse = attention_forward(seq, heads_mine)
    mixed = from_sequence(nc, 2, mixed_seq.reshape(2 * nc, half, span))
    mixed = mixed.reshape(nd, groups, rows, span).transpose(0, 2, 1, 3).reshape(many, -1)

    x = tokens.reshape(rows, width).astype(F32)
    partial = plain(mixed, w_out).astype(BF16).reshape(nd, rows, width)
    r1 = x + jnp.sum(swap_blocks("dp", nd, 3, partial).astype(F32), axis=0)
    hat2, inverse2 = normalize_rows(r1)
    h2_own = (hat2 * gains[2] + gains[3]).astype(BF16)
    h2 = gather("dp", nd, 4, h2_own)[0].reshape(many, width)
    gu = plain(h2, wgu)
    gate, up = gu[:, :hidden], gu[:, hidden:]
    sig = jax.nn.sigmoid(gate)
    m = (gate * sig * up).astype(BF16)
    result = r1 + sum_over_dp(plain(m, w_down))

    dm = last_dims(dyb, w_down)
    d_gate = (dm * up * sig * (1.0 + gate * (1.0 - sig))).astype(BF16)
    d_up = (dm * gate * sig).astype(BF16)
    d_gu = jnp.concatenate([d_gate, d_up], axis=1)
    grad_down = sum_over_ctx(m, dyb, 1)
    partial = last_dims(d_gu, wgu).astype(BF16).reshape(nd, rows, width)
    dh2 = jnp.sum(swap_blocks("dp", nd, 5, partial).astype(F32), axis=0)
    grad_gu = to_rows(sum_over_ctx(h2, d_gu, nd), nd)
    dy = cotangent.reshape(rows, width).astype(F32)
    dr1 = dy + norm_reverse(dh2, gains[2], hat2, inverse2)
    da = gather("dp", nd, 6, dr1.astype(BF16))[0].reshape(many, width)
    grad_out = sum_over_ctx(mixed, da, 1)
    d_mixed = last_dims(da, w_out).astype(BF16)
    packed = d_mixed.reshape(nd, rows, groups, span).transpose(0, 2, 1, 3).reshape(nc, rows, span)
    d_seq = to_sequence(nc, 7, packed).reshape(-1, span)
    d_qkv_seq = attention_backward(seq, lse, d_seq, heads_mine)
    everywhere = rotary_factors(jnp.arange(2 * nc * half, dtype=jnp.int32))
    d_qkv_seq = jnp.concatenate(
        [
            turn(d_qkv_seq[:, : 2 * span], everywhere, -1.0).astype(BF16),
            d_qkv_seq[:, 2 * span :].astype(BF16),
        ],
        axis=1,
    )
    d_qkv = from_sequence(nc, 8, d_qkv_seq.reshape(2 * nc, half, 3 * span))
    d_qkv = d_qkv.reshape(nd, groups, rows, 3, span).transpose(0, 2, 3, 1, 4).reshape(many, -1)
    partial = last_dims(d_qkv, wq).astype(BF16).reshape(nd, rows, width)
    grad_qkv = to_rows(sum_over_ctx(h1, d_qkv, nd), nd)
    grad_qkv = grad_qkv.reshape(-1, nd, 3, width // nd).transpose(0, 2, 1, 3).reshape(-1, 3 * width)
    dh1 = jnp.sum(swap_blocks("dp", nd, 9, partial).astype(F32), axis=0)
    hat1, inverse1 = normalize_rows(x)
    tokens_grad = dr1 + norm_reverse(dh1, gains[0], hat1, inverse1)

    norm_sums = jnp.stack(
        [
            jnp.sum(dh1 * hat1, axis=0),
            jnp.sum(dh1, axis=0),
            jnp.sum(dh2 * hat2, axis=0),
            jnp.sum(dh2, axis=0),
        ]
    )
    bias_sums = jnp.sum(d_qkv.astype(F32), axis=0)
    sums = jnp.concatenate([norm_sums.reshape(-1), bias_sums]).reshape(-1, 128)
    sums = jnp.sum(gather("ctx", nc, 10, sums)[0], axis=0).reshape(-1)
    norm_part = sums[: 4 * width].reshape(4, nd, nc, -1)
    norm_part = lax.dynamic_index_in_dim(norm_part, ctx, 2, keepdims=False)
    small = jnp.concatenate([norm_part.reshape(-1), sums[4 * width :]])
    pad = -small.shape[0] % 1024
    sums = gather("dp", nd, 11, jnp.pad(small, (0, pad)).reshape(-1, 128))[0].reshape(nd, -1)
    norm_sums = jnp.sum(sums[:, : norm_part.size], axis=0).reshape(norm_part.shape)
    norms_grad = lax.dynamic_index_in_dim(norm_sums, dp, 1, keepdims=False)
    bias_sums = sums[:, norm_part.size : small.shape[0]].reshape(nd, 3, -1).transpose(1, 0, 2)
    bias_grad = take(bias_sums.reshape(nd * nc, -1), dp * nc + ctx)

    return (
        result.astype(BF16).reshape(tokens.shape),
        tokens_grad.reshape(tokens.shape),
        grad_qkv,
        bias_grad,
        grad_out,
        grad_gu.reshape(-1, nd, 2, hidden)[:, :, 0].reshape(-1, nd * hidden),
        grad_gu.reshape(-1, nd, 2, hidden)[:, :, 1].reshape(-1, nd * hidden),
        grad_down,
        norms_grad,
    )


def solution(mesh):
    blocks = P("dp", "ctx", None, None, None)
    owned = P(("dp", "ctx"), None)
    return jax.shard_map(
        shards,
        mesh=mesh,
        in_specs=(
            blocks,
            blocks,
            P("dp", None),
            P("dp"),
            P("dp", None),
            P("dp", None),
            P("dp", None),
            P("dp", None),
            P(None, "dp"),
        ),
        out_specs=(
            blocks,
            blocks,
            owned,
            P(("dp", "ctx")),
            owned,
            owned,
            owned,
            owned,
            P(None, ("dp", "ctx")),
        ),
        check_vma=False,
    )
```

time: 5010 us -> 1330 us (0.27)
  waiting for transfers between devices: 4560 us -> 271 us
  Pallas kernels: 0 us -> 571 us
  matrix products: 240 us -> 81.8 us
  local copies, waits for them, and re-layouts: 114 us -> 245 us
  starting transfers between devices: 1.71 us -> 77 us
  blocking collectives: 52.2 us -> 0 us
    reduce_scatter x5 -> x0, waiting for transfers between devices: 3690 us -> none  [the longest x1 970 us: shards(): lax.psum_scatter(grad_up, ('dp', 'ctx'), scatter_dimension=0, tiled=True)]
    all_gather x7 -> x0, waiting for transfers between devices: 699 us -> none  [the longest x1 146 us: shards(): lax.all_gather(w_qkv, 'dp', axis=0, tiled=True)]
    pallas_call x0 -> x14, Pallas kernels: none -> 571 us  [the longest x12 549 us: exchange(): pl.pallas_call(body, out_shape=[jax.ShapeDtypeStruct(shape, x.dtype) for...]
    ppermute x0 -> x33, waiting for transfers between devices: none -> 271 us  [the longest x12 209 us: sum_over_ctx(): lax.ppermute(block, 'ctx', [(i, (i + 2 * k) % nc) for i in range(nc)])]
    unnamed x18 -> x0, waiting for transfers between devices: 173 us -> none
    dot_general x71 -> x16, matrix products: 240 us -> 81.8 us  [the longest x8 32.5 us: first_dims(): lax.dot_general(a, b, (((0,), (0,)), ((), ())), preferred_element_type=F32)]
    ppermute x0 -> x33, starting transfers between devices: none -> 77 us  [the longest x12 55.6 us: sum_over_ctx(): lax.ppermute(block, 'ctx', [(i, (i + 2 * k) % nc) for i in range(nc)])]
  transfers between devices with their start and end apart: 15 -> 33, of which waited for: 14 -> 13; matrix products, arithmetic and copies ran while one was open for 4% -> 21% of each run, Pallas kernels for 0% -> 41%
where the time goes in v1:
time: 1330 us; the launch traced here: 1320 us
  Pallas kernels  571 us (43%)
  waiting for transfers between devices  271 us (20%)
  local copies, waits for them, and re-layouts  245 us (18%)
  matrix products  81.8 us (6%)
  starting transfers between devices  77 us (6%)
  other arithmetic  68.7 us (5%)
    pallas_call x12, Pallas kernels, exchange(): pl.pallas_call(body, out_shape=[jax.ShapeDtypeStruct(shape, x.dtype) for...  549 us
    ppermute x12, waiting for transfers between devices, sum_over_ctx(): lax.ppermute(block, 'ctx', [(i, (i + 2 * k) % nc) for i in range(nc)])  209 us
    ppermute x21, waiting for transfers between devices, flip(): return lax.ppermute(x, axis, [(i, i ^ bits) for i in range(size)])  62.5 us
    ppermute x12, starting transfers between devices, sum_over_ctx(): lax.ppermute(block, 'ctx', [(i, (i + 2 * k) % nc) for i in range(nc)])  55.6 us
    unnamed x101, local copies, waits for them, and re-layouts  37.8 us
    dynamic_slice x13, local copies, waits for them, and re-layouts, take(): return lax.dynamic_index_in_dim(x, index, 0, keepdims=False)  34.5 us
    dot_general x8, matrix products, first_dims(): lax.dot_general(a, b, (((0,), (0,)), ((), ())), preferred_element_type=F32)  32.5 us
    dot_general x4, matrix products, last_dims(): lax.dot_general(a, b, (((1,), (1,)), ((), ())), preferred_element_type=F32)  28.8 us
  transfers between devices with their start and end apart: 33, of which 13 were waited for; matrix products, arithmetic and copies ran while one was open for 21% of the time, Pallas kernels for 41%

profile of v1, /device:TPU:0, one launch (start us, length us, event | category | flops | bytes accessed | tf_op | source)
XLA Modules:
  0.0 1316.8 jit_solution(7516599531960559812)
XLA Ops:
  0.7 8.5 copy.154
  9.2 8.3 copy.153
  17.5 9.9 pad_maximum_fusion
  27.4 8.8 constant_dynamic-slice_fusion.8
  41.2 5.7 pad_maximum_fusion.1
  46.9 8.2 copy.157
  61.2 8.7 copy.141
  82.9 4.7 copy.145
  91.3 111.7 %shard_map.160 = (bf16[4,128,2048]{2,1,0:T(8,128)(2,1)}, bf16[4,128,2048]{2,1,0:T(8,128)(2,1)}, bf16[4,28,128]{2,1,0:T(8,128)(2,1)}) custom-call(bf16[128,2048]{1,0:T(8,128)(2,1)} %bitcast.308, bf16[128,2048]{1,0:T(8,128)(2,1)} %bitcast.348, bf16[28,128]{1,0:T(8,128)(2,1)} %maximum_bitcast_fusion.2.refs_2_), custom_call_target="tpu_custom_call" | custom-call | tf_op jit(solution)/shard_map/pallas_call | solution.py:101
  205.0 4.6 copy.164
  212.8 5.5 reshape.771
  251.3 5.0 broadcast_in_dim.66
  269.4 26.0 %collective-permute-done.2 = bf16[2,256,1536]{2,1,0:T(8,128)(2,1)S(1)} collective-permute-done((bf16[2,256,1536]{2,1,0:T(8,128)(2,1)}, bf16[2,256,1536]{2,1,0:T(8,128)(2,1)S(1)}, u32[]{:S(2)}, u32[]{:S(2)}) %collective-permute-start.2) | collective-permute-done | bytes 1572896 | tf_op jit(solution)/shard_map/ppermute | solution.py:280
  314.9 4.8 copy.149
  322.7 51.5 %shard_map.161 = bf16[16,64,768]{2,1,0:T(8,128)(2,1)} custom-call(bf16[8,128,768]{2,1,0:T(8,128)(2,1)} %copy.150.refs_0_), custom_call_target="tpu_custom_call" | custom-call | tf_op jit(solution)/shard_map/pallas_call | solution.py:101
  374.2 9.2 shard_map.162
  383.5 14.0 %shard_map.163 = bf16[8,128,256]{2,1,0:T(8,128)(2,1)} custom-call(bf16[16,64,256]{2,1,0:T(8,128)(2,1)} %bitcast.386), custom_call_target="tpu_custom_call" | custom-call | tf_op jit(solution)/shard_map/pallas_call | solution.py:101
  405.5 23.9 %shard_map.164 = bf16[4,128,2048]{2,1,0:T(8,128)(2,1)} custom-call(bf16[4,128,2048]{2,1,0:T(8,128)(2,1)} %bitcast.364), custom_call_target="tpu_custom_call" | custom-call | tf_op jit(solution)/shard_map/pallas_call | solution.py:101
  435.4 25.3 %shard_map.165 = bf16[4,128,2048]{2,1,0:T(8,128)(2,1)} custom-call(bf16[128,2048]{1,0:T(8,128)(2,1)} %add_convert_fusion.7.refs_0_), custom_call_target="tpu_custom_call" | custom-call | tf_op jit(solution)/shard_map/pallas_call | solution.py:101
  483.8 9.8 fusion.60
  493.7 6.0 multiply_convert_fusion.1
  500.8 4.6 convolution_convert_fusion.6
  507.9 11.1 convolution_convert_fusion.4
  519.0 25.3 %shard_map.166 = bf16[4,128,2048]{2,1,0:T(8,128)(2,1)} custom-call(bf16[4,128,2048]{2,1,0:T(8,128)(2,1)} %bitcast.362), custom_call_target="tpu_custom_call" | custom-call | tf_op jit(solution)/shard_map/pallas_call | solution.py:101
  554.2 7.9 convolution_convert_fusion
  570.1 6.3 collective-permute-done.9
  579.9 25.1 %shard_map.167 = bf16[4,128,2048]{2,1,0:T(8,128)(2,1)} custom-call(bf16[128,2048]{1,0:T(8,128)(2,1)} %get-tuple-element.67.refs_0_), custom_call_target="tpu_custom_call" | custom-call | tf_op jit(solution)/shard_map/pallas_call | solution.py:101
  612.6 145.0 %shard_map.168 = bf16[16,64,256]{2,1,0:T(8,128)(2,1)} custom-call(bf16[8,128,256]{2,1,0:T(8,128)(2,1)} %bitcast.371), custom_call_target="tpu_custom_call" | custom-call | tf_op jit(solution)/shard_map/pallas_call | solution.py:101
  757.6 13.2 %shard_map.169 = f32[1024,768]{1,0:T(8,128)} custom-call(bf16[1024,768]{1,0:T(8,128)(2,1)} %bitcast.321, f32[4,1024]{1,0:T(4,128)} %get-tuple-element.18.lse_ref, bf16[1024,256]{1,0:T(8,128)(2,1)} %bitcast.361), custom_call_target="tpu_custom_call" | custom-call | tf_op jit(solution)/shard_map/pallas_call | solution.py:255
  781.1 32.0 %shard_map.170 = bf16[8,128,768]{2,1,0:T(8,128)(2,1)} custom-call(bf16[16,64,768]{2,1,0:T(8,128)(2,1)} %bitcast.338), custom_call_target="tpu_custom_call" | custom-call | tf_op jit(solution)/shard_map/pallas_call | solution.py:101
  815.6 5.0 copy.163
  820.6 5.0 reshape.738
  825.6 8.1 convolution_convert_fusion.3
  833.7 23.8 %shard_map.171 = bf16[4,128,2048]{2,1,0:T(8,128)(2,1)} custom-call(bf16[4,128,2048]{2,1,0:T(8,128)(2,1)} %bitcast.363), custom_call_target="tpu_custom_call" | custom-call | tf_op jit(solution)/shard_map/pallas_call | solution.py:101
  871.9 66.9 %shard_map.172 = f32[8,76,128]{2,1,0:T(8,128)} custom-call(f32[76,128]{1,0:T(8,128)} %maximum_bitcast_fusion.refs_0_), custom_call_target="tpu_custom_call" | custom-call | tf_op jit(solution)/shard_map/pallas_call | solution.py:101
  957.1 14.5 %collective-permute-done.18 = bf16[256,2048]{1,0:T(8,128)(2,1)} collective-permute-done((bf16[256,2048]{1,0:T(8,128)(2,1)}, bf16[256,2048]{1,0:T(8,128)(2,1)}, u32[]{:S(2)}, u32[]{:S(2)}) %collective-permute-start.18) | collective-permute-done | bytes 1048608 | tf_op jit(solution)/shard_map/ppermute | solution.py:280
  973.7 10.7 collective-permute-start.21
  995.5 12.6 collective-permute-done.20
  1009.5 30.7 %collective-permute-start.30 = (bf16[176,2048]{1,0:T(8,128)(2,1)}, bf16[176,2048]{1,0:T(8,128)(2,1)}, u32[]{:S(2)}, u32[]{:S(2)}) collective-permute-start(bf16[176,2048]{1,0:T(8,128)(2,1)} %get-tuple-element.51), channel_id=1, source_target_pairs={{0,2},{1,3},{2,4},{3,5},{4,6},{5,7},{6,0},{7,1},{8,10},{9,11},{10,... | collective-permute-start | bytes 2162696 | tf_op jit(solution)/shard_map/ppermute | solution.py:322
  1043.5 25.7 %collective-permute-done.31 = bf16[176,2048]{1,0:T(8,128)(2,1)} collective-permute-done((bf16[176,2048]{1,0:T(8,128)(2,1)}, bf16[176,2048]{1,0:T(8,128)(2,1)}, u32[]{:S(2)}, u32[]{:S(2)}) %collective-permute-start.31) | collective-permute-done | bytes 720928 | tf_op jit(solution)/shard_map/ppermute | solution.py:322
  1081.0 5.2 add_convert_fusion
  1090.4 8.1 collective-permute-done.14
  1099.4 48.7 %collective-permute-done.13 = bf16[256,1536]{1,0:T(8,128)(2,1)S(1)} collective-permute-done((bf16[256,1536]{1,0:T(8,128)(2,1)S(1)}, bf16[256,1536]{1,0:T(8,128)(2,1)S(1)}, u32[]{:S(2)}, u32[]{:S(2)}) %collective-permute-start.13) | collective-permute-done | bytes 786464 | tf_op jit(solution)/shard_map/ppermute | solution.py:322
  1157.0 5.5 collective-permute-done.25
  1162.5 107.7 %collective-permute-done.24 = bf16[256,2816]{1,0:T(8,128)(2,1)S(1)} collective-permute-done((bf16[256,2816]{1,0:T(8,128)(2,1)S(1)}, bf16[256,2816]{1,0:T(8,128)(2,1)S(1)}, u32[]{:S(2)}, u32[]{:S(2)}) %collective-permute-start.24) | collective-permute-done | bytes 1441824 | tf_op jit(solution)/shard_map/ppermute | solution.py:322
  1289.0 5.9 collective-permute-done.27
  1295.6 6.2 collective-permute-done.28
  1306.9 5.3 fusion.57
  (331 shorter events, 288.6 us)
Async XLA Ops:
  0.6 402.3 %copy-start = (bf16[512,2048]{1,0:T(8,128)(2,1)S(1)}, bf16[512,2048]{1,0:T(8,128)(2,1)}, u32[]{:S(2)}) copy-start(bf16[512,2048]{1,0:T(8,128)(2,1)} %param.13) | copy-start | bytes 6291460
  40.7 255.0 %collective-permute-start.4 = (bf16[512,2816]{1,0:T(8,128)(2,1)}, bf16[512,2816]{1,0:T(8,128)(2,1)}, u32[]{:S(2)}, u32[]{:S(2)}) collective-permute-start(bf16[512,2816]{1,0:T(8,128)(2,1)} %bitcast.357), channel_id=1, source_target_pairs={{0,8},{8,0},{16,24},{24,16},{1,9},{9,1},{17,25},{25,17},{2,10},{10... | collective-permute-start | bytes 8650760 | tf_op jit(solution)/shard_map/ppermute | solution.py:280
  58.7 208.7 %collective-permute-start.5 = (bf16[2,256,2816]{2,1,0:T(8,128)(2,1)}, bf16[2,256,2816]{2,1,0:T(8,128)(2,1)}, u32[]{:S(2)}, u32[]{:S(2)}) collective-permute-start(bf16[2,256,2816]{2,1,0:T(8,128)(2,1)} %dynamic-slice_bitcast_fusion), channel_id=1, source_target_pairs={{0,16},{8,24},{16,0},{24,8},{1,17},{9,25},{17,1},{25,9},{2,18},{10... | collective-permute-start | bytes 8650760 | tf_op jit(solution)/shard_map/ppermute | solution.py:280
  78.8 185.7 %collective-permute-start = (bf16[512,1536]{1,0:T(8,128)(2,1)}, bf16[512,1536]{1,0:T(8,128)(2,1)}, u32[]{:S(2)}, u32[]{:S(2)}) collective-permute-start(bf16[512,1536]{1,0:T(8,128)(2,1)} %bitcast.372), channel_id=1, source_target_pairs={{0,8},{8,0},{16,24},{24,16},{1,9},{9,1},{17,25},{25,17},{2,10},{10... | collective-permute-start | bytes 4718600 | tf_op jit(solution)/shard_map/ppermute | solution.py:280
  90.3 167.7 %collective-permute-start.1 = (bf16[2,256,1536]{2,1,0:T(8,128)(2,1)}, bf16[2,256,1536]{2,1,0:T(8,128)(2,1)}, u32[]{:S(2)}, u32[]{:S(2)}) collective-permute-start(bf16[2,256,1536]{2,1,0:T(8,128)(2,1)} %dynamic-slice_bitcast_fusion.1), channel_id=1, source_target_pairs={{0,16},{8,24},{16,0},{24,8},{1,17},{9,25},{17,1},{25,9},{2,18},{10... | collective-permute-start | bytes 4718600 | tf_op jit(solution)/shard_map/ppermute | solution.py:280
  251.3 5.0 copy-start.10
  258.0 37.5 %collective-permute-start.2 = (bf16[2,256,1536]{2,1,0:T(8,128)(2,1)}, bf16[2,256,1536]{2,1,0:T(8,128)(2,1)S(1)}, u32[]{:S(2)}, u32[]{:S(2)}) collective-permute-start(bf16[2,256,1536]{2,1,0:T(8,128)(2,1)} %collective-permute-done.1), channel_id=1, source_target_pairs={{0,1},{1,0},{2,3},{3,2},{4,5},{5,4},{6,7},{7,6},{8,9},{9,8},{10,11... | collective-permute-start | bytes 4718600 | tf_op jit(solution)/shard_map/ppermute | solution.py:280
  267.4 132.2 %collective-permute-start.6 = (bf16[2,256,2816]{2,1,0:T(8,128)(2,1)}, bf16[2,256,2816]{2,1,0:T(8,128)(2,1)}, u32[]{:S(2)}, u32[]{:S(2)}) collective-permute-start(bf16[2,256,2816]{2,1,0:T(8,128)(2,1)} %collective-permute-done.5), channel_id=1, source_target_pairs={{0,1},{1,0},{2,3},{3,2},{4,5},{5,4},{6,7},{7,6},{8,9},{9,8},{10,11... | collective-permute-start | bytes 8650760 | tf_op jit(solution)/shard_map/ppermute | solution.py:280
  295.7 6.3 collective-permute-start.3
  402.9 75.5 %collective-permute-start.7 = (bf16[2,256,2816]{2,1,0:T(8,128)(2,1)}, bf16[2,256,2816]{2,1,0:T(8,128)(2,1)}, u32[]{:S(2)}, u32[]{:S(2)}) collective-permute-start(bf16[2,256,2816]{2,1,0:T(8,128)(2,1)} %pad_maximum_fusion.3), channel_id=1, source_target_pairs={{0,8},{8,0},{16,24},{24,16},{1,9},{9,1},{17,25},{25,17},{2,10},{10... | collective-permute-start | bytes 8650760 | tf_op jit(solution)/shard_map/ppermute | solution.py:280
  474.0 19.7 %slice-start = ((s8[5767168]{0:T(1024)(128)(4,1)}), s8[4194304]{0:T(1024)(128)(4,1)S(1)}, s32[]{:S(2)}) async-start(s8[5767168]{0:T(1024)(128)(4,1)} %bitcast.415), calls=%async_computation | async-start | bytes 8388608
  483.8 9.9 slice-start.1
  483.8 9.9 copy-start.39
  550.5 19.6 %collective-permute-start.10 = (bf16[128,2048]{1,0:T(8,128)(2,1)}, bf16[128,2048]{1,0:T(8,128)(2,1)}, u32[]{:S(2)}, u32[]{:S(2)}) collective-permute-start(bf16[128,2048]{1,0:T(8,128)(2,1)} %get-tuple-element.61), channel_id=1, source_target_pairs={{0,24},{8,16},{16,8},{24,0},{1,25},{9,17},{17,9},{25,1},{2,26},{10... | collective-permute-start | bytes 1572872 | tf_op jit(solution)/shard_map/ppermute | solution.py:280
  552.4 24.0 %collective-permute-start.9 = (bf16[128,2048]{1,0:T(8,128)(2,1)}, bf16[128,2048]{1,0:T(8,128)(2,1)}, u32[]{:S(2)}, u32[]{:S(2)}) collective-permute-start(bf16[128,2048]{1,0:T(8,128)(2,1)} %get-tuple-element.62), channel_id=1, source_target_pairs={{0,16},{8,24},{16,0},{24,8},{1,17},{9,25},{17,1},{25,9},{2,18},{10... | collective-permute-start | bytes 1572872 | tf_op jit(solution)/shard_map/ppermute | solution.py:280
  554.1 22.3 %collective-permute-start.8 = (bf16[128,2048]{1,0:T(8,128)(2,1)}, bf16[128,2048]{1,0:T(8,128)(2,1)}, u32[]{:S(2)}, u32[]{:S(2)}) collective-permute-start(bf16[128,2048]{1,0:T(8,128)(2,1)} %get-tuple-element.60), channel_id=1, source_target_pairs={{0,8},{8,0},{16,24},{24,16},{1,9},{9,1},{17,25},{25,17},{2,10},{10... | collective-permute-start | bytes 1572872 | tf_op jit(solution)/shard_map/ppermute | solution.py:280
  554.2 10.4 copy-start.17
  562.1 518.9 %collective-permute-start.22 = (bf16[1024,2816]{1,0:T(8,128)(2,1)}, bf16[1024,2816]{1,0:T(8,128)(2,1)}, u32[]{:S(2)}, u32[]{:S(2)}) collective-permute-start(bf16[1024,2816]{1,0:T(8,128)(2,1)} %convolution_convert_fusion), channel_id=1, source_target_pairs={{0,1},{1,0},{2,3},{3,2},{4,5},{5,4},{6,7},{7,6},{8,9},{9,8},{10,11... | collective-permute-start | bytes 17301512 | tf_op jit(solution)/shard_map/ppermute | solution.py:280
  565.6 10.9 copy-start.6
  565.6 10.9 copy-start.18
  568.9 415.5 %collective-permute-start.29 = (bf16[704,2048]{1,0:T(8,128)(2,1)}, bf16[704,2048]{1,0:T(8,128)(2,1)}, u32[]{:S(2)}, u32[]{:S(2)}) collective-permute-start(bf16[704,2048]{1,0:T(8,128)(2,1)} %convolution_convert_fusion.2), channel_id=1, source_target_pairs={{0,1},{1,0},{2,3},{3,2},{4,5},{5,4},{6,7},{7,6},{8,9},{9,8},{10,11... | collective-permute-start | bytes 8650760 | tf_op jit(solution)/shard_map/ppermute | solution.py:280
  772.1 4.9 copy-start.13
  864.8 207.7 %collective-permute-start.11 = (bf16[1024,1536]{1,0:T(8,128)(2,1)}, bf16[1024,1536]{1,0:T(8,128)(2,1)}, u32[]{:S(2)}, u32[]{:S(2)}) collective-permute-start(bf16[1024,1536]{1,0:T(8,128)(2,1)} %convolution_convert_fusion.1), channel_id=1, source_target_pairs={{0,1},{1,0},{2,3},{3,2},{4,5},{5,4},{6,7},{7,6},{8,9},{9,8},{10,11... | collective-permute-start | bytes 9437192 | tf_op jit(solution)/shard_map/ppermute | solution.py:280
  944.9 26.6 %collective-permute-start.18 = (bf16[256,2048]{1,0:T(8,128)(2,1)}, bf16[256,2048]{1,0:T(8,128)(2,1)}, u32[]{:S(2)}, u32[]{:S(2)}) collective-permute-start(bf16[256,2048]{1,0:T(8,128)(2,1)} %convolution_convert_fusion.7), channel_id=1, source_target_pairs={{0,1},{1,0},{2,3},{3,2},{4,5},{5,4},{6,7},{7,6},{8,9},{9,8},{10,11... | collective-permute-start | bytes 3145736 | tf_op jit(solution)/shard_map/ppermute | solution.py:280
  953.2 18.3 %copy-start.9 = (bf16[4,128,2048]{2,1,0:T(8,128)(2,1)S(1)}, bf16[4,128,2048]{2,1,0:T(8,128)(2,1)}, u32[]{:S(2)}) copy-start(bf16[4,128,2048]{2,1,0:T(8,128)(2,1)} %shard_map.167) | copy-start | bytes 6291460
  971.5 13.5 %copy-start.31 = (bf16[512,1,4,1,176]{0,4,3,2,1:T(8,128)(2,1)S(1)}, bf16[512,1,4,1,176]{0,4,3,2,1:T(8,128)(2,1)}, u32[]{:S(2)}) copy-start(bf16[512,1,4,1,176]{0,4,3,2,1:T(8,128)(2,1)} %get-tuple-element.70) | copy-start | bytes 2162692
  971.5 13.5 %copy-start.41 = (bf16[4,128,2048]{2,1,0:T(8,128)(2,1)S(1)}, bf16[4,128,2048]{2,1,0:T(8,128)(2,1)}, u32[]{:S(2)}) copy-start(bf16[4,128,2048]{2,1,0:T(8,128)(2,1)} %get-tuple-element.17) | copy-start | bytes 6291460
  973.7 17.4 %collective-permute-start.21 = (bf16[64,2048]{1,0:T(8,128)(2,1)S(1)}, bf16[64,2048]{1,0:T(8,128)(2,1)S(1)}, u32[]{:S(2)}, u32[]{:S(2)}) collective-permute-start(bf16[64,2048]{1,0:T(8,128)(2,1)S(1)} %get-tuple-element.75), channel_id=1, source_target_pairs={{0,6},{1,7},{2,0},{3,1},{4,2},{5,3},{6,4},{7,5},{8,14},{9,15},{10,... | collective-permute-start | bytes 786440 | tf_op jit(solution)/shard_map/ppermute | solution.py:322
  984.4 23.7 %collective-permute-start.20 = (bf16[64,2048]{1,0:T(8,128)(2,1)S(1)}, bf16[64,2048]{1,0:T(8,128)(2,1)S(1)}, u32[]{:S(2)}, u32[]{:S(2)}) collective-permute-start(bf16[64,2048]{1,0:T(8,128)(2,1)S(1)} %get-tuple-element.76), channel_id=1, source_target_pairs={{0,4},{1,5},{2,6},{3,7},{4,0},{5,1},{6,2},{7,3},{8,12},{9,13},{10,... | collective-permute-start | bytes 786440 | tf_op jit(solution)/shard_map/ppermute | solution.py:322
  984.4 23.7 %collective-permute-start.19 = (bf16[64,2048]{1,0:T(8,128)(2,1)S(1)}, bf16[64,2048]{1,0:T(8,128)(2,1)S(1)}, u32[]{:S(2)}, u32[]{:S(2)}) collective-permute-start(bf16[64,2048]{1,0:T(8,128)(2,1)S(1)} %get-tuple-element.74), channel_id=1, source_target_pairs={{0,2},{1,3},{2,4},{3,5},{4,6},{5,7},{6,0},{7,1},{8,10},{9,11},{10,... | collective-permute-start | bytes 786440 | tf_op jit(solution)/shard_map/ppermute | solution.py:322
  991.1 52.3 %collective-permute-start.32 = (bf16[176,2048]{1,0:T(8,128)(2,1)}, bf16[176,2048]{1,0:T(8,128)(2,1)}, u32[]{:S(2)}, u32[]{:S(2)}) collective-permute-start(bf16[176,2048]{1,0:T(8,128)(2,1)} %get-tuple-element.52), channel_id=1, source_target_pairs={{0,6},{1,7},{2,0},{3,1},{4,2},{5,3},{6,4},{7,5},{8,14},{9,15},{10,... | collective-permute-start | bytes 2162696 | tf_op jit(solution)/shard_map/ppermute | solution.py:322
  1008.1 61.1 %collective-permute-start.31 = (bf16[176,2048]{1,0:T(8,128)(2,1)}, bf16[176,2048]{1,0:T(8,128)(2,1)}, u32[]{:S(2)}, u32[]{:S(2)}) collective-permute-start(bf16[176,2048]{1,0:T(8,128)(2,1)} %get-tuple-element.53), channel_id=1, source_target_pairs={{0,4},{1,5},{2,6},{3,7},{4,0},{5,1},{6,2},{7,3},{8,12},{9,13},{10,... | collective-permute-start | bytes 2162696 | tf_op jit(solution)/shard_map/ppermute | solution.py:322
  1009.5 59.7 %collective-permute-start.30 = (bf16[176,2048]{1,0:T(8,128)(2,1)}, bf16[176,2048]{1,0:T(8,128)(2,1)}, u32[]{:S(2)}, u32[]{:S(2)}) collective-permute-start(bf16[176,2048]{1,0:T(8,128)(2,1)} %get-tuple-element.51), channel_id=1, source_target_pairs={{0,2},{1,3},{2,4},{3,5},{4,6},{5,7},{6,0},{7,1},{8,10},{9,11},{10,... | collective-permute-start | bytes 2162696 | tf_op jit(solution)/shard_map/ppermute | solution.py:322
  1043.5 29.1 %copy-start.26 = (bf16[512,1536]{1,0:T(8,128)(2,1)S(1)}, bf16[512,1536]{1,0:T(8,128)(2,1)}, u32[]{:S(2)}) copy-start(bf16[512,1536]{1,0:T(8,128)(2,1)} %reshape.738) | copy-start | bytes 4718596
  1043.5 29.1 %copy-start.28 = (bf16[1,512,4,4,64]{1,4,3,2,0:T(8,128)(2,1)S(1)}, bf16[1,512,4,4,64]{1,4,3,2,0:T(8,128)(2,1)}, u32[]{:S(2)}) copy-start(bf16[1,512,4,4,64]{1,4,3,2,0:T(8,128)(2,1)} %copy.165) | copy-start | bytes 3145732
  1076.3 4.7 copy-start.29
  1076.5 21.9 %collective-permute-start.14 = (bf16[256,1536]{1,0:T(8,128)(2,1)S(1)}, bf16[256,1536]{1,0:T(8,128)(2,1)S(1)}, u32[]{:S(2)}, u32[]{:S(2)}) collective-permute-start(bf16[256,1536]{1,0:T(8,128)(2,1)S(1)} %get-tuple-element.45), channel_id=1, source_target_pairs={{0,6},{1,7},{2,0},{3,1},{4,2},{5,3},{6,4},{7,5},{8,14},{9,15},{10,... | collective-permute-start | bytes 2359304 | tf_op jit(solution)/shard_map/ppermute | solution.py:322
  1079.8 68.2 %collective-permute-start.13 = (bf16[256,1536]{1,0:T(8,128)(2,1)S(1)}, bf16[256,1536]{1,0:T(8,128)(2,1)S(1)}, u32[]{:S(2)}, u32[]{:S(2)}) collective-permute-start(bf16[256,1536]{1,0:T(8,128)(2,1)S(1)} %get-tuple-element.46), channel_id=1, source_target_pairs={{0,4},{1,5},{2,6},{3,7},{4,0},{5,1},{6,2},{7,3},{8,12},{9,13},{10,... | collective-permute-start | bytes 2359304 | tf_op jit(solution)/shard_map/ppermute | solution.py:322
  1079.8 68.2 %collective-permute-start.12 = (bf16[256,1536]{1,0:T(8,128)(2,1)S(1)}, bf16[256,1536]{1,0:T(8,128)(2,1)S(1)}, u32[]{:S(2)}, u32[]{:S(2)}) collective-permute-start(bf16[256,1536]{1,0:T(8,128)(2,1)S(1)} %get-tuple-element.44), channel_id=1, source_target_pairs={{0,2},{1,3},{2,4},{3,5},{4,6},{5,7},{6,0},{7,1},{8,10},{9,11},{10,... | collective-permute-start | bytes 2359304 | tf_op jit(solution)/shard_map/ppermute | solution.py:322
  1086.5 76.0 %collective-permute-start.25 = (bf16[256,2816]{1,0:T(8,128)(2,1)S(1)}, bf16[256,2816]{1,0:T(8,128)(2,1)S(1)}, u32[]{:S(2)}, u32[]{:S(2)}) collective-permute-start(bf16[256,2816]{1,0:T(8,128)(2,1)S(1)} %get-tuple-element.41), channel_id=1, source_target_pairs={{0,6},{1,7},{2,0},{3,1},{4,2},{5,3},{6,4},{7,5},{8,14},{9,15},{10,... | collective-permute-start | bytes 4325384 | tf_op jit(solution)/shard_map/ppermute | solution.py:322
  1089.2 181.0 %collective-permute-start.24 = (bf16[256,2816]{1,0:T(8,128)(2,1)S(1)}, bf16[256,2816]{1,0:T(8,128)(2,1)S(1)}, u32[]{:S(2)}, u32[]{:S(2)}) collective-permute-start(bf16[256,2816]{1,0:T(8,128)(2,1)S(1)} %get-tuple-element.42), channel_id=1, source_target_pairs={{0,4},{1,5},{2,6},{3,7},{4,0},{5,1},{6,2},{7,3},{8,12},{9,13},{10,... | collective-permute-start | bytes 4325384 | tf_op jit(solution)/shard_map/ppermute | solution.py:322
  1098.4 171.8 %collective-permute-start.23 = (bf16[256,2816]{1,0:T(8,128)(2,1)S(1)}, bf16[256,2816]{1,0:T(8,128)(2,1)S(1)}, u32[]{:S(2)}, u32[]{:S(2)}) collective-permute-start(bf16[256,2816]{1,0:T(8,128)(2,1)S(1)} %get-tuple-element.40), channel_id=1, source_target_pairs={{0,2},{1,3},{2,4},{3,5},{4,6},{5,7},{6,0},{7,1},{8,10},{9,11},{10,... | collective-permute-start | bytes 4325384 | tf_op jit(solution)/shard_map/ppermute | solution.py:322
  1148.5 2.7 collective-permute-start.15
  1148.6 7.8 collective-permute-start.16
  1151.2 120.8 %collective-permute-start.17 = (bf16[64,1536]{1,0:T(8,128)(2,1)S(1)}, bf16[64,1536]{1,0:T(8,128)(2,1)S(1)}, u32[]{:S(2)}, u32[]{:S(2)}) collective-permute-start(bf16[64,1536]{1,0:T(8,128)(2,1)S(1)} %get-tuple-element.77), channel_id=1, source_target_pairs={{0,24},{8,16},{16,8},{24,0},{1,25},{9,17},{17,9},{25,1},{2,26},{10... | collective-permute-start | bytes 589832 | tf_op jit(solution)/shard_map/ppermute | solution.py:280
  1272.0 15.3 %collective-permute-start.26 = (bf16[64,2816]{1,0:T(8,128)(2,1)}, bf16[64,2816]{1,0:T(8,128)(2,1)}, u32[]{:S(2)}, u32[]{:S(2)}) collective-permute-start(bf16[64,2816]{1,0:T(8,128)(2,1)} %get-tuple-element.73), channel_id=1, source_target_pairs={{0,8},{8,0},{16,24},{24,16},{1,9},{9,1},{17,25},{25,17},{2,10},{10... | collective-permute-start | bytes 1081352 | tf_op jit(solution)/shard_map/ppermute | solution.py:280
  1283.4 11.4 collective-permute-start.27
  1284.1 17.7 %collective-permute-start.28 = (bf16[64,2816]{1,0:T(8,128)(2,1)}, bf16[64,2816]{1,0:T(8,128)(2,1)S(1)}, u32[]{:S(2)}, u32[]{:S(2)}) collective-permute-start(bf16[64,2816]{1,0:T(8,128)(2,1)} %get-tuple-element.71), channel_id=1, source_target_pairs={{0,24},{8,16},{16,8},{24,0},{1,25},{9,17},{17,9},{25,1},{2,26},{10... | collective-permute-start | bytes 1081352 | tf_op jit(solution)/shard_map/ppermute | solution.py:280
  (31 other events, 78.9 us)

commit v2 on v1

--- a/solution.py
+++ b/solution.py
@@ -1,5 +1,6 @@
 import jax
 import jax.numpy as jnp
+import numpy as np
 from jax import lax
 from jax.experimental import pallas as pl
 from jax.experimental.pallas import tpu as pltpu
@@ -11,7 +12,7 @@
 MESH = pl.DeviceIdType.MESH
 F32 = jnp.float32
 BF16 = jnp.bfloat16
-VMEM_BYTES = 56 * 1024 * 1024
+VMEM_BYTES = 60 * 1024 * 1024
 
 
 def normalize_rows(field):
@@ -178,45 +179,469 @@
     return jnp.where(keys <= queries, scores, -1e30)
 
 
-def attention_forward(qkv, heads):
-    length = qkv.shape[0]
+def flip_one(i):
+    return i + 1 - 2 * (i % 2)
+
+
+def halves(start, size):
+    return pl.ds(pl.multiple_of(start, 64), size)
+
+
+def lanes(start, size):
+    return pl.ds(pl.multiple_of(start, 128), size)
+
+
+class Copies:
+    def __init__(self, send, recv, local):
+        self.send, self.recv, self.local = send, recv, local
+        self.remotes, self.locals = [], []
+
+    def to(self, device, src, dst):
+        at = len(self.remotes)
+        copy = pltpu.make_async_remote_copy(
+            src_ref=src,
+            dst_ref=dst,
+            send_sem=self.send.at[at],
+            recv_sem=self.recv.at[at],
+            device_id=device,
+            device_id_type=MESH,
+        )
+        copy.start()
+        self.remotes.append(copy)
+        return copy
+
+    def here(self, src, dst):
+        copy = pltpu.make_async_copy(src, dst, self.local.at[len(self.locals)])
+        copy.start()
+        self.locals.append(copy)
+        return copy
+
+
+def meet(axis_sizes):
+    barrier = pltpu.get_barrier_semaphore()
+    met = 0
+    for axis, size in axis_sizes:
+        me = lax.axis_index(axis)
+        for k in range(1, size):
+            pl.semaphore_signal(
+                barrier, inc=1, device_id={axis: lax.rem(me + k, size)}, device_id_type=MESH
+            )
+            met += 1
+    pl.semaphore_wait(barrier, met)
+
+
+def attend(x_ref, o_ref, lse_ref, heads, head):
+    length = x_ref.shape[0]
     block, segments, inner = attention_shapes(length)
-
-    def body(x_ref, o_ref, lse_ref):
+    q_at, k_at, v_at = (head_columns(heads, i, head) for i in range(3))
+    for segment in range(segments):
+        count = (segment + 1) * inner * block
+        keys = x_ref[:count, k_at]
+        values = x_ref[:count, v_at]
+
+        def step(i, _):
+            start = pl.multiple_of((segment * inner + i) * block, block)
+            query = x_ref[pl.ds(start, block), q_at] * 0.125
+            scores = causal(last_dims(keys, query), start)
+            top = jnp.max(scores, axis=0, keepdims=True)
+            expo = jnp.exp(scores - top)
+            total = jnp.sum(expo, axis=0, keepdims=True)
+            mixed = first_dims(values, expo.astype(BF16)) / total
+            o_ref[pl.ds(start, block), head * HDIM : (head + 1) * HDIM] = mixed.T.astype(BF16)
+            lse_ref[head : head + 1, pl.ds(start, block)] = top + jnp.log(total)
+            return 0
+
+        if inner == 1:
+            step(0, 0)
+        else:
+            lax.fori_loop(0, inner, step, 0)
+
+
+def rotate_pair(u, keep, sine):
+    lane = lax.broadcasted_iota(jnp.int32, u.shape, 1) % HDIM
+    other = jnp.where(lane < ROT // 2, pltpu.roll(u, 128 - ROT // 2, 1), pltpu.roll(u, ROT // 2, 1))
+    return u * keep + other * sine
+
+
+def rotary_pair_tables(length):
+    pairs = ROT // 2
+    inverse = np.power(np.float32(10000.0), -np.arange(pairs, dtype=np.float32) / np.float32(pairs))
+    angle = np.arange(length, dtype=np.float32)[:, None] * inverse.astype(np.float32)[None, :]
+    cosine, sine = np.cos(angle), np.sin(angle)
+    keep = np.concatenate([cosine, cosine, np.ones((length, HDIM - ROT), np.float32)], axis=1)
+    signed = np.concatenate([-sine, sine, np.zeros((length, HDIM - ROT), np.float32)], axis=1)
+    return np.tile(keep, (1, 2)).astype(np.float32), np.tile(signed, (1, 2)).astype(np.float32)
+
+
+def tiles(total, size):
+    return [(at, min(size, total - at)) for at in range(0, total, size)]
+
+
+def over_tiles(total, size, step):
+    whole = total // size
+    if whole:
+
+        def run(i, _):
+            step(pl.multiple_of(i * size, size), size)
+            return 0
+
+        lax.fori_loop(0, whole, run, 0)
+    if total % size:
+        step(whole * size, total % size)
+
+
+def forward(nd, nc, tokens, cotangent, small, w_qkv, w_gate, w_up, w_out, w_down):
+    rows, width = tokens.shape
+    half = rows // 2
+    many = nd * rows
+    length = 2 * nc * half
+    depth = w_qkv.shape[0]
+    part_depth = depth // 2
+    heads_here = HEADS // nd
+    groups = nc // nd
+    heads = heads_here // groups
+    span = heads * HDIM
+    cols = heads_here * HDIM
+    hidden = w_gate.shape[1] // nd
+    down = w_down.shape[0]
+    keep, sine = rotary_pair_tables(length)
+
+    def body(
+        tok_i, cot_i, small_i, wq_i, wg_i, wu_i, wo_i, wd_i, keep_i, sine_i,
+        h1_o, dy_o, wq_o, seq_o, lse_o, mixed_o, r1_o, h2_o, m_o, dgu_o, pout_o, pdh2_o, small_o,
+        tok, dy, sm, wq, h1, qkv, seq, lse, o, mixed, wo, part, ra, rb, r1, h2, wg, wu, wd, m, dgu,
+        turns, send, recv, local,
+    ):
+        dp, ctx = lax.axis_index("dp"), lax.axis_index("ctx")
+        odd = ctx % 2
+        near, across, far = flip_one(dp), (dp + 2) % nd, nd - 1 - dp
+        beside = flip_one(ctx)
+        links = Copies(send, recv, local)
+        blocks = lambda ref, b: ref.at[halves(b * rows, rows)]
+
+        get_tok = links.here(tok_i, blocks(tok, dp))
+        get_turns = [
+            links.here(table.at[halves(block * half, half)], turns.at[t, pl.ds(i * half, half)])
+            for t, table in enumerate((keep_i, sine_i))
+            for i, block in enumerate((ctx, 2 * nc - 1 - ctx))
+        ]
+        get_small = links.here(small_i, sm.at[dp])
+        get_wq = [
+            links.here(
+                wq_i.at[:, lanes(j * width + dp * cols, cols)],
+                wq.at[halves(dp * depth, depth), pl.ds(j * cols, cols)],
+            )
+            for j in range(3)
+        ]
+        meet((("dp", nd), ("ctx", nc)))
+
+        send_tok = [links.to({"dp": e}, tok_i, blocks(tok, dp)) for e in (near, across)]
+        send_small = [links.to({"dp": e}, small_i, sm.at[dp]) for e in (near, across, far)]
+
+        def columns(w_i, w, e, at, n, to, full):
+            start = dp * depth + (0 if full else odd * part_depth)
+            size = depth if full else part_depth
+            first = 0 if full else odd * part_depth
+            return links.to(
+                {"dp": e},
+                w_i.at[halves(first, size), lanes(at, n)],
+                w.at[halves(start, size), pl.ds(to, n)],
+            )
+
+        def relay(w, source):
+            block = w.at[halves(source * depth + odd * part_depth, part_depth)]
+            return links.to({"ctx": beside}, block, block)
+
+        wq_x = [
+            [columns(wq_i, wq, e, j * width + e * cols, cols, j * cols, False) for j in range(3)]
+            for e in (across, far)
+        ]
+        wq_near = [
+            columns(wq_i, wq, near, j * width + near * cols, cols, j * cols, True) for j in range(3)
+        ]
+        get_wo = links.here(wo_i, wo)
+        get_wd = links.here(wd_i, wd)
+        get_dy = links.here(cot_i, blocks(dy, dp))
+        get_wgu = [
+            links.here(w_i.at[:, lanes(dp * hidden, hidden)], w.at[halves(dp * depth, depth)])
+            for w_i, w in ((wg_i, wg), (wu_i, wu))
+        ]
+
+        send_tok[1].wait_recv()
+        forward_tok = links.to({"dp": near}, blocks(tok, across), blocks(tok, across))
+        get_small.wait()
+        for copy in send_small:
+            copy.wait_recv()
+
+        def gain(row):
+            lines = [
+                sm[b, row * 4 + q : row * 4 + q + 1, :]
+                for b in range(nd)
+                for q in range(width // nd // 128)
+            ]
+            return jnp.concatenate(lines, axis=1)
+
+        def first_norm(b):
+            at = halves(b * rows, rows)
+            hat, _ = normalize_rows(tok[at, :].astype(F32))
+            h1[at, :] = (hat * gain(0) + gain(1)).astype(BF16)
+
+        get_tok.wait()
+        first_norm(dp)
+        send_tok[0].wait_recv()
+        first_norm(near)
+        first_norm(across)
+        forward_tok.wait_recv()
+        first_norm(far)
+        put_h1 = links.here(h1, h1_o)
+        put_small = links.here(sm, small_o)
+
+        wq_y = []
+        for source, copies in ((across, wq_x[0]), (far, wq_x[1])):
+            for copy in copies:
+                copy.wait_recv()
+            wq_y.append(relay(wq, source))
+        wgu_x = [
+            [columns(w_i, w, e, e * hidden, hidden, 0, False) for e in (across, far)]
+            for w_i, w in ((wg_i, wg), (wu_i, wu))
+        ]
+        wgu_near = [
+            columns(w_i, w, near, near * hidden, hidden, 0, True)
+            for w_i, w in ((wg_i, wg), (wu_i, wu))
+        ]
+        for copy in get_wq + get_turns:
+            copy.wait()
+        for copy in wq_near + wq_y:
+            copy.wait_recv()
+        put_wq = links.here(wq, wq_o)
+
+        for at, n in tiles(3 * cols, 256):
+            j = at // cols
+            acc = plain(h1[...], wq[:, at : at + n])
+            for q in range(n // 128):
+                first = at % cols + q * 128
+                line = (j * width + dp * cols + first) // 128
+                per = 3 * width // nd // 128
+                bias = sm[line // per, pl.ds(4 * (width // nd) // 128 + line % per, 1), :]
+                for s in range(nd):
+                    u = acc[s * rows : (s + 1) * rows, q * 128 : (q + 1) * 128] + bias
+                    if j < 2:
+                        u = rotate_pair(u, turns[0], turns[1])
+                    u = u.astype(BF16)
+                    if heads > 1:
+                        g, off = first // span, first % span
+                        qkv[g, s * rows : (s + 1) * rows, j * span + off : j * span + off + 128] = u
+                    else:
+                        for i in range(2):
+                            qkv[
+                                first // HDIM + i, s * rows : (s + 1) * rows, j * HDIM : (j + 1) * HDIM
+                            ] = u[:, i * HDIM : (i + 1) * HDIM]
+
+        mirror = 2 * nc - 1 - ctx
+        go = []
+        for k in range(1, nc):
+            peer = lax.rem(ctx + k, nc)
+            s, g = peer // groups, peer % groups
+            for i, block in enumerate((ctx, mirror)):
+                go.append(
+                    links.to(
+                        {"ctx": peer},
+                        qkv.at[g, halves(s * rows + i * half, half)],
+                        seq.at[halves(block * half, half)],
+                    )
+                )
+        s, g = ctx // groups, ctx % groups
+        stay = [
+            links.here(
+                qkv.at[g, halves(s * rows + i * half, half)], seq.at[halves(block * half, half)]
+            )
+            for i, block in enumerate((ctx, mirror))
+        ]
+        send_dy = [links.to({"dp": e}, cot_i, blocks(dy, dp)) for e in (near, across)]
+        wgu_y = []
+
+        def pass_on(w, source, copy):
+            copy.wait_recv()
+            wgu_y.append(relay(w, source))
+
+        pass_on(wg, across, wgu_x[0][0])
+        pass_on(wg, far, wgu_x[0][1])
+        for copy in stay:
+            copy.wait()
+        for copy in go:
+            copy.wait_recv()
+        put_seq = links.here(seq, seq_o)
+        pass_on(wu, across, wgu_x[1][0])
+
         for head in range(heads):
-            q_at, k_at, v_at = (head_columns(heads, i, head) for i in range(3))
-            for segment in range(segments):
-                count = (segment + 1) * inner * block
-                keys = x_ref[:count, k_at]
-                values = x_ref[:count, v_at]
-
-                def step(i, _):
-                    start = pl.multiple_of((segment * inner + i) * block, block)
-                    query = x_ref[pl.ds(start, block), q_at] * 0.125
-                    scores = causal(last_dims(keys, query), start)
-                    top = jnp.max(scores, axis=0, keepdims=True)
-                    expo = jnp.exp(scores - top)
-                    total = jnp.sum(expo, axis=0, keepdims=True)
-                    mixed = first_dims(values, expo.astype(BF16)) / total
-                    o_ref[pl.ds(start, block), head * HDIM : (head + 1) * HDIM] = mixed.T.astype(
-                        BF16
+            attend(seq, o, lse, heads, head)
+
+        back = []
+        for k in range(1, nc):
+            peer = lax.rem(ctx + k, nc)
+            for i, block in enumerate((peer, 2 * nc - 1 - peer)):
+                back.append(
+                    links.to(
+                        {"ctx": peer},
+                        o.at[halves(block * half, half)],
+                        mixed.at[g, halves(s * rows + i * half, half)],
                     )
-                    lse_ref[head : head + 1, pl.ds(start, block)] = top + jnp.log(total)
-                    return 0
-
-                if inner == 1:
-                    step(0, 0)
-                else:
-                    lax.fori_loop(0, inner, step, 0)
-
-    return pl.pallas_call(
+                )
+        stay = [
+            links.here(
+                o.at[halves(block * half, half)], mixed.at[g, halves(s * rows + i * half, half)]
+            )
+            for i, block in enumerate((ctx, mirror))
+        ]
+        put_lse = links.here(lse, lse_o)
+        pass_on(wu, far, wgu_x[1][1])
+        send_dy[1].wait_recv()
+        forward_dy = links.to({"dp": near}, blocks(dy, across), blocks(dy, across))
+        get_wo.wait()
+        for copy in stay:
+            copy.wait()
+        for copy in back:
+            copy.wait_recv()
+        put_mixed = links.here(mixed, mixed_o)
+
+        def out_tile(at, n):
+            acc = plain(mixed[0], wo[0:span, pl.ds(at, n)])
+            for i in range(1, groups):
+                acc += plain(mixed[i], wo[i * span : (i + 1) * span, pl.ds(at, n)])
+            part[:, pl.ds(at, n)] = acc.astype(BF16)
+
+        over_tiles(width, 512, out_tile)
+
+        to_near = [
+            links.to({"dp": near}, blocks(part, far), blocks(ra, 0)),
+            links.to({"dp": near}, blocks(part, near), blocks(ra, 1)),
+        ]
+        to_near[0].wait_recv()
+        across_at = halves(across * rows, rows)
+        part[across_at, :] = (part[across_at, :].astype(F32) + ra[:rows, :].astype(F32)).astype(BF16)
+        to_across = links.to({"dp": across}, blocks(part, across), rb)
+        to_near[1].wait_recv()
+        own_at = halves(dp * rows, rows)
+        r1[...] = tok[own_at, :].astype(F32) + (
+            part[own_at, :].astype(F32) + ra[rows:, :].astype(F32)
+        )
+        to_across.wait_recv()
+        r1[...] += rb[...].astype(F32)
+        put_r1 = links.here(r1, r1_o)
+        hat, _ = normalize_rows(r1[...])
+        h2[own_at, :] = (hat * gain(2) + gain(3)).astype(BF16)
+        send_h2 = [links.to({"dp": e}, blocks(h2, dp), blocks(h2, dp)) for e in (near, across)]
+        send_h2[1].wait_recv()
+        forward_h2 = links.to({"dp": near}, blocks(h2, across), blocks(h2, across))
+        get_wd.wait()
+        get_dy.wait()
+        for copy in get_wgu:
+            copy.wait()
+        for copy in wgu_near + wgu_y + [send_dy[0], forward_dy, send_h2[0], forward_h2]:
+            copy.wait_recv()
+        put_h2 = links.here(h2, h2_o)
+        put_dy = links.here(dy, dy_o)
+        put_h1.wait()
+
+        def hidden_tile(at, n):
+            here = pl.ds(at, n)
+            gate = plain(h2[...], wg[:, here])
+            up = plain(h2[...], wu[:, here])
+            dm = last_dims(dy[...], wd[here, :])
+            sig = jax.nn.sigmoid(gate)
+            m[:, here] = (gate * sig * up).astype(BF16)
+            dgu[:, here] = (dm * up * sig * (1.0 + gate * (1.0 - sig))).astype(BF16)
+            dgu[:, pl.ds(hidden + at, n)] = (dm * gate * sig).astype(BF16)
+
+        over_tiles(hidden, 256, hidden_tile)
+        put_m = links.here(m, m_o)
+        put_dgu = links.here(dgu, dgu_o)
+
+        def dh2_tile(at, n):
+            here = pl.ds(at, n)
+            acc = last_dims(dgu[:, :hidden], wg[here, :]) + last_dims(dgu[:, hidden:], wu[here, :])
+            h1[:, here] = acc.astype(BF16)
+
+        over_tiles(width, 256, dh2_tile)
+        put_pdh2 = links.here(h1, pdh2_o)
+        for copy in send_tok + [forward_tok]:
+            copy.wait_send()
+
+        def result_tile(at, n):
+            here = pl.ds(at, n)
+            tok[:, here] = plain(m[...], wd[:, here]).astype(BF16)
+
+        over_tiles(width, 256, result_tile)
+        put_pout = links.here(tok, pout_o)
+
+        done = send_tok + [forward_tok]
+        for copy in links.remotes:
+            if not any(copy is other for other in done):
+                copy.wait_send()
+        for copy in (
+            put_small, put_wq, put_seq, put_lse, put_mixed, put_r1, put_h2, put_dy, put_m, put_dgu,
+            put_pdh2, put_pout,
+        ):
+            copy.wait()
+
+    anywhere = pl.BlockSpec(memory_space=pl.ANY)
+    shape = jax.ShapeDtypeStruct
+    remotes = 2 + 3 + 6 + 3 + 1 + 2 + 4 + 2 + 2 * (nc - 1) * 2 + 2 + 4 + 1 + 3 + 2 + 1
+    outs = dict(
+        h1=((many, width), BF16),
+        dy=((many, width), BF16),
+        wq=((width, 3 * cols), BF16),
+        seq=((length, 3 * span), BF16),
+        lse=((heads, length), F32),
+        mixed=((groups, many, span), BF16),
+        r1=((rows, width), F32),
+        h2=((many, width), BF16),
+        m=((many, hidden), BF16),
+        dgu=((many, 2 * hidden), BF16),
+        pout=((many, width), BF16),
+        pdh2=((many, width), BF16),
+        small=((nd,) + small.shape, F32),
+    )
+    scratch = [
+        ((many, width), BF16),
+        ((many, width), BF16),
+        ((nd,) + small.shape, F32),
+        ((width, 3 * cols), BF16),
+        ((many, width), BF16),
+        ((groups, many, 3 * span), BF16),
+        ((length, 3 * span), BF16),
+        ((heads, length), F32),
+        ((length, span), BF16),
+        ((groups, many, span), BF16),
+        ((cols, width), BF16),
+        ((many, width), BF16),
+        ((2 * rows, width), BF16),
+        ((rows, width), BF16),
+        ((rows, width), F32),
+        ((many, width), BF16),
+        ((width, hidden), BF16),
+        ((width, hidden), BF16),
+        ((down, width), BF16),
+        ((many, hidden), BF16),
+        ((many, 2 * hidden), BF16),
+        ((2, rows, 128), F32),
+    ]
+    results = pl.pallas_call(
         body,
-        out_shape=[
-            jax.ShapeDtypeStruct((length, heads * HDIM), BF16),
-            jax.ShapeDtypeStruct((heads, length), F32),
+        out_shape=[shape(*o) for o in outs.values()],
+        in_specs=[anywhere] * 10,
+        out_specs=[anywhere] * len(outs),
+        scratch_shapes=[pltpu.VMEM(*s) for s in scratch]
+        + [
+            pltpu.SemaphoreType.DMA((remotes,)),
+            pltpu.SemaphoreType.DMA((remotes,)),
+            pltpu.SemaphoreType.DMA((40,)),
         ],
-        compiler_params=pltpu.CompilerParams(vmem_limit_bytes=VMEM_BYTES),
-    )(qkv)
+        compiler_params=pltpu.CompilerParams(
+            collective_id=0, has_side_effects=True, vmem_limit_bytes=VMEM_BYTES
+        ),
+    )(tokens, cotangent, small, w_qkv, w_gate, w_up, w_out, w_down, keep, sine)
+    return dict(zip(outs, results))
 
 
 def attention_backward(qkv, lse, d_mixed, heads):
@@ -278,27 +703,6 @@
     def flip(x, axis, bits):
         size = nd if axis == "dp" else nc
         return lax.ppermute(x, axis, [(i, i ^ bits) for i in range(size)])
-
-    def columns_of(w):
-        depth, cols = w.shape[1:]
-        odd = ctx % 2
-        other = jnp.stack([take(w, dp ^ 2), take(w, dp ^ 3)])
-        there = other.reshape(2, 2, depth // 2, cols)
-        mine = lax.dynamic_index_in_dim(there, odd, 1, keepdims=False)
-        near = flip(mine, "dp", 2)
-        far = flip(near, "ctx", 1)
-        buffer = jnp.zeros((nd, 2, depth // 2, cols), w.dtype)
-        place = lambda buf, block, a, b: lax.dynamic_update_slice(
-            buf, block.reshape(1, -1, depth // 2, cols), (a, b, 0, 0)
-        )
-        buffer = place(buffer, take(w, dp), dp, 0)
-        buffer = place(buffer, flip(take(w, dp ^ 1), "dp", 1), dp ^ 1, 0)
-        buffer = place(buffer, near[0], dp ^ 2, odd)
-        buffer = place(buffer, far[0], dp ^ 2, 1 - odd)
-        swapped = flip(jnp.stack([near[1], far[1]]), "dp", 1)
-        buffer = place(buffer, swapped[0], dp ^ 3, odd)
-        buffer = place(buffer, swapped[1], dp ^ 3, 1 - odd)
-        return buffer.reshape(nd * depth, cols)
 
     def sum_over_dp(partial):
         blocks = partial.astype(BF16).reshape(nd, rows, width)
@@ -335,61 +739,24 @@
             out = lax.dynamic_update_slice(out, block[:, None], (0, dp ^ k, 0))
         return out.astype(F32)
 
-    wq = columns_of(w_qkv.reshape(-1, 3, nd, width // nd).transpose(2, 0, 1, 3).reshape(nd, -1, 3 * width // nd))
     hidden = w_gate.shape[1] // nd
-    both = jnp.stack([w_gate.reshape(-1, nd, hidden), w_up.reshape(-1, nd, hidden)], axis=2)
-    wgu = columns_of(both.transpose(1, 0, 2, 3).reshape(nd, -1, 2 * hidden))
-
-    small = jnp.concatenate([norms.reshape(-1), b_qkv]).reshape(-1, 128)
-    all_tokens, all_cotangents, all_small = gather(
-        "dp", nd, 0, tokens.reshape(rows, width), cotangent.reshape(rows, width), small
+    small = jnp.concatenate([norms.reshape(-1), b_qkv]).astype(F32)
+    small = jnp.pad(small, (0, -small.shape[0] % 1024)).reshape(-1, 128)
+    f = forward(
+        nd, nc, tokens.reshape(rows, width), cotangent.reshape(rows, width), small,
+        w_qkv, w_gate, w_up, w_out, w_down,
     )
-    all_small = all_small.reshape(nd, -1)
-    gains = all_small[:, : 4 * (width // nd)].reshape(nd, 4, -1).transpose(1, 0, 2)
-    gains = gains.reshape(4, width).astype(F32)
-    bias = all_small[:, 4 * (width // nd) :].reshape(3, nd, width // nd)
-    bias = lax.dynamic_index_in_dim(bias, dp, 1, keepdims=False).reshape(-1).astype(F32)
-
-    x_all = all_tokens.reshape(many, width).astype(F32)
-    dyb = all_cotangents.reshape(many, width)
-    hat1_all, _ = normalize_rows(x_all)
-    h1 = (hat1_all * gains[0] + gains[1]).astype(BF16)
-    qkv = plain(h1, wq) + bias
-
-    offsets = jnp.arange(rows, dtype=jnp.int32)
-    positions = jnp.where(
-        offsets < half, ctx * half + offsets, (2 * nc - 1 - ctx) * half + offsets - half
-    )
-    turned = turn(
-        qkv[:, : 2 * heads_here * HDIM].reshape(nd, rows, -1), rotary_factors(positions), 1.0
-    )
-    qkv = jnp.concatenate(
-        [turned.astype(BF16).reshape(many, -1), qkv[:, 2 * heads_here * HDIM :].astype(BF16)], axis=1
-    )
-    packed = qkv.reshape(nd, rows, 3, groups, span).transpose(0, 3, 1, 2, 4)
-    seq = to_sequence(nc, 1, packed.reshape(nc, rows, 3 * span)).reshape(-1, 3 * span)
-    mixed_seq, lse = attention_forward(seq, heads_mine)
-    mixed = from_sequence(nc, 2, mixed_seq.reshape(2 * nc, half, span))
-    mixed = mixed.reshape(nd, groups, rows, span).transpose(0, 2, 1, 3).reshape(many, -1)
-
+    h1, dyb, wq, seq, lse, r1, h2 = (f[k] for k in ("h1", "dy", "wq", "seq", "lse", "r1", "h2"))
+    m, d_gu = f["m"], f["dgu"]
+    gains = f["small"].reshape(nd, -1)[:, : 4 * (width // nd)].reshape(nd, 4, -1)
+    gains = gains.transpose(1, 0, 2).reshape(4, width)
+    mixed = f["mixed"].transpose(1, 0, 2).reshape(many, -1)
     x = tokens.reshape(rows, width).astype(F32)
-    partial = plain(mixed, w_out).astype(BF16).reshape(nd, rows, width)
-    r1 = x + jnp.sum(swap_blocks("dp", nd, 3, partial).astype(F32), axis=0)
     hat2, inverse2 = normalize_rows(r1)
-    h2_own = (hat2 * gains[2] + gains[3]).astype(BF16)
-    h2 = gather("dp", nd, 4, h2_own)[0].reshape(many, width)
-    gu = plain(h2, wgu)
-    gate, up = gu[:, :hidden], gu[:, hidden:]
-    sig = jax.nn.sigmoid(gate)
-    m = (gate * sig * up).astype(BF16)
-    result = r1 + sum_over_dp(plain(m, w_down))
-
-    dm = last_dims(dyb, w_down)
-    d_gate = (dm * up * sig * (1.0 + gate * (1.0 - sig))).astype(BF16)
-    d_up = (dm * gate * sig).astype(BF16)
-    d_gu = jnp.concatenate([d_gate, d_up], axis=1)
+    result = r1 + sum_over_dp(f["pout"])
+
     grad_down = sum_over_ctx(m, dyb, 1)
-    partial = last_dims(d_gu, wgu).astype(BF16).reshape(nd, rows, width)
+    partial = f["pdh2"].reshape(nd, rows, width)
     dh2 = jnp.sum(swap_blocks("dp", nd, 5, partial).astype(F32), axis=0)
     grad_gu = to_rows(sum_over_ctx(h2, d_gu, nd), nd)
     dy = cotangent.reshape(rows, width).astype(F32)

time: 1330 us -> 884 us (0.66)
  the two profiles are of different devices: /device:TPU:0 before, /device:TPU:9 now
where the time goes in v2:
time: 884 us; the launch traced here: 879 us
  Pallas kernels  431 us (49%)
  waiting for transfers between devices  255 us (29%)
  local copies, waits for them, and re-layouts  95.6 us (11%)
  matrix products  40.8 us (5%)
  starting transfers between devices  28.1 us (3%)
  other arithmetic  27.1 us (3%)
    ppermute x12, waiting for transfers between devices, sum_over_ctx(): lax.ppermute(block, 'ctx', [(i, (i + 2 * k) % nc) for i in range(nc)])  241 us
    pallas_call x7, Pallas kernels, exchange(): pl.pallas_call(body, out_shape=[jax.ShapeDtypeStruct(shape, x.dtype) for...  215 us
    pallas_call x1, Pallas kernels, forward(): pl.pallas_call(body, out_shape=[shape(*o) for o in outs.values()], in_spe...  203 us
    dot_general x8, matrix products, first_dims(): lax.dot_general(a, b, (((0,), (0,)), ((), ())), preferred_element_type=F32)  29.9 us
  transfers between devices with their start and end apart: 25, of which 14 were waited for; matrix products, arithmetic and copies ran while one was open for 16% of the time, Pallas kernels for 26%

profile of v2, /device:TPU:9, one launch (start us, length us, event | category | flops | bytes accessed | tf_op | source)
XLA Modules:
  0.0 878.7 jit_solution(1246469032484401107)
XLA Ops:
  2.7 203.0 %shard_map.178 = (bf16[512,2048]{1,0:T(8,128)(2,1)}, bf16[512,2048]{1,0:T(8,128)(2,1)}, bf16[2048,1536]{1,0:T(8,128)(2,1)}, bf16[1024,768]{1,0:T(8,128)(2,1)}, f...) custom-call(bf16[128,2048]{1,0:T(8,128)(2,1)} %bitcast.201, ...), custom_call_target="tpu_custom_call" | custom-call | tf_op jit(solution)/shard_map/pallas_call | solution.py:629
  209.4 3.3 convolution_convert_fusion.2
  212.9 2.9 copy.75
  215.8 3.9 copy.81
  219.7 3.4 dynamic-slice_bitcast_fusion.3
  223.2 4.9 convolution_convert_fusion
  237.3 42.6 %shard_map.179 = bf16[4,128,2048]{2,1,0:T(8,128)(2,1)} custom-call(bf16[4,128,2048]{2,1,0:T(8,128)(2,1)} %bitcast.229), custom_call_target="tpu_custom_call" | custom-call | tf_op jit(solution)/shard_map/pallas_call | solution.py:102
  287.3 2.9 copy.70
  292.8 2.9 copy.71
  297.2 3.3 copy.72
  305.6 3.7 fusion.32
  309.2 25.6 %shard_map.180 = bf16[4,128,2048]{2,1,0:T(8,128)(2,1)} custom-call(bf16[128,2048]{1,0:T(8,128)(2,1)} %get-tuple-element.44.refs_0_), custom_call_target="tpu_custom_call" | custom-call | tf_op jit(solution)/shard_map/pallas_call | solution.py:102
  334.8 2.9 convolution_convert_fusion.5
  338.7 67.9 %shard_map.181 = bf16[16,64,256]{2,1,0:T(8,128)(2,1)} custom-call(bf16[8,128,256]{2,1,0:T(8,128)(2,1)} %bitcast.231), custom_call_target="tpu_custom_call" | custom-call | tf_op jit(solution)/shard_map/pallas_call | solution.py:102
  406.7 12.9 %shard_map.182 = f32[1024,768]{1,0:T(8,128)} custom-call(bf16[1024,768]{1,0:T(8,128)(2,1)} %get-tuple-element.26.x_ref, f32[4,1024]{1,0:T(4,128)} %get-tuple-element.27.lse_ref, bf16[1024,256]{1,0:T(8,128)(2,1)} %bitcast.227), custom_call_target="tpu_custom_call" | custom-call | tf_op jit(solution)/shard_map/pallas_call | solution.py:680
  419.6 3.3 fusion.34
  429.2 38.7 %shard_map.183 = bf16[8,128,768]{2,1,0:T(8,128)(2,1)} custom-call(bf16[16,64,768]{2,1,0:T(8,128)(2,1)} %bitcast.208), custom_call_target="tpu_custom_call" | custom-call | tf_op jit(solution)/shard_map/pallas_call | solution.py:102
  470.5 5.0 copy.74
  475.5 4.8 reshape.364
  480.3 8.0 convolution_convert_fusion.3
  488.4 26.4 %shard_map.184 = bf16[4,128,2048]{2,1,0:T(8,128)(2,1)} custom-call(bf16[4,128,2048]{2,1,0:T(8,128)(2,1)} %bitcast.230), custom_call_target="tpu_custom_call" | custom-call | tf_op jit(solution)/shard_map/pallas_call | solution.py:102
  519.6 9.8 %shard_map.185 = f32[8,76,128]{2,1,0:T(8,128)} custom-call(f32[76,128]{1,0:T(8,128)} %maximum_bitcast_fusion.refs_0_), custom_call_target="tpu_custom_call" | custom-call | tf_op jit(solution)/shard_map/pallas_call | solution.py:102
  532.8 3.8 shard_map.186
  537.4 5.2 convolution_convert_fusion.1
  543.9 2.8 multiply_add_fusion
  552.0 3.5 add_convert_fusion.2
  558.4 12.7 %collective-permute-done.12 = bf16[64,2048]{1,0:T(8,128)(2,1)S(1)} collective-permute-done((bf16[64,2048]{1,0:T(8,128)(2,1)S(1)}, bf16[64,2048]{1,0:T(8,128)(2,1)S(1)}, u32[]{:S(2)}, u32[]{:S(2)}) %collective-permute-start.12) | collective-permute-done | bytes 262176 | tf_op jit(solution)/shard_map/ppermute | solution.py:726
  571.1 3.1 collective-permute-start.23
  574.2 31.8 %collective-permute-done.13 = bf16[64,2048]{1,0:T(8,128)(2,1)S(1)} collective-permute-done((bf16[64,2048]{1,0:T(8,128)(2,1)S(1)}, bf16[64,2048]{1,0:T(8,128)(2,1)S(1)}, u32[]{:S(2)}, u32[]{:S(2)}) %collective-permute-start.13) | collective-permute-done | bytes 262176 | tf_op jit(solution)/shard_map/ppermute | solution.py:726
  610.0 7.6 collective-permute-done.22
  617.5 15.4 %collective-permute-done.23 = bf16[176,2048]{1,0:T(8,128)(2,1)} collective-permute-done((bf16[176,2048]{1,0:T(8,128)(2,1)}, bf16[176,2048]{1,0:T(8,128)(2,1)}, u32[]{:S(2)}, u32[]{:S(2)}) %collective-permute-start.23) | collective-permute-done | bytes 720928 | tf_op jit(solution)/shard_map/ppermute | solution.py:726
  633.0 3.9 collective-permute-done.24
  636.9 3.1 fusion.10
  640.0 3.8 add_convert_fusion.1
  644.0 3.2 collective-permute-start.5
  647.3 5.4 add_convert_fusion
  656.4 6.3 collective-permute-done.4
  662.6 3.1 collective-permute-start.17
  665.8 45.6 %collective-permute-done.5 = bf16[256,1536]{1,0:T(8,128)(2,1)S(1)} collective-permute-done((bf16[256,1536]{1,0:T(8,128)(2,1)S(1)}, bf16[256,1536]{1,0:T(8,128)(2,1)S(1)}, u32[]{:S(2)}, u32[]{:S(2)}) %collective-permute-start.5) | collective-permute-done | bytes 786464 | tf_op jit(solution)/shard_map/ppermute | solution.py:726
  711.4 65.1 %collective-permute-done.6 = bf16[256,1536]{1,0:T(8,128)(2,1)S(1)} collective-permute-done((bf16[256,1536]{1,0:T(8,128)(2,1)S(1)}, bf16[256,1536]{1,0:T(8,128)(2,1)S(1)}, u32[]{:S(2)}, u32[]{:S(2)}) %collective-permute-start.6) | collective-permute-done | bytes 786464 | tf_op jit(solution)/shard_map/ppermute | solution.py:726
  786.0 18.0 %collective-permute-done.15 = bf16[256,2816]{1,0:T(8,128)(2,1)S(1)} collective-permute-done((bf16[256,2816]{1,0:T(8,128)(2,1)S(1)}, bf16[256,2816]{1,0:T(8,128)(2,1)S(1)}, u32[]{:S(2)}, u32[]{:S(2)}) %collective-permute-start.15) | collective-permute-done | bytes 1441824 | tf_op jit(solution)/shard_map/ppermute | solution.py:726
  804.1 30.9 %collective-permute-done.16 = bf16[256,2816]{1,0:T(8,128)(2,1)S(1)} collective-permute-done((bf16[256,2816]{1,0:T(8,128)(2,1)S(1)}, bf16[256,2816]{1,0:T(8,128)(2,1)S(1)}, u32[]{:S(2)}, u32[]{:S(2)}) %collective-permute-start.16) | collective-permute-done | bytes 1441824 | tf_op jit(solution)/shard_map/ppermute | solution.py:726
  835.0 3.3 collective-permute-done.17
  841.9 2.7 reshape.411
  846.8 3.3 reshape.403
  855.5 4.7 collective-permute-done.19
  860.9 7.1 collective-permute-done.20
  868.8 3.2 reshape.407
  (184 shorter events, 96.4 us)
Async XLA Ops:
  207.6 1.9 copy-start.23
  212.7 338.6 %collective-permute-start.21 = (bf16[704,2048]{1,0:T(8,128)(2,1)}, bf16[704,2048]{1,0:T(8,128)(2,1)}, u32[]{:S(2)}, u32[]{:S(2)}) collective-permute-start(bf16[704,2048]{1,0:T(8,128)(2,1)} %convolution_convert_fusion.2), channel_id=1, source_target_pairs={{0,1},{1,0},{2,3},{3,2},{4,5},{5,4},{6,7},{7,6},{8,9},{9,8},{10,11... | collective-permute-start | bytes 8650760 | tf_op jit(solution)/shard_map/ppermute | solution.py:705
  219.7 3.5 copy-start.21
  228.1 5.9 copy-start.4
  228.1 419.2 %collective-permute-start.14 = (bf16[1024,2816]{1,0:T(8,128)(2,1)}, bf16[1024,2816]{1,0:T(8,128)(2,1)}, u32[]{:S(2)}, u32[]{:S(2)}) collective-permute-start(bf16[1024,2816]{1,0:T(8,128)(2,1)} %convolution_convert_fusion), channel_id=1, source_target_pairs={{0,1},{1,0},{2,3},{3,2},{4,5},{5,4},{6,7},{7,6},{8,9},{9,8},{10,11... | collective-permute-start | bytes 17301512 | tf_op jit(solution)/shard_map/ppermute | solution.py:705
  231.9 5.0 copy-start.2
  231.9 73.6 %collective-permute-start = (bf16[128,2048]{1,0:T(8,128)(2,1)}, bf16[128,2048]{1,0:T(8,128)(2,1)}, u32[]{:S(2)}, u32[]{:S(2)}) collective-permute-start(bf16[128,2048]{1,0:T(8,128)(2,1)} %get-tuple-element.65), channel_id=1, source_target_pairs={{0,8},{8,0},{16,24},{24,16},{1,9},{9,1},{17,25},{25,17},{2,10},{10... | collective-permute-start | bytes 1572872 | tf_op jit(solution)/shard_map/ppermute | solution.py:705
  231.9 73.7 %collective-permute-start.1 = (bf16[128,2048]{1,0:T(8,128)(2,1)}, bf16[128,2048]{1,0:T(8,128)(2,1)}, u32[]{:S(2)}, u32[]{:S(2)}) collective-permute-start(bf16[128,2048]{1,0:T(8,128)(2,1)} %get-tuple-element.67), channel_id=1, source_target_pairs={{0,16},{8,24},{16,0},{24,8},{1,17},{9,25},{17,1},{25,9},{2,18},{10... | collective-permute-start | bytes 1572872 | tf_op jit(solution)/shard_map/ppermute | solution.py:705
  232.2 73.4 %collective-permute-start.2 = (bf16[128,2048]{1,0:T(8,128)(2,1)}, bf16[128,2048]{1,0:T(8,128)(2,1)}, u32[]{:S(2)}, u32[]{:S(2)}) collective-permute-start(bf16[128,2048]{1,0:T(8,128)(2,1)} %get-tuple-element.66), channel_id=1, source_target_pairs={{0,24},{8,16},{16,8},{24,0},{1,25},{9,17},{17,9},{25,1},{2,26},{10... | collective-permute-start | bytes 1572872 | tf_op jit(solution)/shard_map/ppermute | solution.py:705
  279.9 2.5 copy-start.20
  304.0 1.6 copy-start.11
  309.2 25.6 %copy-start.10 = (bf16[512,2048]{1,0:T(8,128)(2,1)S(1)}, bf16[512,2048]{1,0:T(8,128)(2,1)}, u32[]{:S(2)}) copy-start(bf16[512,2048]{1,0:T(8,128)(2,1)} %wo_i.1) | copy-start | bytes 6291460
  419.6 3.3 copy-start
  419.6 6.8 copy-start.8
  422.9 1.6 copy-start.1
  423.1 3.3 copy-start.6
  423.1 3.3 copy-start.7
  426.2 120.5 %collective-permute-start.10 = (bf16[256,2048]{1,0:T(8,128)(2,1)}, bf16[256,2048]{1,0:T(8,128)(2,1)}, u32[]{:S(2)}, u32[]{:S(2)}) collective-permute-start(bf16[256,2048]{1,0:T(8,128)(2,1)} %convolution_convert_fusion.4), channel_id=1, source_target_pairs={{0,1},{1,0},{2,3},{3,2},{4,5},{5,4},{6,7},{7,6},{8,9},{9,8},{10,11... | collective-permute-start | bytes 3145736 | tf_op jit(solution)/shard_map/ppermute | solution.py:705
  514.8 2.5 copy-start.5
  542.6 97.4 %collective-permute-start.3 = (bf16[1024,1536]{1,0:T(8,128)(2,1)}, bf16[1024,1536]{1,0:T(8,128)(2,1)}, u32[]{:S(2)}, u32[]{:S(2)}) collective-permute-start(bf16[1024,1536]{1,0:T(8,128)(2,1)} %convolution_convert_fusion.1), channel_id=1, source_target_pairs={{0,1},{1,0},{2,3},{3,2},{4,5},{5,4},{6,7},{7,6},{8,9},{9,8},{10,11... | collective-permute-start | bytes 9437192 | tf_op jit(solution)/shard_map/ppermute | solution.py:705
  546.6 5.4 copy-start.15
  546.6 5.4 copy-start.24
  548.8 8.8 %collective-permute-start.11 = (bf16[64,2048]{1,0:T(8,128)(2,1)S(1)}, bf16[64,2048]{1,0:T(8,128)(2,1)S(1)}, u32[]{:S(2)}, u32[]{:S(2)}) collective-permute-start(bf16[64,2048]{1,0:T(8,128)(2,1)S(1)} %get-tuple-element.73), channel_id=1, source_target_pairs={{0,2},{1,3},{2,4},{3,5},{4,6},{5,7},{6,0},{7,1},{8,10},{9,11},{10,... | collective-permute-start | bytes 786440 | tf_op jit(solution)/shard_map/ppermute | solution.py:726
  548.9 22.2 %collective-permute-start.12 = (bf16[64,2048]{1,0:T(8,128)(2,1)S(1)}, bf16[64,2048]{1,0:T(8,128)(2,1)S(1)}, u32[]{:S(2)}, u32[]{:S(2)}) collective-permute-start(bf16[64,2048]{1,0:T(8,128)(2,1)S(1)} %get-tuple-element.75), channel_id=1, source_target_pairs={{0,4},{1,5},{2,6},{3,7},{4,0},{5,1},{6,2},{7,3},{8,12},{9,13},{10,... | collective-permute-start | bytes 786440 | tf_op jit(solution)/shard_map/ppermute | solution.py:726
  551.3 54.7 %collective-permute-start.13 = (bf16[64,2048]{1,0:T(8,128)(2,1)S(1)}, bf16[64,2048]{1,0:T(8,128)(2,1)S(1)}, u32[]{:S(2)}, u32[]{:S(2)}) collective-permute-start(bf16[64,2048]{1,0:T(8,128)(2,1)S(1)} %get-tuple-element.74), channel_id=1, source_target_pairs={{0,6},{1,7},{2,0},{3,1},{4,2},{5,3},{6,4},{7,5},{8,14},{9,15},{10,... | collective-permute-start | bytes 786440 | tf_op jit(solution)/shard_map/ppermute | solution.py:726
  555.6 2.1 copy-start.9
  557.7 59.9 %collective-permute-start.22 = (bf16[176,2048]{1,0:T(8,128)(2,1)}, bf16[176,2048]{1,0:T(8,128)(2,1)S(1)}, u32[]{:S(2)}, u32[]{:S(2)}) collective-permute-start(bf16[176,2048]{1,0:T(8,128)(2,1)} %get-tuple-element.56), channel_id=1, source_target_pairs={{0,2},{1,3},{2,4},{3,5},{4,6},{5,7},{6,0},{7,1},{8,10},{9,11},{10,... | collective-permute-start | bytes 2162696 | tf_op jit(solution)/shard_map/ppermute | solution.py:726
  571.1 34.9 %copy-start.18 = (bf16[64,2048]{1,0:T(8,128)(2,1)}, bf16[64,2048]{1,0:T(8,128)(2,1)S(1)}, u32[]{:S(2)}) copy-start(bf16[64,2048]{1,0:T(8,128)(2,1)S(1)} %collective-permute-done.12) | copy-start | bytes 786436
  571.1 61.9 %collective-permute-start.23 = (bf16[176,2048]{1,0:T(8,128)(2,1)}, bf16[176,2048]{1,0:T(8,128)(2,1)}, u32[]{:S(2)}, u32[]{:S(2)}) collective-permute-start(bf16[176,2048]{1,0:T(8,128)(2,1)} %get-tuple-element.58), channel_id=1, source_target_pairs={{0,4},{1,5},{2,6},{3,7},{4,0},{5,1},{6,2},{7,3},{8,12},{9,13},{10,... | collective-permute-start | bytes 2162696 | tf_op jit(solution)/shard_map/ppermute | solution.py:726
  606.0 30.9 %collective-permute-start.24 = (bf16[176,2048]{1,0:T(8,128)(2,1)S(1)}, bf16[176,2048]{1,0:T(8,128)(2,1)}, u32[]{:S(2)}, u32[]{:S(2)}) collective-permute-start(bf16[176,2048]{1,0:T(8,128)(2,1)S(1)} %get-tuple-element.57), channel_id=1, source_target_pairs={{0,6},{1,7},{2,0},{3,1},{4,2},{5,3},{6,4},{7,5},{8,14},{9,15},{10,... | collective-permute-start | bytes 2162696 | tf_op jit(solution)/shard_map/ppermute | solution.py:726
  610.0 30.0 %copy-start.12 = (bf16[512,1536]{1,0:T(8,128)(2,1)S(1)}, bf16[512,1536]{1,0:T(8,128)(2,1)}, u32[]{:S(2)}) copy-start(bf16[512,1536]{1,0:T(8,128)(2,1)} %reshape.364) | copy-start | bytes 4718596
  610.0 30.0 %copy-start.14 = (bf16[1,512,4,4,64]{1,4,3,2,0:T(8,128)(2,1)S(1)}, bf16[1,512,4,4,64]{1,4,3,2,0:T(8,128)(2,1)}, u32[]{:S(2)}) copy-start(bf16[1,512,4,4,64]{1,4,3,2,0:T(8,128)(2,1)} %copy.76) | copy-start | bytes 3145732
  643.8 3.5 copy-start.13
  643.8 3.5 copy-start.22
  644.0 18.7 %collective-permute-start.4 = (bf16[256,1536]{1,0:T(8,128)(2,1)S(1)}, bf16[256,1536]{1,0:T(8,128)(2,1)S(1)}, u32[]{:S(2)}, u32[]{:S(2)}) collective-permute-start(bf16[256,1536]{1,0:T(8,128)(2,1)S(1)} %get-tuple-element.49), channel_id=1, source_target_pairs={{0,2},{1,3},{2,4},{3,5},{4,6},{5,7},{6,0},{7,1},{8,10},{9,11},{10,... | collective-permute-start | bytes 2359304 | tf_op jit(solution)/shard_map/ppermute | solution.py:726
  644.0 67.3 %collective-permute-start.5 = (bf16[256,1536]{1,0:T(8,128)(2,1)S(1)}, bf16[256,1536]{1,0:T(8,128)(2,1)S(1)}, u32[]{:S(2)}, u32[]{:S(2)}) collective-permute-start(bf16[256,1536]{1,0:T(8,128)(2,1)S(1)} %get-tuple-element.51), channel_id=1, source_target_pairs={{0,4},{1,5},{2,6},{3,7},{4,0},{5,1},{6,2},{7,3},{8,12},{9,13},{10,... | collective-permute-start | bytes 2359304 | tf_op jit(solution)/shard_map/ppermute | solution.py:726
  647.3 129.2 %collective-permute-start.6 = (bf16[256,1536]{1,0:T(8,128)(2,1)S(1)}, bf16[256,1536]{1,0:T(8,128)(2,1)S(1)}, u32[]{:S(2)}, u32[]{:S(2)}) collective-permute-start(bf16[256,1536]{1,0:T(8,128)(2,1)S(1)} %get-tuple-element.50), channel_id=1, source_target_pairs={{0,6},{1,7},{2,0},{3,1},{4,2},{5,3},{6,4},{7,5},{8,14},{9,15},{10,... | collective-permute-start | bytes 2359304 | tf_op jit(solution)/shard_map/ppermute | solution.py:726
  653.1 151.0 %collective-permute-start.15 = (bf16[256,2816]{1,0:T(8,128)(2,1)S(1)}, bf16[256,2816]{1,0:T(8,128)(2,1)S(1)}, u32[]{:S(2)}, u32[]{:S(2)}) collective-permute-start(bf16[256,2816]{1,0:T(8,128)(2,1)S(1)} %get-tuple-element.46), channel_id=1, source_target_pairs={{0,2},{1,3},{2,4},{3,5},{4,6},{5,7},{6,0},{7,1},{8,10},{9,11},{10,... | collective-permute-start | bytes 4325384 | tf_op jit(solution)/shard_map/ppermute | solution.py:726
  654.6 180.4 %collective-permute-start.16 = (bf16[256,2816]{1,0:T(8,128)(2,1)S(1)}, bf16[256,2816]{1,0:T(8,128)(2,1)S(1)}, u32[]{:S(2)}, u32[]{:S(2)}) collective-permute-start(bf16[256,2816]{1,0:T(8,128)(2,1)S(1)} %get-tuple-element.48), channel_id=1, source_target_pairs={{0,4},{1,5},{2,6},{3,7},{4,0},{5,1},{6,2},{7,3},{8,12},{9,13},{10,... | collective-permute-start | bytes 4325384 | tf_op jit(solution)/shard_map/ppermute | solution.py:726
  662.6 175.6 %collective-permute-start.17 = (bf16[256,2816]{1,0:T(8,128)(2,1)S(1)}, bf16[256,2816]{1,0:T(8,128)(2,1)S(1)}, u32[]{:S(2)}, u32[]{:S(2)}) collective-permute-start(bf16[256,2816]{1,0:T(8,128)(2,1)S(1)} %get-tuple-element.47), channel_id=1, source_target_pairs={{0,6},{1,7},{2,0},{3,1},{4,2},{5,3},{6,4},{7,5},{8,14},{9,15},{10,... | collective-permute-start | bytes 4325384 | tf_op jit(solution)/shard_map/ppermute | solution.py:726
  776.9 4.7 collective-permute-start.7
  778.9 6.5 collective-permute-start.8
  781.6 59.6 %collective-permute-start.9 = (bf16[64,1536]{1,0:T(8,128)(2,1)S(1)}, bf16[64,1536]{1,0:T(8,128)(2,1)S(1)}, u32[]{:S(2)}, u32[]{:S(2)}) collective-permute-start(bf16[64,1536]{1,0:T(8,128)(2,1)S(1)} %get-tuple-element.77), channel_id=1, source_target_pairs={{0,24},{8,16},{16,8},{24,0},{1,25},{9,17},{17,9},{25,1},{2,26},{10... | collective-permute-start | bytes 589832 | tf_op jit(solution)/shard_map/ppermute | solution.py:705
  840.1 13.7 %collective-permute-start.18 = (bf16[64,2816]{1,0:T(8,128)(2,1)}, bf16[64,2816]{1,0:T(8,128)(2,1)}, u32[]{:S(2)}, u32[]{:S(2)}) collective-permute-start(bf16[64,2816]{1,0:T(8,128)(2,1)} %get-tuple-element.72), channel_id=1, source_target_pairs={{0,8},{8,0},{16,24},{24,16},{1,9},{9,1},{17,25},{25,17},{2,10},{10... | collective-permute-start | bytes 1081352 | tf_op jit(solution)/shard_map/ppermute | solution.py:705
  846.8 3.3 copy-start.17
  846.8 4.4 copy-start.16
  850.1 10.0 %collective-permute-start.19 = (bf16[64,2816]{1,0:T(8,128)(2,1)S(1)}, bf16[64,2816]{1,0:T(8,128)(2,1)S(1)}, u32[]{:S(2)}, u32[]{:S(2)}) collective-permute-start(bf16[64,2816]{1,0:T(8,128)(2,1)S(1)} %copy-done.17), channel_id=1, source_target_pairs={{0,16},{8,24},{16,0},{24,8},{1,17},{9,25},{17,1},{25,9},{2,18},{10... | collective-permute-start | bytes 1081352 | tf_op jit(solution)/shard_map/ppermute | solution.py:705
  851.2 16.8 %collective-permute-start.20 = (bf16[64,2816]{1,0:T(8,128)(2,1)S(1)}, bf16[64,2816]{1,0:T(8,128)(2,1)S(1)}, u32[]{:S(2)}, u32[]{:S(2)}) collective-permute-start(bf16[64,2816]{1,0:T(8,128)(2,1)S(1)} %copy-done.16), channel_id=1, source_target_pairs={{0,24},{8,16},{16,8},{24,0},{1,25},{9,17},{17,9},{25,1},{2,26},{10... | collective-permute-start | bytes 1081352 | tf_op jit(solution)/shard_map/ppermute | solution.py:705
  (2 other events, 2.1 us)

commit v3 on v2

--- a/solution.py
+++ b/solution.py
@@ -12,7 +12,7 @@
 MESH = pl.DeviceIdType.MESH
 F32 = jnp.float32
 BF16 = jnp.bfloat16
-VMEM_BYTES = 60 * 1024 * 1024
+VMEM_BYTES = 62 * 1024 * 1024
 
 
 def normalize_rows(field):
@@ -30,126 +30,6 @@
     )
 
 
-def rotary_factors(positions):
-    pairs = ROT // 2
-    inverse = jnp.power(10000.0, -jnp.arange(pairs, dtype=F32) / pairs)
-    angle = positions.astype(F32)[:, None] * inverse[None, :]
-    cosine, sine = jnp.cos(angle), jnp.sin(angle)
-    rows = positions.shape[0]
-    none = jnp.zeros((rows, HDIM - ROT), F32)
-    blank = jnp.zeros((rows, pairs), F32)
-    keep = jnp.concatenate([cosine, cosine, none + 1.0], axis=1)
-    left = jnp.concatenate([-sine, blank, none], axis=1)
-    right = jnp.concatenate([blank, sine, none], axis=1)
-    return keep, left, right
-
-
-def turn(field, factors, sign):
-    keep, left, right = factors
-    heads = field.shape[-1] // HDIM
-    pairs = ROT // 2
-    keep, left, right = (jnp.tile(t, (1, heads)) for t in (keep, left, right))
-    return (
-        field * keep
-        + jnp.roll(field, -pairs, axis=-1) * (left * sign)
-        + jnp.roll(field, pairs, axis=-1) * (right * sign)
-    )
-
-
-def exchange(axis, size, cid, items):
-    counts = [len(plan(0, 0)) for _, _, plan in items]
-    total = sum(counts)
-
-    def body(*refs):
-        ins = refs[: len(items)]
-        outs = refs[len(items) : 2 * len(items)]
-        send, recv, local = refs[2 * len(items) :]
-        me = lax.axis_index(axis)
-        barrier = pltpu.get_barrier_semaphore()
-        for k in range(1, size):
-            pl.semaphore_signal(
-                barrier, inc=1, device_id={axis: lax.rem(me + k, size)}, device_id_type=MESH
-            )
-        pl.semaphore_wait(barrier, size - 1)
-        copies = []
-        for k in range(1, size):
-            peer = lax.rem(me + k, size)
-            at = 0
-            for (_, _, plan), src, dst in zip(items, ins, outs):
-                for a, b in plan(me, peer):
-                    copy = pltpu.make_async_remote_copy(
-                        src_ref=src.at[a],
-                        dst_ref=dst.at[b],
-                        send_sem=send.at[k - 1, at],
-                        recv_sem=recv.at[k - 1, at],
-                        device_id={axis: peer},
-                        device_id_type=MESH,
-                    )
-                    copy.start()
-                    copies.append(copy)
-                    at += 1
-        at = 0
-        for (_, _, plan), src, dst in zip(items, ins, outs):
-            for a, b in plan(me, me):
-                copy = pltpu.make_async_copy(src.at[a], dst.at[b], local.at[at])
-                copy.start()
-                copies.append(copy)
-                at += 1
-        for copy in copies:
-            copy.wait()
-
-    anywhere = pl.BlockSpec(memory_space=pl.ANY)
-    return pl.pallas_call(
-        body,
-        out_shape=[jax.ShapeDtypeStruct(shape, x.dtype) for x, shape, _ in items],
-        in_specs=[anywhere] * len(items),
-        out_specs=[anywhere] * len(items),
-        scratch_shapes=[
-            pltpu.SemaphoreType.DMA((size - 1, total)),
-            pltpu.SemaphoreType.DMA((size - 1, total)),
-            pltpu.SemaphoreType.DMA((total,)),
-        ],
-        compiler_params=pltpu.CompilerParams(collective_id=cid, has_side_effects=True),
-    )(*[x for x, _, _ in items])
-
-
-def gather(axis, size, cid, *arrays):
-    return exchange(
-        axis,
-        size,
-        cid,
-        [(x, (size,) + x.shape, lambda me, peer: [(slice(None), me)]) for x in arrays],
-    )
-
-
-def swap_blocks(axis, size, cid, x):
-    return exchange(axis, size, cid, [(x, x.shape, lambda me, peer: [(peer, me)])])[0]
-
-
-def to_sequence(size, cid, x):
-    half = x.shape[1] // 2
-
-    def plan(me, peer):
-        return [
-            ((peer, pl.ds(0, half)), me),
-            ((peer, pl.ds(half, half)), 2 * size - 1 - me),
-        ]
-
-    return exchange("ctx", size, cid, [(x, (2 * size, half, x.shape[2]), plan)])[0]
-
-
-def from_sequence(size, cid, x):
-    half = x.shape[1]
-
-    def plan(me, peer):
-        return [
-            (peer, (me, pl.ds(0, half))),
-            (2 * size - 1 - peer, (me, pl.ds(half, half))),
-        ]
-
-    return exchange("ctx", size, cid, [(x, (size, 2 * half, x.shape[2]), plan)])[0]
-
-
 def last_dims(a, b):
     return lax.dot_general(a, b, (((1,), (1,)), ((), ())), preferred_element_type=F32)
 
@@ -163,7 +43,7 @@
 
 
 def attention_shapes(length):
-    block = min(256, length)
+    block = min(256 if length <= 1024 else 128, length)
     segments = min(4, length // block)
     return block, segments, length // block // segments
 
@@ -194,7 +74,7 @@
 class Copies:
     def __init__(self, send, recv, local):
         self.send, self.recv, self.local = send, recv, local
-        self.remotes, self.locals = [], []
+        self.remotes, self.locals, self.left = [], [], []
 
     def to(self, device, src, dst):
         at = len(self.remotes)
@@ -208,7 +88,13 @@
         )
         copy.start()
         self.remotes.append(copy)
+        self.left.append(copy)
         return copy
+
+    def gone(self, *copies):
+        for copy in copies:
+            copy.wait_send()
+            self.left = [other for other in self.left if other is not copy]
 
     def here(self, src, dst):
         copy = pltpu.make_async_copy(src, dst, self.local.at[len(self.locals)])
@@ -564,8 +450,7 @@
 
         over_tiles(width, 256, dh2_tile)
         put_pdh2 = links.here(h1, pdh2_o)
-        for copy in send_tok + [forward_tok]:
-            copy.wait_send()
+        links.gone(*send_tok, forward_tok)
 
         def result_tile(at, n):
             here = pl.ds(at, n)
@@ -574,10 +459,7 @@
         over_tiles(width, 256, result_tile)
         put_pout = links.here(tok, pout_o)
 
-        done = send_tok + [forward_tok]
-        for copy in links.remotes:
-            if not any(copy is other for other in done):
-                copy.wait_send()
+        links.gone(*links.left)
         for copy in (
             put_small, put_wq, put_seq, put_lse, put_mixed, put_r1, put_h2, put_dy, put_m, put_dgu,
             put_pdh2, put_pout,
@@ -644,44 +526,442 @@
     return dict(zip(outs, results))
 
 
-def attention_backward(qkv, lse, d_mixed, heads):
-    length = qkv.shape[0]
+def flip_bit(i, bit):
+    return i + (1 << bit) - (2 << bit) * ((i // (1 << bit)) % 2)
+
+
+def attend_back(x_ref, lse_ref, do_ref, d_ref, heads, head):
+    length = x_ref.shape[0]
     block, segments, inner = attention_shapes(length)
-
-    def body(x_ref, lse_ref, do_ref, d_ref):
-        d_ref[...] = jnp.zeros_like(d_ref)
+    q_at, k_at, v_at = (head_columns(heads, i, head) for i in range(3))
+    o_at = slice(head * HDIM, (head + 1) * HDIM)
+    for segment in range(segments):
+        count = (segment + 1) * inner * block
+        keys = x_ref[:count, k_at]
+        values = x_ref[:count, v_at]
+
+        def step(i, _):
+            start = pl.multiple_of((segment * inner + i) * block, block)
+            query = x_ref[pl.ds(start, block), q_at] * 0.125
+            dout = do_ref[pl.ds(start, block), o_at]
+            scores = causal(last_dims(keys, query), start)
+            probs = jnp.exp(scores - lse_ref[head : head + 1, pl.ds(start, block)])
+            d_probs = last_dims(values, dout)
+            centre = jnp.sum(probs * d_probs, axis=0, keepdims=True)
+            d_scores = (probs * (d_probs - centre)).astype(BF16)
+            d_ref[:count, v_at] += plain(probs.astype(BF16), dout)
+            d_ref[:count, k_at] += plain(d_scores, query)
+            d_ref[pl.ds(start, block), q_at] = first_dims(keys, d_scores).T * 0.125
+            return 0
+
+        if inner == 1:
+            step(0, 0)
+        else:
+            lax.fori_loop(0, inner, step, 0)
+
+
+class GroupSum:
+    def __init__(self, links, dp, nd, rows, part, ra, rb):
+        self.links, self.rows = links, rows
+        self.part, self.ra, self.rb = part, ra, rb
+        self.near, self.across, self.far = flip_one(dp), (dp + 2) % nd, nd - 1 - dp
+        self.dp = dp
+        block = lambda ref, b: ref.at[halves(b * rows, rows)]
+        self.a = [
+            links.to({"dp": self.near}, block(part, self.far), block(ra, 0)),
+            links.to({"dp": self.near}, block(part, self.near), block(ra, 1)),
+        ]
+
+    def middle(self):
+        rows, at = self.rows, halves(self.across * self.rows, self.rows)
+        self.a[0].wait_recv()
+        self.part[at, :] = (
+            self.part[at, :].astype(F32) + self.ra[:rows, :].astype(F32)
+        ).astype(BF16)
+        self.b = self.links.to({"dp": self.across}, self.part.at[at], self.rb)
+
+    def total(self):
+        rows, at = self.rows, halves(self.dp * self.rows, self.rows)
+        self.a[1].wait_recv()
+        self.b.wait_recv()
+        return (
+            self.part[at, :].astype(F32)
+            + self.ra[rows:, :].astype(F32)
+            + self.rb[...].astype(F32)
+        )
+
+
+class Gradient:
+    def __init__(self, links, ctx, nc, left, right, slots, landing, stage):
+        self.links, self.ctx, self.nc = links, ctx, nc
+        self.left, self.right, self.slots = left, right, slots
+        self.landing = landing
+        self.stage = stage.at[pl.ds(0, slots.shape[1]), pl.ds(0, slots.shape[2])]
+        self.sent = {}
+
+    def _landing(self, bit, j):
+        base = sum(self.nc >> (b + 1) for b in range(bit))
+        return self.landing.at[base + (j >> bit)]
+
+    def _owner(self, e):
+        owner = self.ctx
+        bit = 0
+        while e >> bit:
+            if (e >> bit) & 1:
+                owner = flip_bit(owner, bit)
+            bit += 1
+        return owner
+
+    def give(self, j):
+        left = self.left[self._owner(2 * j + 1)]
+
+        def step(at, n):
+            here = pl.ds(at, n)
+            self.slots[j, :, here] = plain(left, self.right[:, here]).astype(BF16)
+
+        over_tiles(self.right.shape[1], 512, step)
+        self.sent[0, j] = self.links.to(
+            {"ctx": flip_bit(self.ctx, 0)}, self.slots.at[j], self._landing(0, j)
+        )
+
+    def _load(self, bit, j):
+        self.sent[bit, j if bit == 0 else j + (1 << (bit - 1))].wait_recv()
+        copy = self.links.here(self._landing(bit, j), self.stage)
+        copy.wait()
+
+    def keep(self, j):
+        left = self.left[self._owner(2 * j)]
+        self._load(0, j)
+        self.links.gone(self.sent[0, j])
+
+        def step(at, n):
+            here = pl.ds(at, n)
+            acc = plain(left, self.right[:, here]) + self.stage[:, here].astype(F32)
+            self.slots[j, :, here] = acc.astype(BF16)
+
+        over_tiles(self.right.shape[1], 512, step)
+        self._pass(1, j)
+
+    def _pass(self, bit, j):
+        low = j & -j
+        if j and low == 1 << (bit - 1):
+            self.sent[bit, j] = self.links.to(
+                {"ctx": flip_bit(self.ctx, bit)}, self.slots.at[j], self._landing(bit, j - low)
+            )
+
+    def add(self, bit, j):
+        self._load(bit, j)
+
+        def step(at, n):
+            here = pl.ds(at, n)
+            acc = self.slots[j, :, here].astype(F32) + self.stage[:, here].astype(F32)
+            self.slots[j, :, here] = acc.astype(BF16)
+
+        over_tiles(self.right.shape[1], 512, step)
+        self._pass(bit + 1, j)
+
+    def order(self):
+        return sorted(range(self.nc // 2), key=lambda j: (j & -j) or self.nc)
+
+    def finish(self, after=1):
+        bit = after
+        while 1 << bit < self.nc:
+            step = 1 << bit
+            for j in sorted(range(0, self.nc // 2, step), key=lambda j: (j & -j) or self.nc):
+                self.add(bit, j)
+            bit += 1
+
+
+def backward(nd, nc, f, small, tokens, w_out, lefts):
+    rows, width = tokens.shape
+    half = rows // 2
+    many = nd * rows
+    length, wide = f["seq"].shape
+    heads = f["lse"].shape[0]
+    span = heads * HDIM
+    groups = nc // nd
+    cols = groups * span
+    cot_rows = f["dy"]
+    keep_t, sine_t = rotary_pair_tables(length)
+    chunk = min(length, 1024)
+    names = ("gu", "down", "out", "qkv")
+    right_cols = {"gu": f["dgu"].shape[1], "down": width, "out": width, "qkv": 3 * cols}
+    left_rows = {k: lefts[k].shape[1] for k in names}
+    slots = nc // 2
+
+    def body(
+        h2_l, m_l, mixed_l, h1_l, dy_i, dgu_i, wq_i, seq_i, lse_i, r1_i, pdh2_i, pout_i,
+        small_i, tok_i, wo_i, keep_i, sine_i,
+        out_o, tg_o, gu_o, down_o, out_g_o, qkv_o, sums_o, land_gu, land_down, land_out, land_qkv,
+        l_gu, l_down, l_out, l_qkv, dgu, dy, da, dq, s_gu, s_down, s_out, s_qkv,
+        stage,
+        part, ra, rb, ra2, rb2, r1, dr1, x, sm, wq, wo, seq, lse,
+        dmix, dseq, dx, keep, sine, dback, sums, sums_in,
+        send, recv, local,
+    ):
+        dp, ctx = lax.axis_index("dp"), lax.axis_index("ctx")
+        near, across, far = flip_one(dp), (dp + 2) % nd, nd - 1 - dp
+        links = Copies(send, recv, local)
+        blocks = lambda ref, b: ref.at[halves(b * rows, rows)]
+        own_at = halves(dp * rows, rows)
+
+        get_part = links.here(pdh2_i, part)
+        get_gu = [links.here(h2_l, l_gu), links.here(dgu_i, dgu)]
+        get_first = [links.here(a, b) for a, b in ((r1_i, r1), (small_i, sm), (dy_i, dy))]
+        get_wo = links.here(wo_i, wo)
+        get_down = links.here(m_l, l_down)
+        get_attn = [
+            links.here(a, b)
+            for a, b in ((seq_i, seq), (lse_i, lse))
+        ]
+
+        def tables(c):
+            at = pl.ds(c * chunk, chunk)
+            return [links.here(a.at[at], b) for a, b in ((keep_i, keep), (sine_i, sine))]
+
+        get_tables = tables(0)
+        get_out = links.here(mixed_l, l_out)
+        get_qkv = [links.here(a, b) for a, b in ((wq_i, wq), (h1_l, l_qkv), (tok_i, x))]
+
+        gu = Gradient(links, ctx, nc, l_gu, dgu, s_gu, land_gu, stage)
+        down = Gradient(links, ctx, nc, l_down, dy, s_down, land_down, stage)
+        out = Gradient(links, ctx, nc, l_out, da, s_out, land_out, stage)
+        qkv = Gradient(links, ctx, nc, l_qkv, dq, s_qkv, land_qkv, stage)
+        order = gu.order()
+        quarter = max(1, len(order) // 4)
+        turns = [order[i : i + quarter] for i in range(0, len(order), quarter)]
+
+        def gain(row):
+            lines = [
+                sm[b, row * 4 + q : row * 4 + q + 1, :]
+                for b in range(nd)
+                for q in range(width // nd // 128)
+            ]
+            return jnp.concatenate(lines, axis=1)
+
+        meet((("dp", nd), ("ctx", nc)))
+        get_part.wait()
+        sum2 = GroupSum(links, dp, nd, rows, part, ra, rb)
+        for copy in get_gu:
+            copy.wait()
+        for j in turns[0]:
+            gu.give(j)
+        sum2.middle()
+        for copy in get_first:
+            copy.wait()
+        for j in turns[1]:
+            gu.give(j)
+
+        dh2 = sum2.total()
+        hat, inverse = normalize_rows(r1[...])
+        dr1[...] = dy[own_at, :].astype(F32) + norm_reverse(dh2, gain(2), hat, inverse)
+        da[own_at, :] = dr1[...].astype(BF16)
+        send_da = [links.to({"dp": e}, blocks(da, dp), blocks(da, dp)) for e in (near, across)]
+        sums[2:3, :] = jnp.sum(dh2 * hat, axis=0, keepdims=True)
+        sums[3:4, :] = jnp.sum(dh2, axis=0, keepdims=True)
+        get_down.wait()
+        send_da[1].wait_recv()
+        forward_da = links.to({"dp": near}, blocks(da, across), blocks(da, across))
+        get_wo.wait()
+        send_da[0].wait_recv()
+        forward_da.wait_recv()
+
+        for g in range(groups):
+            dmix[g] = last_dims(da[...], wo[g * span : (g + 1) * span, :]).astype(BF16)
+        mirror = 2 * nc - 1 - ctx
+        go = []
+        for k in range(1, nc):
+            peer = lax.rem(ctx + k, nc)
+            s, g = peer // groups, peer % groups
+            for i, block in enumerate((ctx, mirror)):
+                go.append(
+                    links.to(
+                        {"ctx": peer},
+                        dmix.at[g, halves(s * rows + i * half, half)],
+                        dseq.at[halves(block * half, half)],
+                    )
+                )
+        s, g = ctx // groups, ctx % groups
+        stay = [
+            links.here(
+                dmix.at[g, halves(s * rows + i * half, half)], dseq.at[halves(block * half, half)]
+            )
+            for i, block in enumerate((ctx, mirror))
+        ]
+        dx[...] = jnp.zeros_like(dx)
+        for j in turns[0]:
+            gu.keep(j)
+        for copy in get_attn + stay:
+            copy.wait()
+        for copy in go:
+            copy.wait_recv()
+        for j in turns[2]:
+            gu.give(j)
         for head in range(heads):
-            q_at, k_at, v_at = (head_columns(heads, i, head) for i in range(3))
-            o_at = slice(head * HDIM, (head + 1) * HDIM)
-            for segment in range(segments):
-                count = (segment + 1) * inner * block
-                keys = x_ref[:count, k_at]
-                values = x_ref[:count, v_at]
-
-                def step(i, _):
-                    start = pl.multiple_of((segment * inner + i) * block, block)
-                    query = x_ref[pl.ds(start, block), q_at] * 0.125
-                    dout = do_ref[pl.ds(start, block), o_at]
-                    scores = causal(last_dims(keys, query), start)
-                    probs = jnp.exp(scores - lse_ref[head : head + 1, pl.ds(start, block)])
-                    d_probs = last_dims(values, dout)
-                    centre = jnp.sum(probs * d_probs, axis=0, keepdims=True)
-                    d_scores = (probs * (d_probs - centre)).astype(BF16)
-                    d_ref[:count, v_at] += plain(probs.astype(BF16), dout)
-                    d_ref[:count, k_at] += plain(d_scores, query)
-                    d_ref[pl.ds(start, block), q_at] = first_dims(keys, d_scores).T * 0.125
-                    return 0
-
-                if inner == 1:
-                    step(0, 0)
-                else:
-                    lax.fori_loop(0, inner, step, 0)
-
+            attend_back(seq, lse, dseq, dx, heads, head)
+        for c in range(length // chunk):
+            for copy in get_tables if c == 0 else tables(c):
+                copy.wait()
+            here = slice(c * chunk, (c + 1) * chunk)
+            for at in range(0, wide, 128):
+                n = min(128, wide - at)
+                u = dx[here, at : at + n]
+                if at < 2 * span:
+                    u = rotate_pair(u, keep[...], -sine[...])
+                seq[here, at : at + n] = u.astype(BF16)
+
+        back = []
+        for k in range(1, nc):
+            peer = lax.rem(ctx + k, nc)
+            for i, block in enumerate((peer, 2 * nc - 1 - peer)):
+                back.append(
+                    links.to(
+                        {"ctx": peer},
+                        seq.at[halves(block * half, half)],
+                        dback.at[g, halves(s * rows + i * half, half)],
+                    )
+                )
+        stay = [
+            links.here(
+                seq.at[halves(block * half, half)], dback.at[g, halves(s * rows + i * half, half)]
+            )
+            for i, block in enumerate((ctx, mirror))
+        ]
+        for j in turns[3]:
+            gu.give(j)
+        for j in turns[1]:
+            gu.keep(j)
+        for j in turns[0]:
+            down.give(j)
+        for copy in get_qkv + stay:
+            copy.wait()
+        for copy in back:
+            copy.wait_recv()
+        for g_ in range(groups):
+            for j in range(3):
+                at = j * cols + g_ * span
+                dq[:, at : at + span] = dback[g_, :, j * span : (j + 1) * span]
+
+        def dh1_tile(at, n):
+            here = pl.ds(at, n)
+            part[:, here] = last_dims(dq[...], wq[here, :]).astype(BF16)
+
+        links.gone(*sum2.a, sum2.b)
+        over_tiles(width, 256, dh1_tile)
+        sum1 = GroupSum(links, dp, nd, rows, part, ra2, rb2)
+        for j in turns[1]:
+            down.give(j)
+        sums[4:, :] = jnp.zeros((nd, width), F32)
+        sums[pl.ds(4 + dp, 1), : 3 * cols] = jnp.sum(dq[...].astype(F32), axis=0, keepdims=True)
+        sum1.middle()
+        for j in turns[2] + turns[3]:
+            down.give(j)
+        dh1 = sum1.total()
+        hat1, inverse1 = normalize_rows(x[...].astype(F32))
+        sums[0:1, :] = jnp.sum(dh1 * hat1, axis=0, keepdims=True)
+        sums[1:2, :] = jnp.sum(dh1, axis=0, keepdims=True)
+        partners = [("ctx", flip_bit(ctx, b)) for b in range(nc.bit_length() - 1)]
+        partners += [("dp", flip_bit(dp, b)) for b in range(nd.bit_length() - 1)]
+
+        def exchange_sums(i):
+            copy = links.to({partners[i][0]: partners[i][1]}, sums, sums_in.at[i])
+            copy.wait_recv()
+            links.gone(copy)
+            sums[...] += sums_in[i]
+
+        dr1[...] += norm_reverse(dh1, gain(0), hat1, inverse1)
+        put_tg = links.here(dr1, tg_o)
+        links.gone(*sum1.a, sum1.b)
+        get_pout = links.here(pout_i, part)
+        get_pout.wait()
+        sum0 = GroupSum(links, dp, nd, rows, part, ra, rb)
+        for j in turns[2]:
+            gu.keep(j)
+        for j in order:
+            qkv.give(j)
+        get_out.wait()
+        sum0.middle()
+        for j in order:
+            out.give(j)
+        for j in turns[3]:
+            gu.keep(j)
+        x[...] = (r1[...] + sum0.total()).astype(BF16)
+        put_out = links.here(x, out_o)
+        for i in range(len(partners)):
+            exchange_sums(i)
+        for piece, before in ((down, gu), (qkv, down), (out, qkv)):
+            for j in order:
+                piece.keep(j)
+            before.finish()
+        out.finish()
+        put = [
+            links.here(s_gu.at[0], gu_o),
+            links.here(s_down.at[0], down_o),
+            links.here(s_out.at[0], out_g_o),
+            links.here(s_qkv.at[0], qkv_o),
+        ]
+        put_sums = [links.here(sums, sums_o), put_tg, put_out]
+        links.gone(*links.left)
+        for copy in put + put_sums:
+            copy.wait()
+
+    anywhere = pl.BlockSpec(memory_space=pl.ANY)
+    shape = jax.ShapeDtypeStruct
+    landings = nc - 1
+    outs = [
+        ((rows, width), BF16),
+        ((rows, width), F32),
+        *[((left_rows[k], right_cols[k]), BF16) for k in names],
+        ((4 + nd, width), F32),
+        *[((landings, left_rows[k], right_cols[k]), BF16) for k in names],
+    ]
+    scratch = [
+        *[((nc, left_rows[k], many), BF16) for k in names],
+        ((many, right_cols["gu"]), BF16),
+        ((many, width), BF16),
+        ((many, width), BF16),
+        ((many, 3 * cols), BF16),
+        *[((slots, left_rows[k], right_cols[k]), BF16) for k in names],
+        ((max(left_rows.values()), max(right_cols.values())), BF16),
+        ((many, width), BF16),
+        *[((2 * rows, width), BF16), ((rows, width), BF16)] * 2,
+        ((rows, width), F32),
+        ((rows, width), F32),
+        ((rows, width), BF16),
+        (small.shape, F32),
+        ((width, 3 * cols), BF16),
+        ((cols, width), BF16),
+        ((length, wide), BF16),
+        ((heads, length), F32),
+        ((groups, many, span), BF16),
+        ((length, span), BF16),
+        ((length, wide), F32),
+        ((chunk, 128), F32),
+        ((chunk, 128), F32),
+        ((groups, many, wide), BF16),
+        ((4 + nd, width), F32),
+        ((nc.bit_length() + nd.bit_length() - 2, 4 + nd, width), F32),
+    ]
+    remotes = 9 + 3 + 4 * (nc - 1) + 4 * (nc - 1) + (nc - 1) + 3 + 8
     return pl.pallas_call(
         body,
-        out_shape=jax.ShapeDtypeStruct(qkv.shape, F32),
-        compiler_params=pltpu.CompilerParams(vmem_limit_bytes=VMEM_BYTES),
-    )(qkv, lse, d_mixed)
+        out_shape=[shape(*o) for o in outs],
+        in_specs=[anywhere] * 17,
+        out_specs=[anywhere] * len(outs),
+        scratch_shapes=[pltpu.VMEM(*s) for s in scratch]
+        + [
+            pltpu.SemaphoreType.DMA((remotes,)),
+            pltpu.SemaphoreType.DMA((remotes,)),
+            pltpu.SemaphoreType.DMA((40 + 4 * nc,)),
+        ],
+        compiler_params=pltpu.CompilerParams(
+            collective_id=1, has_side_effects=True, vmem_limit_bytes=VMEM_BYTES
+        ),
+    )(
+        lefts["gu"], lefts["down"], lefts["out"], lefts["qkv"],
+        f["dy"], f["dgu"], f["wq"], f["seq"], f["lse"], f["r1"], f["pdh2"], f["pout"],
+        small, tokens, w_out, keep_t, sine_t,
+    )
 
 
 def take(x, index):
@@ -690,130 +970,64 @@
 
 def shards(tokens, cotangent, w_qkv, b_qkv, w_out, w_gate, w_up, w_down, norms):
     width = tokens.shape[-1]
-    half = tokens.shape[3]
-    rows = 2 * half
+    rows = 2 * tokens.shape[3]
     nd, nc = lax.axis_size("dp"), lax.axis_size("ctx")
     dp, ctx = lax.axis_index("dp"), lax.axis_index("ctx")
-    heads_here = HEADS // nd
-    groups = nc // nd
-    heads_mine = heads_here // groups
-    span = heads_mine * HDIM
     many = nd * rows
-
-    def flip(x, axis, bits):
-        size = nd if axis == "dp" else nc
-        return lax.ppermute(x, axis, [(i, i ^ bits) for i in range(size)])
-
-    def sum_over_dp(partial):
-        blocks = partial.astype(BF16).reshape(nd, rows, width)
-        total = take(blocks, dp).astype(F32)
-        for k in range(1, nd):
-            total = total + flip(take(blocks, dp ^ k), "dp", k).astype(F32)
-        return total
-
-    def sum_over_ctx(left, right, outer):
+    hidden = w_gate.shape[1] // nd
+    x = tokens.reshape(rows, width)
+
+    small = jnp.concatenate([norms.reshape(-1), b_qkv]).astype(F32)
+    small = jnp.pad(small, (0, -small.shape[0] % 1024)).reshape(-1, 128)
+    f = forward(
+        nd, nc, x, cotangent.reshape(rows, width), small, w_qkv, w_gate, w_up, w_out, w_down
+    )
+
+    def by_owner(left, outer):
         part = left.shape[1] // (outer * nc)
-        split = left.reshape(many, outer, nc // 2, 2, part).transpose(3, 0, 2, 1, 4)
-        odd, place = ctx % 2, ctx // 2
-        size = (nc // 2, outer * part, right.shape[1])
-        sent = first_dims(take(split, 1 - odd).reshape(many, -1), right).astype(BF16)
-        got = flip(sent, "ctx", 1)
-        kept = first_dims(take(split, odd).reshape(many, -1), right) + got.astype(F32)
-        kept = kept.astype(BF16).reshape(size)
-        total = take(kept, place).astype(F32)
-        for k in range(1, nc // 2):
-            block = take(kept, lax.rem(place + k, nc // 2))
-            total = total + lax.ppermute(
-                block, "ctx", [(i, (i + 2 * k) % nc) for i in range(nc)]
-            ).astype(F32)
-        return total
-
-    def to_rows(total, outer):
-        blocks = total.astype(BF16).reshape(nd, -1, total.shape[1])
+        left = left.T.reshape(outer, nc, part, many).transpose(1, 0, 2, 3)
+        left = left.reshape(nc, outer * part, many)
+        return jnp.pad(left, ((0, 0), (0, -left.shape[1] % 16), (0, 0)))
+
+    lefts = {
+        "gu": by_owner(f["h2"], nd),
+        "down": by_owner(f["m"], 1),
+        "out": by_owner(f["mixed"].transpose(1, 0, 2).reshape(many, -1), 1),
+        "qkv": by_owner(f["h1"], nd),
+    }
+    result, tokens_grad, g_gu, g_down, g_out, g_qkv, sums = backward(
+        nd, nc, f, f["small"], x, w_out, lefts
+    )[:7]
+
+    def to_rows(total):
+        blocks = total.reshape(nd, -1, total.shape[1])
         part, cols = blocks.shape[1:]
         out = jnp.zeros((part, nd, cols), BF16)
         for k in range(nd):
             block = take(blocks, dp ^ k)
             if k:
-                block = flip(block, "dp", k)
+                block = lax.ppermute(block, "dp", [(i, i ^ k) for i in range(nd)])
             out = lax.dynamic_update_slice(out, block[:, None], (0, dp ^ k, 0))
         return out.astype(F32)
 
-    hidden = w_gate.shape[1] // nd
-    small = jnp.concatenate([norms.reshape(-1), b_qkv]).astype(F32)
-    small = jnp.pad(small, (0, -small.shape[0] % 1024)).reshape(-1, 128)
-    f = forward(
-        nd, nc, tokens.reshape(rows, width), cotangent.reshape(rows, width), small,
-        w_qkv, w_gate, w_up, w_out, w_down,
-    )
-    h1, dyb, wq, seq, lse, r1, h2 = (f[k] for k in ("h1", "dy", "wq", "seq", "lse", "r1", "h2"))
-    m, d_gu = f["m"], f["dgu"]
-    gains = f["small"].reshape(nd, -1)[:, : 4 * (width // nd)].reshape(nd, 4, -1)
-    gains = gains.transpose(1, 0, 2).reshape(4, width)
-    mixed = f["mixed"].transpose(1, 0, 2).reshape(many, -1)
-    x = tokens.reshape(rows, width).astype(F32)
-    hat2, inverse2 = normalize_rows(r1)
-    result = r1 + sum_over_dp(f["pout"])
-
-    grad_down = sum_over_ctx(m, dyb, 1)
-    partial = f["pdh2"].reshape(nd, rows, width)
-    dh2 = jnp.sum(swap_blocks("dp", nd, 5, partial).astype(F32), axis=0)
-    grad_gu = to_rows(sum_over_ctx(h2, d_gu, nd), nd)
-    dy = cotangent.reshape(rows, width).astype(F32)
-    dr1 = dy + norm_reverse(dh2, gains[2], hat2, inverse2)
-    da = gather("dp", nd, 6, dr1.astype(BF16))[0].reshape(many, width)
-    grad_out = sum_over_ctx(mixed, da, 1)
-    d_mixed = last_dims(da, w_out).astype(BF16)
-    packed = d_mixed.reshape(nd, rows, groups, span).transpose(0, 2, 1, 3).reshape(nc, rows, span)
-    d_seq = to_sequence(nc, 7, packed).reshape(-1, span)
-    d_qkv_seq = attention_backward(seq, lse, d_seq, heads_mine)
-    everywhere = rotary_factors(jnp.arange(2 * nc * half, dtype=jnp.int32))
-    d_qkv_seq = jnp.concatenate(
-        [
-            turn(d_qkv_seq[:, : 2 * span], everywhere, -1.0).astype(BF16),
-            d_qkv_seq[:, 2 * span :].astype(BF16),
-        ],
-        axis=1,
-    )
-    d_qkv = from_sequence(nc, 8, d_qkv_seq.reshape(2 * nc, half, 3 * span))
-    d_qkv = d_qkv.reshape(nd, groups, rows, 3, span).transpose(0, 2, 3, 1, 4).reshape(many, -1)
-    partial = last_dims(d_qkv, wq).astype(BF16).reshape(nd, rows, width)
-    grad_qkv = to_rows(sum_over_ctx(h1, d_qkv, nd), nd)
+    grad_gu = to_rows(g_gu)
+    grad_qkv = to_rows(g_qkv)
     grad_qkv = grad_qkv.reshape(-1, nd, 3, width // nd).transpose(0, 2, 1, 3).reshape(-1, 3 * width)
-    dh1 = jnp.sum(swap_blocks("dp", nd, 9, partial).astype(F32), axis=0)
-    hat1, inverse1 = normalize_rows(x)
-    tokens_grad = dr1 + norm_reverse(dh1, gains[0], hat1, inverse1)
-
-    norm_sums = jnp.stack(
-        [
-            jnp.sum(dh1 * hat1, axis=0),
-            jnp.sum(dh1, axis=0),
-            jnp.sum(dh2 * hat2, axis=0),
-            jnp.sum(dh2, axis=0),
-        ]
-    )
-    bias_sums = jnp.sum(d_qkv.astype(F32), axis=0)
-    sums = jnp.concatenate([norm_sums.reshape(-1), bias_sums]).reshape(-1, 128)
-    sums = jnp.sum(gather("ctx", nc, 10, sums)[0], axis=0).reshape(-1)
-    norm_part = sums[: 4 * width].reshape(4, nd, nc, -1)
-    norm_part = lax.dynamic_index_in_dim(norm_part, ctx, 2, keepdims=False)
-    small = jnp.concatenate([norm_part.reshape(-1), sums[4 * width :]])
-    pad = -small.shape[0] % 1024
-    sums = gather("dp", nd, 11, jnp.pad(small, (0, pad)).reshape(-1, 128))[0].reshape(nd, -1)
-    norm_sums = jnp.sum(sums[:, : norm_part.size], axis=0).reshape(norm_part.shape)
-    norms_grad = lax.dynamic_index_in_dim(norm_sums, dp, 1, keepdims=False)
-    bias_sums = sums[:, norm_part.size : small.shape[0]].reshape(nd, 3, -1).transpose(1, 0, 2)
-    bias_grad = take(bias_sums.reshape(nd * nc, -1), dp * nc + ctx)
+    part_down, part_out = w_down.shape[0] // nc, w_out.shape[0] // nc
+
+    place = dp * nc + ctx
+    norms_grad = lax.dynamic_index_in_dim(sums[:4].reshape(4, nd * nc, -1), place, 1, keepdims=False)
+    bias = sums[4:, : 3 * width // nd].reshape(nd, 3, -1).transpose(1, 0, 2)
 
     return (
-        result.astype(BF16).reshape(tokens.shape),
+        result.reshape(tokens.shape),
         tokens_grad.reshape(tokens.shape),
         grad_qkv,
-        bias_grad,
-        grad_out,
-        grad_gu.reshape(-1, nd, 2, hidden)[:, :, 0].reshape(-1, nd * hidden),
-        grad_gu.reshape(-1, nd, 2, hidden)[:, :, 1].reshape(-1, nd * hidden),
-        grad_down,
+        take(bias.reshape(nd * nc, -1), place),
+        g_out[:part_out].astype(F32),
+        grad_gu[:, :, :hidden].reshape(-1, nd * hidden),
+        grad_gu[:, :, hidden:].reshape(-1, nd * hidden),
+        g_down[:part_down].astype(F32),
         norms_grad,
     )
 

time: 884 us -> 814 us (0.921)
  the two profiles are of different devices: /device:TPU:9 before, /device:TPU:0 now
where the time goes in v3:
time: 814 us; the launch traced here: 809 us
  Pallas kernels  714 us (88%)
  local copies, waits for them, and re-layouts  82.4 us (10%)
    pallas_call x1, Pallas kernels, backward(): pl.pallas_call(body, out_shape=[shape(*o) for o in outs], in_specs=[anywh...  510 us
    pallas_call x1, Pallas kernels, forward(): pl.pallas_call(body, out_shape=[shape(*o) for o in outs.values()], in_spe...  204 us
    dynamic_update_slice x8, local copies, waits for them, and re-layouts, to_rows(): out = lax.dynamic_update_slice(out, block[:, None], (0, dp ^ k, 0))  45.3 us
  transfers between devices with their start and end apart: 6, of which 2 were waited for; matrix products, arithmetic and copies ran while one was open for 4% of the time, Pallas kernels for 0%

profile of v3, /device:TPU:0, one launch (start us, length us, event | category | flops | bytes accessed | tf_op | source)
XLA Modules:
  0.0 808.8 jit_solution(3588573794114561598)
XLA Ops:
  0.7 0.7 copy.46
  1.4 1.3 fusion.4.small_i
  2.6 203.9 %shard_map.196 = (bf16[512,2048]{1,0:T(8,128)(2,1)}, bf16[512,2048]{1,0:T(8,128)(2,1)}, bf16[2048,1536]{1,0:T(8,128)(2,1)}, bf16[1024,768]{1,0:T(8,128)(2,1)}, f...) custom-call(bf16[128,2048]{1,0:T(8,128)(2,1)} %bitcast.76, ...), custom_call_target="tpu_custom_call" | custom-call | tf_op jit(solution)/shard_map/pallas_call | solution.py:511
  206.6 2.9 copy.39
  209.5 1.5 copy.40
  211.0 3.3 copy.35
  214.3 1.5 copy.36
  215.8 0.5 copy-done.1
  216.3 1.5 copy.37
  217.8 1.0 copy.38
  218.8 510.4 %shard_map.197 = (bf16[128,2048]{1,0:T(8,128)(2,1)}, f32[128,2048]{1,0:T(8,128)}, bf16[256,2816]{1,0:T(8,128)(2,1)}, bf16[176,2048]{1,0:T(8,128)(2,1)}, bf16[64,...) custom-call(bf16[8,256,512]{2,1,0:T(8,128)(2,1)} %bitcast.69, ...), custom_call_target="tpu_custom_call" | custom-call | tf_op jit(solution)/shard_map/pallas_call | solution.py:946
  729.2 2.4 dynamic-slice_bitcast_fusion
  731.6 1.6 collective-permute-start.4
  733.2 0.3 collective-permute-start.5
  733.5 0.4 collective-permute-start
  733.9 1.5 collective-permute-start.1
  735.5 0.6 copy.42
  736.0 1.3 convert_element_type.15
  737.3 0.8 convert_element_type.13
  738.1 0.1 reshape.107
  738.2 0.1 reshape.103
  738.3 0.6 constant_dynamic-slice_fusion.1
  738.9 0.6 constant_dynamic-slice_fusion
  739.5 0.4 broadcast_in_dim.35
  739.8 10.2 %dynamic_update_slice.28 = bf16[64,4,2816]{2,1,0:T(4,128)(2,1)S(1)} dynamic-update-slice(bf16[64,4,2816]{2,1,0:T(4,128)(2,1)S(1)} %broadcast_in_dim.35, bf16[64,1,2816]{2,1,0:T(2,128)(2,1)S(1)} %copy.42, s32[]{:T(128)} %constant.50.clone.1, s32[]{:T(128)S(6)} %select_n.32, s32[]{:T(128)} %constant.50.clone.1) | dynamic-update-slice | bytes 720900 | tf_op jit(solution)/shard_map/dynamic_update_slice | solution.py:1010
  750.0 0.9 broadcast_in_dim.30
  751.0 0.7 bitcast_dynamic-update-slice_fusion.3
  751.6 0.0 collective-permute-start.2
  751.7 1.6 bitcast_dynamic-update-slice_fusion.2
  753.3 1.4 collective-permute-done.1
  754.7 1.6 bitcast_dynamic-update-slice_fusion.1
  756.3 2.4 collective-permute-done.2
  758.7 0.7 bitcast_dynamic-update-slice_fusion
  759.4 2.7 reshape.114
  762.2 2.2 copy.41
  764.4 3.4 reshape.111
  767.8 1.5 copy.43
  769.3 1.5 copy.44
  770.9 2.4 copy.45
  773.3 10.1 %dynamic_update_slice.29 = bf16[64,4,2816]{2,1,0:T(4,128)(2,1)S(1)} dynamic-update-slice(bf16[64,4,2816]{2,1,0:T(4,128)(2,1)S(1)} %dynamic_update_slice.28, bf16[64,1,2816]{2,1,0:T(2,128)(2,1)S(1)} %copy.43, s32[]{:T(128)} %constant.50.clone.1, s32[]{:T(128)S(6)} %select_n.33, s32[]{:T(128)} %constant.50.clone.1) | dynamic-update-slice | bytes 720900 | tf_op jit(solution)/shard_map/dynamic_update_slice | solution.py:1010
  783.4 0.0 copy-start
  783.4 10.2 %dynamic_update_slice.30 = bf16[64,4,2816]{2,1,0:T(4,128)(2,1)S(1)} dynamic-update-slice(bf16[64,4,2816]{2,1,0:T(4,128)(2,1)S(1)} %dynamic_update_slice.29, bf16[64,1,2816]{2,1,0:T(2,128)(2,1)S(1)} %copy.44, s32[]{:T(128)} %constant.50.clone.1, s32[]{:T(128)S(6)} %select_n.34, s32[]{:T(128)} %constant.50.clone.1) | dynamic-update-slice | bytes 720900 | tf_op jit(solution)/shard_map/dynamic_update_slice | solution.py:1010
  793.6 10.2 %dynamic_update_slice.31 = bf16[64,4,2816]{2,1,0:T(4,128)(2,1)S(1)} dynamic-update-slice(bf16[64,4,2816]{2,1,0:T(4,128)(2,1)S(1)} %dynamic_update_slice.30, bf16[64,1,2816]{2,1,0:T(2,128)(2,1)S(1)} %copy-done, s32[]{:T(128)} %constant.50.clone.1, s32[]{:T(128)S(6)} %select_n.35, s32[]{:T(128)} %constant.50.clone.1) | dynamic-update-slice | bytes 720900 | tf_op jit(solution)/shard_map/dynamic_update_slice | solution.py:1010
  803.9 0.6 fusion.5
  804.4 1.2 copy.47
  805.6 1.2 copy.48
  806.8 0.8 copy.59
  807.6 1.0 copy.60
  (24 shorter events, 0.1 us)
Async XLA Ops:
  214.3 2.0 copy-start.1
  215.8 2.0 copy-start.6
  729.2 4.3 copy-start.3
  729.2 6.2 copy-start.8
  731.6 4.4 copy-start.4
  731.6 36.2 %collective-permute-start.3 = (bf16[64,2816]{1,0:T(8,128)(2,1)}, bf16[64,2816]{1,0:T(8,128)(2,1)}, u32[]{:S(2)}, u32[]{:S(2)}) collective-permute-start(bf16[64,2816]{1,0:T(8,128)(2,1)} %get-tuple-element.53), channel_id=1, source_target_pairs={{0,8},{8,0},{16,24},{24,16},{1,9},{9,1},{17,25},{25,17},{2,10},{10... | collective-permute-start | bytes 1081352 | tf_op jit(solution)/shard_map/ppermute | solution.py:1009
  731.6 37.7 %collective-permute-start.4 = (bf16[64,2816]{1,0:T(8,128)(2,1)}, bf16[64,2816]{1,0:T(8,128)(2,1)}, u32[]{:S(2)}, u32[]{:S(2)}) collective-permute-start(bf16[64,2816]{1,0:T(8,128)(2,1)} %get-tuple-element.52), channel_id=1, source_target_pairs={{0,16},{8,24},{16,0},{24,8},{1,17},{9,25},{17,1},{25,9},{2,18},{10... | collective-permute-start | bytes 1081352 | tf_op jit(solution)/shard_map/ppermute | solution.py:1009
  733.2 37.7 %collective-permute-start.5 = (bf16[64,2816]{1,0:T(8,128)(2,1)}, bf16[64,2816]{1,0:T(8,128)(2,1)}, u32[]{:S(2)}, u32[]{:S(2)}) collective-permute-start(bf16[64,2816]{1,0:T(8,128)(2,1)} %get-tuple-element.51), channel_id=1, source_target_pairs={{0,24},{8,16},{16,8},{24,0},{1,25},{9,17},{17,9},{25,1},{2,26},{10... | collective-permute-start | bytes 1081352 | tf_op jit(solution)/shard_map/ppermute | solution.py:1009
  733.5 3.8 copy-start.7
  733.5 18.1 %collective-permute-start = (bf16[64,1536]{1,0:T(8,128)(2,1)S(1)}, bf16[64,1536]{1,0:T(8,128)(2,1)}, u32[]{:S(2)}, u32[]{:S(2)}) collective-permute-start(bf16[64,1536]{1,0:T(8,128)(2,1)S(1)} %get-tuple-element.57), channel_id=1, source_target_pairs={{0,8},{8,0},{16,24},{24,16},{1,9},{9,1},{17,25},{25,17},{2,10},{10... | collective-permute-start | bytes 589832 | tf_op jit(solution)/shard_map/ppermute | solution.py:1009
  733.9 20.8 %collective-permute-start.1 = (bf16[64,1536]{1,0:T(8,128)(2,1)S(1)}, bf16[64,1536]{1,0:T(8,128)(2,1)}, u32[]{:S(2)}, u32[]{:S(2)}) collective-permute-start(bf16[64,1536]{1,0:T(8,128)(2,1)S(1)} %get-tuple-element.56), channel_id=1, source_target_pairs={{0,16},{8,24},{16,0},{24,8},{1,17},{9,25},{17,1},{25,9},{2,18},{10... | collective-permute-start | bytes 589832 | tf_op jit(solution)/shard_map/ppermute | solution.py:1009
  751.6 7.1 collective-permute-start.2
  783.4 10.2 %copy-start = (bf16[64,1,2816]{2,1,0:T(2,128)(2,1)S(1)}, bf16[64,1,2816]{2,1,0:T(2,128)(2,1)}, u32[]{:S(2)}) copy-start(bf16[64,1,2816]{2,1,0:T(2,128)(2,1)} %copy.45) | copy-start | bytes 1081348
  805.6 1.2 copy-start.5
  805.6 2.0 copy-start.2

commit v4 on v3

--- a/solution.py
+++ b/solution.py
@@ -174,6 +174,17 @@
         lax.fori_loop(0, whole, run, 0)
     if total % size:
         step(whole * size, total % size)
+
+
+def turn_block(block, left, source, nd, nc):
+    rows, width = block.shape
+    part = width // (nd * nc)
+    here = lanes(source * rows, rows)
+    for at in range(0, width, 128):
+        turned = block[:, at : at + 128].T
+        for i in range(0, 128, part):
+            d, c = (at + i) // (part * nc), (at + i) // part % nc
+            left[c, d * part : (d + 1) * part, here] = turned[i : i + part]
 
 
 def forward(nd, nc, tokens, cotangent, small, w_qkv, w_gate, w_up, w_out, w_down):
@@ -196,7 +207,7 @@
         tok_i, cot_i, small_i, wq_i, wg_i, wu_i, wo_i, wd_i, keep_i, sine_i,
         h1_o, dy_o, wq_o, seq_o, lse_o, mixed_o, r1_o, h2_o, m_o, dgu_o, pout_o, pdh2_o, small_o,
         tok, dy, sm, wq, h1, qkv, seq, lse, o, mixed, wo, part, ra, rb, r1, h2, wg, wu, wd, m, dgu,
-        turns, send, recv, local,
+        turns, left1, left2, m_t, mixed_t, send, recv, local,
     ):
         dp, ctx = lax.axis_index("dp"), lax.axis_index("ctx")
         odd = ctx % 2
@@ -279,7 +290,9 @@
         first_norm(across)
         forward_tok.wait_recv()
         first_norm(far)
-        put_h1 = links.here(h1, h1_o)
+        for b in range(nd):
+            turn_block(h1[b * rows : (b + 1) * rows, :], left1, b, nd, nc)
+        put_h1 = links.here(left1, h1_o)
         put_small = links.here(sm, small_o)
 
         wq_y = []
@@ -388,7 +401,6 @@
             copy.wait()
         for copy in back:
             copy.wait_recv()
-        put_mixed = links.here(mixed, mixed_o)
 
         def out_tile(at, n):
             acc = plain(mixed[0], wo[0:span, pl.ds(at, n)])
@@ -402,6 +414,9 @@
             links.to({"dp": near}, blocks(part, far), blocks(ra, 0)),
             links.to({"dp": near}, blocks(part, near), blocks(ra, 1)),
         ]
+        for i in range(groups):
+            mixed_t[i * span : (i + 1) * span, :] = mixed[i].T
+        put_mixed = links.here(mixed_t, mixed_o)
         to_near[0].wait_recv()
         across_at = halves(across * rows, rows)
         part[across_at, :] = (part[across_at, :].astype(F32) + ra[:rows, :].astype(F32)).astype(BF16)
@@ -417,18 +432,21 @@
         hat, _ = normalize_rows(r1[...])
         h2[own_at, :] = (hat * gain(2) + gain(3)).astype(BF16)
         send_h2 = [links.to({"dp": e}, blocks(h2, dp), blocks(h2, dp)) for e in (near, across)]
+        turn_block(h2[own_at, :], left2, dp, nd, nc)
+        send_h2[0].wait_recv()
+        turn_block(h2[halves(near * rows, rows), :], left2, near, nd, nc)
         send_h2[1].wait_recv()
         forward_h2 = links.to({"dp": near}, blocks(h2, across), blocks(h2, across))
+        turn_block(h2[halves(across * rows, rows), :], left2, across, nd, nc)
         get_wd.wait()
         get_dy.wait()
         for copy in get_wgu:
             copy.wait()
-        for copy in wgu_near + wgu_y + [send_dy[0], forward_dy, send_h2[0], forward_h2]:
+        for copy in wgu_near + wgu_y + [send_dy[0], forward_dy, forward_h2]:
             copy.wait_recv()
-        put_h2 = links.here(h2, h2_o)
+        turn_block(h2[halves(far * rows, rows), :], left2, far, nd, nc)
+        put_h2 = links.here(left2, h2_o)
         put_dy = links.here(dy, dy_o)
-        put_h1.wait()
-
         def hidden_tile(at, n):
             here = pl.ds(at, n)
             gate = plain(h2[...], wg[:, here])
@@ -440,7 +458,12 @@
             dgu[:, pl.ds(hidden + at, n)] = (dm * gate * sig).astype(BF16)
 
         over_tiles(hidden, 256, hidden_tile)
-        put_m = links.here(m, m_o)
+
+        def turn_tile(at, n):
+            m_t[pl.ds(at, n), :] = m[:, pl.ds(at, n)].T
+
+        over_tiles(hidden, 128, turn_tile)
+        put_m = links.here(m_t, m_o)
         put_dgu = links.here(dgu, dgu_o)
 
         def dh2_tile(at, n):
@@ -461,7 +484,7 @@
 
         links.gone(*links.left)
         for copy in (
-            put_small, put_wq, put_seq, put_lse, put_mixed, put_r1, put_h2, put_dy, put_m, put_dgu,
+            put_small, put_h1, put_wq, put_seq, put_lse, put_mixed, put_r1, put_h2, put_dy, put_m, put_dgu,
             put_pdh2, put_pout,
         ):
             copy.wait()
@@ -470,15 +493,15 @@
     shape = jax.ShapeDtypeStruct
     remotes = 2 + 3 + 6 + 3 + 1 + 2 + 4 + 2 + 2 * (nc - 1) * 2 + 2 + 4 + 1 + 3 + 2 + 1
     outs = dict(
-        h1=((many, width), BF16),
+        h1=((nc, width // nc, many), BF16),
         dy=((many, width), BF16),
         wq=((width, 3 * cols), BF16),
         seq=((length, 3 * span), BF16),
         lse=((heads, length), F32),
-        mixed=((groups, many, span), BF16),
+        mixed=((cols, many), BF16),
         r1=((rows, width), F32),
-        h2=((many, width), BF16),
-        m=((many, hidden), BF16),
+        h2=((nc, width // nc, many), BF16),
+        m=((hidden, many), BF16),
         dgu=((many, 2 * hidden), BF16),
         pout=((many, width), BF16),
         pdh2=((many, width), BF16),
@@ -507,6 +530,10 @@
         ((many, hidden), BF16),
         ((many, 2 * hidden), BF16),
         ((2, rows, 128), F32),
+        ((nc, width // nc, many), BF16),
+        ((nc, width // nc, many), BF16),
+        ((hidden, many), BF16),
+        ((cols, many), BF16),
     ]
     results = pl.pallas_call(
         body,
@@ -663,14 +690,6 @@
     def order(self):
         return sorted(range(self.nc // 2), key=lambda j: (j & -j) or self.nc)
 
-    def finish(self, after=1):
-        bit = after
-        while 1 << bit < self.nc:
-            step = 1 << bit
-            for j in sorted(range(0, self.nc // 2, step), key=lambda j: (j & -j) or self.nc):
-                self.add(bit, j)
-            bit += 1
-
 
 def backward(nd, nc, f, small, tokens, w_out, lefts):
     rows, width = tokens.shape
@@ -688,11 +707,13 @@
     right_cols = {"gu": f["dgu"].shape[1], "down": width, "out": width, "qkv": 3 * cols}
     left_rows = {k: lefts[k].shape[1] for k in names}
     slots = nc // 2
+    share = left_rows["gu"] // nd
+    hidden = right_cols["gu"] // 2
 
     def body(
         h2_l, m_l, mixed_l, h1_l, dy_i, dgu_i, wq_i, seq_i, lse_i, r1_i, pdh2_i, pout_i,
         small_i, tok_i, wo_i, keep_i, sine_i,
-        out_o, tg_o, gu_o, down_o, out_g_o, qkv_o, sums_o, land_gu, land_down, land_out, land_qkv,
+        out_o, tg_o, gate_o, up_o, qkv_o, down_o, out_g_o, sums_o, land_gu, land_down, land_out, land_qkv,
         l_gu, l_down, l_out, l_qkv, dgu, dy, da, dq, s_gu, s_down, s_out, s_qkv,
         stage,
         part, ra, rb, ra2, rb2, r1, dr1, x, sm, wq, wo, seq, lse,
@@ -860,8 +881,8 @@
         hat1, inverse1 = normalize_rows(x[...].astype(F32))
         sums[0:1, :] = jnp.sum(dh1 * hat1, axis=0, keepdims=True)
         sums[1:2, :] = jnp.sum(dh1, axis=0, keepdims=True)
-        partners = [("ctx", flip_bit(ctx, b)) for b in range(nc.bit_length() - 1)]
-        partners += [("dp", flip_bit(dp, b)) for b in range(nd.bit_length() - 1)]
+        partners = [("dp", flip_bit(dp, b)) for b in range(nd.bit_length() - 1)]
+        partners += [("ctx", flip_bit(ctx, b)) for b in range(nc.bit_length() - 1)]
 
         def exchange_sums(i):
             copy = links.to({partners[i][0]: partners[i][1]}, sums, sums_in.at[i])
@@ -877,30 +898,66 @@
         sum0 = GroupSum(links, dp, nd, rows, part, ra, rb)
         for j in turns[2]:
             gu.keep(j)
+        get_out.wait()
         for j in order:
             qkv.give(j)
-        get_out.wait()
         sum0.middle()
         for j in order:
             out.give(j)
+        exchange_sums(0)
+        exchange_sums(1)
         for j in turns[3]:
             gu.keep(j)
         x[...] = (r1[...] + sum0.total()).astype(BF16)
         put_out = links.here(x, out_o)
-        for i in range(len(partners)):
-            exchange_sums(i)
-        for piece, before in ((down, gu), (qkv, down), (out, qkv)):
+        arriving, put = [], []
+
+        def to_owner(slots, spans):
+            for e in (near, across, far, dp):
+                for dst, at, to, n in spans:
+                    src = slots.at[0, pl.ds(pl.multiple_of(e * share, 16), share), pl.ds(at, n)]
+                    place = dst.at[:, lanes(to + dp * n, n)]
+                    if e is dp:
+                        put.append(links.here(src, place))
+                    else:
+                        arriving.append(links.to({"dp": e}, src, place))
+
+        def first_steps(piece):
             for j in order:
-                piece.keep(j)
-            before.finish()
-        out.finish()
-        put = [
-            links.here(s_gu.at[0], gu_o),
-            links.here(s_down.at[0], down_o),
-            links.here(s_out.at[0], out_g_o),
-            links.here(s_qkv.at[0], qkv_o),
-        ]
+                yield lambda j=j: piece.keep(j)
+
+        def later_steps(piece, close):
+            bit = 1
+            while 1 << bit < nc:
+                for j in sorted(range(0, nc // 2, 1 << bit), key=lambda j: (j & -j) or nc):
+                    yield lambda bit=bit, j=j: piece.add(bit, j)
+                bit += 1
+            yield close
+
+        gu_spans = ((gate_o, 0, 0, hidden), (up_o, hidden, 0, hidden))
+        qkv_spans = tuple((qkv_o, j * cols, j * width, cols) for j in range(3))
+        closes = (
+            lambda: to_owner(s_gu, gu_spans),
+            lambda: put.append(links.here(s_down.at[0], down_o)),
+            lambda: to_owner(s_qkv, qkv_spans),
+            lambda: put.append(links.here(s_out.at[0], out_g_o)),
+        )
+        pieces = (gu, down, qkv, out)
+        for i in range(1, len(pieces) + 1):
+            later = list(later_steps(pieces[i - 1], closes[i - 1]))
+            first = list(first_steps(pieces[i])) if i < len(pieces) else []
+            if i == len(pieces):
+                exchange_sums(2)
+            while later or first:
+                if first:
+                    first.pop(0)()
+                if later and len(first) <= len(later):
+                    later.pop(0)()
+        for k in range(3, len(partners)):
+            exchange_sums(k)
         put_sums = [links.here(sums, sums_o), put_tg, put_out]
+        for copy in arriving:
+            copy.wait_recv()
         links.gone(*links.left)
         for copy in put + put_sums:
             copy.wait()
@@ -911,7 +968,11 @@
     outs = [
         ((rows, width), BF16),
         ((rows, width), F32),
-        *[((left_rows[k], right_cols[k]), BF16) for k in names],
+        ((share, nd * hidden), BF16),
+        ((share, nd * hidden), BF16),
+        ((share, 3 * width), BF16),
+        ((left_rows["down"], width), BF16),
+        ((left_rows["out"], width), BF16),
         ((4 + nd, width), F32),
         *[((landings, left_rows[k], right_cols[k]), BF16) for k in names],
     ]
@@ -942,7 +1003,7 @@
         ((4 + nd, width), F32),
         ((nc.bit_length() + nd.bit_length() - 2, 4 + nd, width), F32),
     ]
-    remotes = 9 + 3 + 4 * (nc - 1) + 4 * (nc - 1) + (nc - 1) + 3 + 8
+    remotes = 9 + 3 + 4 * (nc - 1) + 4 * (nc - 1) + nc.bit_length() + nd.bit_length() + 3 * 5 + 8
     return pl.pallas_call(
         body,
         out_shape=[shape(*o) for o in outs],
@@ -974,7 +1035,6 @@
     nd, nc = lax.axis_size("dp"), lax.axis_size("ctx")
     dp, ctx = lax.axis_index("dp"), lax.axis_index("ctx")
     many = nd * rows
-    hidden = w_gate.shape[1] // nd
     x = tokens.reshape(rows, width)
 
     small = jnp.concatenate([norms.reshape(-1), b_qkv]).astype(F32)
@@ -983,36 +1043,19 @@
         nd, nc, x, cotangent.reshape(rows, width), small, w_qkv, w_gate, w_up, w_out, w_down
     )
 
-    def by_owner(left, outer):
-        part = left.shape[1] // (outer * nc)
-        left = left.T.reshape(outer, nc, part, many).transpose(1, 0, 2, 3)
-        left = left.reshape(nc, outer * part, many)
+    def by_owner(left):
+        left = left.reshape(nc, -1, many)
         return jnp.pad(left, ((0, 0), (0, -left.shape[1] % 16), (0, 0)))
 
     lefts = {
-        "gu": by_owner(f["h2"], nd),
-        "down": by_owner(f["m"], 1),
-        "out": by_owner(f["mixed"].transpose(1, 0, 2).reshape(many, -1), 1),
-        "qkv": by_owner(f["h1"], nd),
+        "gu": f["h2"],
+        "down": by_owner(f["m"]),
+        "out": by_owner(f["mixed"]),
+        "qkv": f["h1"],
     }
-    result, tokens_grad, g_gu, g_down, g_out, g_qkv, sums = backward(
+    result, tokens_grad, g_gate, g_up, g_qkv, g_down, g_out, sums = backward(
         nd, nc, f, f["small"], x, w_out, lefts
-    )[:7]
-
-    def to_rows(total):
-        blocks = total.reshape(nd, -1, total.shape[1])
-        part, cols = blocks.shape[1:]
-        out = jnp.zeros((part, nd, cols), BF16)
-        for k in range(nd):
-            block = take(blocks, dp ^ k)
-            if k:
-                block = lax.ppermute(block, "dp", [(i, i ^ k) for i in range(nd)])
-            out = lax.dynamic_update_slice(out, block[:, None], (0, dp ^ k, 0))
-        return out.astype(F32)
-
-    grad_gu = to_rows(g_gu)
-    grad_qkv = to_rows(g_qkv)
-    grad_qkv = grad_qkv.reshape(-1, nd, 3, width // nd).transpose(0, 2, 1, 3).reshape(-1, 3 * width)
+    )[:8]
     part_down, part_out = w_down.shape[0] // nc, w_out.shape[0] // nc
 
     place = dp * nc + ctx
@@ -1022,11 +1065,11 @@
     return (
         result.reshape(tokens.shape),
         tokens_grad.reshape(tokens.shape),
-        grad_qkv,
+        g_qkv.astype(F32),
         take(bias.reshape(nd * nc, -1), place),
         g_out[:part_out].astype(F32),
-        grad_gu[:, :, :hidden].reshape(-1, nd * hidden),
-        grad_gu[:, :, hidden:].reshape(-1, nd * hidden),
+        g_gate.astype(F32),
+        g_up.astype(F32),
         g_down[:part_down].astype(F32),
         norms_grad,
     )

time: 814 us -> 589 us (0.72)
  Pallas kernels: 714 us -> 565 us
  local copies, waits for them, and re-layouts: 82.4 us -> 3.84 us
    pallas_call x1, Pallas kernels: 510 us -> 360 us  [backward(): pl.pallas_call(body, out_shape=[shape(*o) for o in outs], in_specs=[anywh...]
    dynamic_update_slice x8 -> x0, local copies, waits for them, and re-layouts: 45.3 us -> none  [to_rows(): out = lax.dynamic_update_slice(out, block[:, None], (0, dp ^ k, 0))]
    transpose x6 -> x0, local copies, waits for them, and re-layouts: 11.7 us -> none  [the longest x5 10.7 us: by_owner(): left = left.T.reshape(outer, nc, part, many).transpose(1, 0, 2, 3)]
    reshape x3 -> x0, local copies, waits for them, and re-layouts: 8.35 us -> none  [shards(): grad_qkv.reshape(-1, nd, 3, width // nd).transpose(0, 2, 1, 3)]
  transfers between devices with their start and end apart: 6 -> 0, of which waited for: 2 -> 0; matrix products, arithmetic and copies ran while one was open for 4% -> 0% of each run, Pallas kernels for 0% -> 0%
where the time goes in v4:
time: 589 us; the launch traced here: 579 us
  Pallas kernels  565 us (96%)
  other arithmetic  8.26 us (1%)
    pallas_call x1, Pallas kernels, backward(): pl.pallas_call(body, out_shape=[shape(*o) for o in outs], in_specs=[anywh...  360 us
    pallas_call x1, Pallas kernels, forward(): pl.pallas_call(body, out_shape=[shape(*o) for o in outs.values()], in_spe...  205 us

profile of v4, /device:TPU:0, one launch (start us, length us, event | category | flops | bytes accessed | tf_op | source)
XLA Modules:
  0.0 578.7 jit_solution(2099236368421402750)
XLA Ops:
  0.6 0.7 copy.22
  1.3 1.3 fusion.4.small_i
  2.6 205.3 %shard_map.196 = (bf16[8,256,512]{2,1,0:T(8,128)(2,1)}, bf16[512,2048]{1,0:T(8,128)(2,1)}, bf16[2048,1536]{1,0:T(8,128)(2,1)}, bf16[1024,768]{1,0:T(8,128)(2,1)}...) custom-call(bf16[128,2048]{1,0:T(8,128)(2,1)} %bitcast.18, ...), custom_call_target="tpu_custom_call" | custom-call | tf_op jit(solution)/shard_map/pallas_call | solution.py:538
  207.9 360.2 %shard_map.197 = (bf16[128,2048]{1,0:T(8,128)(2,1)}, f32[128,2048]{1,0:T(8,128)}, bf16[64,5632]{1,0:T(8,128)(2,1)}, bf16[64,5632]{1,0:T(8,128)(2,1)}, bf16[64,61...) custom-call(bf16[8,256,512]{2,1,0:T(8,128)(2,1)} %get-tuple-element., ...), custom_call_target="tpu_custom_call" | custom-call | tf_op jit(solution)/shard_map/pallas_call | solution.py:1007
  568.1 0.0 copy-start.3
  568.1 0.0 copy-start.2
  568.1 2.5 convert_element_type.18
  570.6 0.0 copy-done.3
  570.6 0.0 copy-start.1
  570.6 1.2 convert_element_type.20
  571.8 0.0 copy-done.2
  571.8 0.0 copy-start.5
  571.8 0.0 copy-start.6
  571.8 1.2 convert_element_type.21
  573.0 0.0 copy-start.4
  573.0 0.0 copy-done.1
  573.0 0.0 copy-start
  573.0 1.3 convert_element_type.22
  574.3 0.0 copy-done.5
  574.3 0.8 convert_element_type.19
  575.1 0.0 copy-done.6
  575.1 0.1 reshape.64
  575.2 0.6 constant_dynamic-slice_fusion
  575.8 0.1 reshape.63
  575.9 0.6 constant_dynamic-slice_fusion.1
  576.5 0.0 copy-done.4
  576.5 0.8 copy.25
  577.3 0.0 copy-done
  577.3 1.0 copy.26
  (2 shorter events, 0.0 us)
Async XLA Ops:
  568.1 2.5 copy-start.3
  568.1 3.7 copy-start.2
  570.6 2.4 copy-start.1
  571.8 2.5 copy-start.5
  571.8 3.3 copy-start.6
  573.0 3.5 copy-start.4
  573.0 4.3 copy-start

commit v5 on v4

--- a/solution.py
+++ b/solution.py
@@ -61,6 +61,10 @@
 
 def flip_one(i):
     return i + 1 - 2 * (i % 2)
+
+
+def flip_bit(i, bit):
+    return i + (1 << bit) - (2 << bit) * ((i // (1 << bit)) % 2)
 
 
 def halves(start, size):
@@ -193,7 +197,7 @@
     many = nd * rows
     length = 2 * nc * half
     depth = w_qkv.shape[0]
-    part_depth = depth // 2
+    quarter = depth // 4
     heads_here = HEADS // nd
     groups = nc // nd
     heads = heads_here // groups
@@ -206,13 +210,13 @@
     def body(
         tok_i, cot_i, small_i, wq_i, wg_i, wu_i, wo_i, wd_i, keep_i, sine_i,
         h1_o, dy_o, wq_o, seq_o, lse_o, mixed_o, r1_o, h2_o, m_o, dgu_o, pout_o, pdh2_o, small_o,
-        tok, dy, sm, wq, h1, qkv, seq, lse, o, mixed, wo, part, ra, rb, r1, h2, wg, wu, wd, m, dgu,
+        tok, dy, sm, wq, h1, qkv, seq, lse, o, mixed, wo, part, ra, rb, r1, h2, wgu, wd, m, dgu,
         turns, left1, left2, m_t, mixed_t, send, recv, local,
     ):
         dp, ctx = lax.axis_index("dp"), lax.axis_index("ctx")
-        odd = ctx % 2
         near, across, far = flip_one(dp), (dp + 2) % nd, nd - 1 - dp
-        beside = flip_one(ctx)
+        spot = ctx % 4
+        sides = [{"ctx": flip_bit(ctx, bit)} for bit in range(2)]
         links = Copies(send, recv, local)
         blocks = lambda ref, b: ref.at[halves(b * rows, rows)]
 
@@ -236,32 +240,50 @@
         send_small = [links.to({"dp": e}, small_i, sm.at[dp]) for e in (near, across, far)]
 
         def columns(w_i, w, e, at, n, to, full):
-            start = dp * depth + (0 if full else odd * part_depth)
-            size = depth if full else part_depth
-            first = 0 if full else odd * part_depth
+            first, size = (0, depth) if full else (spot * quarter, quarter)
             return links.to(
                 {"dp": e},
                 w_i.at[halves(first, size), lanes(at, n)],
-                w.at[halves(start, size), pl.ds(to, n)],
+                w.at[halves(dp * depth + first, size), pl.ds(to, n)],
             )
 
-        def relay(w, source):
-            block = w.at[halves(source * depth + odd * part_depth, part_depth)]
-            return links.to({"ctx": beside}, block, block)
-
-        wq_x = [
-            [columns(wq_i, wq, e, j * width + e * cols, cols, j * cols, False) for j in range(3)]
-            for e in (across, far)
-        ]
-        wq_near = [
-            columns(wq_i, wq, near, j * width + near * cols, cols, j * cols, True) for j in range(3)
-        ]
+        def share(w, copies, source):
+            for copy in copies:
+                copy.wait_recv()
+            block = w.at[halves(source * depth + spot * quarter, quarter)]
+            return [links.to(side, block, block) for side in sides]
+
+        def cross(w, shared, source):
+            passed = []
+            for bit in range(2):
+                shared[bit].wait_recv()
+                start = source * depth + flip_bit(spot, bit) * quarter + bit * (quarter // 2)
+                block = w.at[halves(start, quarter // 2)]
+                passed.append(links.to(sides[1 - bit], block, block))
+            return passed
+
+        def qkv_columns(e, full):
+            return [
+                columns(wq_i, wq, e, j * width + e * cols, cols, j * cols, full) for j in range(3)
+            ]
+
+        def hidden_columns(e, full):
+            return [
+                columns(w_i, wgu, e, e * hidden, hidden, i * hidden, full)
+                for i, w_i in enumerate((wg_i, wu_i))
+            ]
+
+        wq_x = [qkv_columns(e, False) for e in (across, far)]
+        wq_near = qkv_columns(near, True)
         get_wo = links.here(wo_i, wo)
         get_wd = links.here(wd_i, wd)
         get_dy = links.here(cot_i, blocks(dy, dp))
         get_wgu = [
-            links.here(w_i.at[:, lanes(dp * hidden, hidden)], w.at[halves(dp * depth, depth)])
-            for w_i, w in ((wg_i, wg), (wu_i, wu))
+            links.here(
+                w_i.at[:, lanes(dp * hidden, hidden)],
+                wgu.at[halves(dp * depth, depth), pl.ds(i * hidden, hidden)],
+            )
+            for i, w_i in enumerate((wg_i, wu_i))
         ]
 
         send_tok[1].wait_recv()
@@ -295,22 +317,14 @@
         put_h1 = links.here(left1, h1_o)
         put_small = links.here(sm, small_o)
 
-        wq_y = []
-        for source, copies in ((across, wq_x[0]), (far, wq_x[1])):
-            for copy in copies:
-                copy.wait_recv()
-            wq_y.append(relay(wq, source))
-        wgu_x = [
-            [columns(w_i, w, e, e * hidden, hidden, 0, False) for e in (across, far)]
-            for w_i, w in ((wg_i, wg), (wu_i, wu))
-        ]
-        wgu_near = [
-            columns(w_i, w, near, near * hidden, hidden, 0, True)
-            for w_i, w in ((wg_i, wg), (wu_i, wu))
-        ]
+        wq_s = [share(wq, copies, e) for copies, e in zip(wq_x, (across, far))]
+        wgu_x = [hidden_columns(e, False) for e in (across, far)]
+        wgu_near = hidden_columns(near, True)
+        send_dy = [links.to({"dp": e}, cot_i, blocks(dy, dp)) for e in (near, across)]
+        wq_c = [c for shared, e in zip(wq_s, (across, far)) for c in cross(wq, shared, e)]
         for copy in get_wq + get_turns:
             copy.wait()
-        for copy in wq_near + wq_y:
+        for copy in wq_near + wq_c:
             copy.wait_recv()
         put_wq = links.here(wq, wq_o)
 
@@ -356,46 +370,30 @@
             )
             for i, block in enumerate((ctx, mirror))
         ]
-        send_dy = [links.to({"dp": e}, cot_i, blocks(dy, dp)) for e in (near, across)]
-        wgu_y = []
-
-        def pass_on(w, source, copy):
-            copy.wait_recv()
-            wgu_y.append(relay(w, source))
-
-        pass_on(wg, across, wgu_x[0][0])
-        pass_on(wg, far, wgu_x[0][1])
         for copy in stay:
             copy.wait()
         for copy in go:
             copy.wait_recv()
         put_seq = links.here(seq, seq_o)
-        pass_on(wu, across, wgu_x[1][0])
-
+        wgu_s = [share(wgu, copies, e) for copies, e in zip(wgu_x, (across, far))]
+
+        back, stay = [], []
+        step = min(heads, 2)
         for head in range(heads):
             attend(seq, o, lse, heads, head)
-
-        back = []
-        for k in range(1, nc):
-            peer = lax.rem(ctx + k, nc)
-            for i, block in enumerate((peer, 2 * nc - 1 - peer)):
-                back.append(
-                    links.to(
-                        {"ctx": peer},
-                        o.at[halves(block * half, half)],
-                        mixed.at[g, halves(s * rows + i * half, half)],
-                    )
-                )
-        stay = [
-            links.here(
-                o.at[halves(block * half, half)], mixed.at[g, halves(s * rows + i * half, half)]
-            )
-            for i, block in enumerate((ctx, mirror))
-        ]
+            if (head + 1) % step:
+                continue
+            here = pl.ds((head + 1 - step) * HDIM, step * HDIM)
+            for k in range(nc):
+                peer = lax.rem(ctx + k, nc)
+                for i, block in enumerate((peer, 2 * nc - 1 - peer)):
+                    src = o.at[halves(block * half, half), here]
+                    dst = mixed.at[g, halves(s * rows + i * half, half), here]
+                    if k:
+                        back.append(links.to({"ctx": peer}, src, dst))
+                    else:
+                        stay.append(links.here(src, dst))
         put_lse = links.here(lse, lse_o)
-        pass_on(wu, far, wgu_x[1][1])
-        send_dy[1].wait_recv()
-        forward_dy = links.to({"dp": near}, blocks(dy, across), blocks(dy, across))
         get_wo.wait()
         for copy in stay:
             copy.wait()
@@ -421,6 +419,9 @@
         across_at = halves(across * rows, rows)
         part[across_at, :] = (part[across_at, :].astype(F32) + ra[:rows, :].astype(F32)).astype(BF16)
         to_across = links.to({"dp": across}, blocks(part, across), rb)
+        wgu_c = [c for shared, e in zip(wgu_s, (across, far)) for c in cross(wgu, shared, e)]
+        send_dy[1].wait_recv()
+        forward_dy = links.to({"dp": near}, blocks(dy, across), blocks(dy, across))
         to_near[1].wait_recv()
         own_at = halves(dp * rows, rows)
         r1[...] = tok[own_at, :].astype(F32) + (
@@ -442,15 +443,15 @@
         get_dy.wait()
         for copy in get_wgu:
             copy.wait()
-        for copy in wgu_near + wgu_y + [send_dy[0], forward_dy, forward_h2]:
+        for copy in wgu_near + wgu_c + [send_dy[0], forward_dy, forward_h2]:
             copy.wait_recv()
         turn_block(h2[halves(far * rows, rows), :], left2, far, nd, nc)
         put_h2 = links.here(left2, h2_o)
         put_dy = links.here(dy, dy_o)
         def hidden_tile(at, n):
             here = pl.ds(at, n)
-            gate = plain(h2[...], wg[:, here])
-            up = plain(h2[...], wu[:, here])
+            gate = plain(h2[...], wgu[:, here])
+            up = plain(h2[...], wgu[:, pl.ds(hidden + at, n)])
             dm = last_dims(dy[...], wd[here, :])
             sig = jax.nn.sigmoid(gate)
             m[:, here] = (gate * sig * up).astype(BF16)
@@ -468,8 +469,7 @@
 
         def dh2_tile(at, n):
             here = pl.ds(at, n)
-            acc = last_dims(dgu[:, :hidden], wg[here, :]) + last_dims(dgu[:, hidden:], wu[here, :])
-            h1[:, here] = acc.astype(BF16)
+            h1[:, here] = last_dims(dgu[...], wgu[here, :]).astype(BF16)
 
         over_tiles(width, 256, dh2_tile)
         put_pdh2 = links.here(h1, pdh2_o)
@@ -491,7 +491,7 @@
 
     anywhere = pl.BlockSpec(memory_space=pl.ANY)
     shape = jax.ShapeDtypeStruct
-    remotes = 2 + 3 + 6 + 3 + 1 + 2 + 4 + 2 + 2 * (nc - 1) * 2 + 2 + 4 + 1 + 3 + 2 + 1
+    remotes = 48 + 6 * (nc - 1)
     outs = dict(
         h1=((nc, width // nc, many), BF16),
         dy=((many, width), BF16),
@@ -524,8 +524,7 @@
         ((rows, width), BF16),
         ((rows, width), F32),
         ((many, width), BF16),
-        ((width, hidden), BF16),
-        ((width, hidden), BF16),
+        ((width, 2 * hidden), BF16),
         ((down, width), BF16),
         ((many, hidden), BF16),
         ((many, 2 * hidden), BF16),
@@ -551,10 +550,6 @@
         ),
     )(tokens, cotangent, small, w_qkv, w_gate, w_up, w_out, w_down, keep, sine)
     return dict(zip(outs, results))
-
-
-def flip_bit(i, bit):
-    return i + (1 << bit) - (2 << bit) * ((i // (1 << bit)) % 2)
 
 
 def attend_back(x_ref, lse_ref, do_ref, d_ref, heads, head):
@@ -883,13 +878,21 @@
         sums[1:2, :] = jnp.sum(dh1, axis=0, keepdims=True)
         partners = [("dp", flip_bit(dp, b)) for b in range(nd.bit_length() - 1)]
         partners += [("ctx", flip_bit(ctx, b)) for b in range(nc.bit_length() - 1)]
-
-        def exchange_sums(i):
-            copy = links.to({partners[i][0]: partners[i][1]}, sums, sums_in.at[i])
-            copy.wait_recv()
-            links.gone(copy)
+        sums_out = []
+
+        def start_sums():
+            i = len(sums_out)
+            if i < len(partners):
+                axis, device = partners[i]
+                sums_out.append(links.to({axis: device}, sums, sums_in.at[i]))
+
+        def end_sums():
+            i = len(sums_out) - 1
+            sums_out[i].wait_recv()
+            links.gone(sums_out[i])
             sums[...] += sums_in[i]
 
+        start_sums()
         dr1[...] += norm_reverse(dh1, gain(0), hat1, inverse1)
         put_tg = links.here(dr1, tg_o)
         links.gone(*sum1.a, sum1.b)
@@ -899,13 +902,15 @@
         for j in turns[2]:
             gu.keep(j)
         get_out.wait()
+        end_sums()
+        start_sums()
         for j in order:
             qkv.give(j)
         sum0.middle()
+        end_sums()
+        start_sums()
         for j in order:
             out.give(j)
-        exchange_sums(0)
-        exchange_sums(1)
         for j in turns[3]:
             gu.keep(j)
         x[...] = (r1[...] + sum0.total()).astype(BF16)
@@ -922,17 +927,13 @@
                     else:
                         arriving.append(links.to({"dp": e}, src, place))
 
-        def first_steps(piece):
+        def keep_all(piece):
             for j in order:
-                yield lambda j=j: piece.keep(j)
-
-        def later_steps(piece, close):
-            bit = 1
-            while 1 << bit < nc:
-                for j in sorted(range(0, nc // 2, 1 << bit), key=lambda j: (j & -j) or nc):
-                    yield lambda bit=bit, j=j: piece.add(bit, j)
-                bit += 1
-            yield close
+                piece.keep(j)
+
+        def add_all(piece, bit):
+            for j in sorted(range(0, nc // 2, 1 << bit), key=lambda j: (j & -j) or nc):
+                piece.add(bit, j)
 
         gu_spans = ((gate_o, 0, 0, hidden), (up_o, hidden, 0, hidden))
         qkv_spans = tuple((qkv_o, j * cols, j * width, cols) for j in range(3))
@@ -943,18 +944,22 @@
             lambda: put.append(links.here(s_out.at[0], out_g_o)),
         )
         pieces = (gu, down, qkv, out)
-        for i in range(1, len(pieces) + 1):
-            later = list(later_steps(pieces[i - 1], closes[i - 1]))
-            first = list(first_steps(pieces[i])) if i < len(pieces) else []
-            if i == len(pieces):
-                exchange_sums(2)
-            while later or first:
-                if first:
-                    first.pop(0)()
-                if later and len(first) <= len(later):
-                    later.pop(0)()
-        for k in range(3, len(partners)):
-            exchange_sums(k)
+        bits = nc.bit_length() - 1
+        for i in range(len(pieces) + bits - 1):
+            if 0 < i < len(pieces):
+                keep_all(pieces[i])
+            if i == len(pieces) - 1:
+                end_sums()
+                start_sums()
+            for bit in range(1, bits):
+                if 0 <= i - (bit - 1) < len(pieces):
+                    add_all(pieces[i - (bit - 1)], bit)
+                    if bit == bits - 1:
+                        closes[i - (bit - 1)]()
+        while len(sums_out) < len(partners):
+            end_sums()
+            start_sums()
+        end_sums()
         put_sums = [links.here(sums, sums_o), put_tg, put_out]
         for copy in arriving:
             copy.wait_recv()

time: 589 us -> 575 us (0.976)
  the two profiles are of different devices: /device:TPU:0 before, /device:TPU:20 now
where the time goes in v5:
time: 575 us; the launch traced here: 564 us
  Pallas kernels  551 us (96%)
  other arithmetic  8.26 us (1%)
    pallas_call x1, Pallas kernels, backward(): pl.pallas_call(body, out_shape=[shape(*o) for o in outs], in_specs=[anywh...  358 us
    pallas_call x1, Pallas kernels, forward(): pl.pallas_call(body, out_shape=[shape(*o) for o in outs.values()], in_spe...  193 us

profile of v5, /device:TPU:20, one launch (start us, length us, event | category | flops | bytes accessed | tf_op | source)
XLA Modules:
  0.0 564.3 jit_solution(6703540033276347287)
XLA Ops:
  0.6 0.7 copy.22
  1.3 1.3 fusion.4.small_i
  2.6 192.7 %shard_map.196 = (bf16[8,256,512]{2,1,0:T(8,128)(2,1)}, bf16[512,2048]{1,0:T(8,128)(2,1)}, bf16[2048,1536]{1,0:T(8,128)(2,1)}, bf16[1024,768]{1,0:T(8,128)(2,1)}...) custom-call(bf16[128,2048]{1,0:T(8,128)(2,1)} %bitcast.18, ...), custom_call_target="tpu_custom_call" | custom-call | tf_op jit(solution)/shard_map/pallas_call | solution.py:537
  195.4 358.3 %shard_map.197 = (bf16[128,2048]{1,0:T(8,128)(2,1)}, f32[128,2048]{1,0:T(8,128)}, bf16[64,5632]{1,0:T(8,128)(2,1)}, bf16[64,5632]{1,0:T(8,128)(2,1)}, bf16[64,61...) custom-call(bf16[8,256,512]{2,1,0:T(8,128)(2,1)} %get-tuple-element., ...), custom_call_target="tpu_custom_call" | custom-call | tf_op jit(solution)/shard_map/pallas_call | solution.py:1012
  553.7 0.0 copy-start.3
  553.7 0.0 copy-start.2
  553.7 2.5 convert_element_type.18
  556.2 0.0 copy-done.3
  556.2 0.0 copy-start.1
  556.2 1.2 convert_element_type.20
  557.4 0.0 copy-done.2
  557.4 0.0 copy-start.5
  557.4 0.0 copy-start.6
  557.4 1.2 convert_element_type.21
  558.6 0.0 copy-start.4
  558.6 0.0 copy-done.1
  558.6 0.0 copy-start
  558.6 1.3 convert_element_type.22
  559.9 0.0 copy-done.5
  559.9 0.8 convert_element_type.19
  560.7 0.0 copy-done.6
  560.7 0.1 reshape.64
  560.8 0.6 constant_dynamic-slice_fusion
  561.4 0.1 reshape.63
  561.5 0.6 constant_dynamic-slice_fusion.1
  562.1 0.0 copy-done.4
  562.1 0.8 copy.25
  562.9 0.0 copy-done
  562.9 1.0 copy.26
  (2 shorter events, 0.0 us)
Async XLA Ops:
  553.7 2.5 copy-start.3
  553.7 3.7 copy-start.2
  556.2 2.4 copy-start.1
  557.4 2.5 copy-start.5
  557.4 3.3 copy-start.6
  558.6 3.5 copy-start.4
  558.6 4.3 copy-start

commit v6 on v5

--- a/solution.py
+++ b/solution.py
@@ -65,6 +65,13 @@
 
 def flip_bit(i, bit):
     return i + (1 << bit) - (2 << bit) * ((i // (1 << bit)) % 2)
+
+
+def flip_bits(i, mask):
+    for bit in range(mask.bit_length()):
+        if mask >> bit & 1:
+            i = flip_bit(i, bit)
+    return i
 
 
 def halves(start, size):
@@ -205,11 +212,14 @@
     cols = heads_here * HDIM
     hidden = w_gate.shape[1] // nd
     down = w_down.shape[0]
+    share_down = down // nc
+    padded = share_down + -share_down % 16
     keep, sine = rotary_pair_tables(length)
 
     def body(
         tok_i, cot_i, small_i, wq_i, wg_i, wu_i, wo_i, wd_i, keep_i, sine_i,
         h1_o, dy_o, wq_o, seq_o, lse_o, mixed_o, r1_o, h2_o, m_o, dgu_o, pout_o, pdh2_o, small_o,
+        dyp_o, mp_o,
         tok, dy, sm, wq, h1, qkv, seq, lse, o, mixed, wo, part, ra, rb, r1, h2, wgu, wd, m, dgu,
         turns, left1, left2, m_t, mixed_t, send, recv, local,
     ):
@@ -236,11 +246,8 @@
         ]
         meet((("dp", nd), ("ctx", nc)))
 
-        send_tok = [links.to({"dp": e}, tok_i, blocks(tok, dp)) for e in (near, across)]
-        send_small = [links.to({"dp": e}, small_i, sm.at[dp]) for e in (near, across, far)]
-
-        def columns(w_i, w, e, at, n, to, full):
-            first, size = (0, depth) if full else (spot * quarter, quarter)
+        def columns(w_i, w, e, at, n, to, which):
+            first, size = (0, depth) if which is None else (which * quarter, quarter)
             return links.to(
                 {"dp": e},
                 w_i.at[halves(first, size), lanes(at, n)],
@@ -262,19 +269,23 @@
                 passed.append(links.to(sides[1 - bit], block, block))
             return passed
 
-        def qkv_columns(e, full):
+        def qkv_columns(e, which):
             return [
-                columns(wq_i, wq, e, j * width + e * cols, cols, j * cols, full) for j in range(3)
+                columns(wq_i, wq, e, j * width + e * cols, cols, j * cols, which) for j in range(3)
             ]
 
-        def hidden_columns(e, full):
+        def hidden_columns(e, which):
             return [
-                columns(w_i, wgu, e, e * hidden, hidden, i * hidden, full)
+                columns(w_i, wgu, e, e * hidden, hidden, i * hidden, which)
                 for i, w_i in enumerate((wg_i, wu_i))
             ]
 
-        wq_x = [qkv_columns(e, False) for e in (across, far)]
-        wq_near = qkv_columns(near, True)
+        send_small = [links.to({"dp": e}, small_i, sm.at[dp]) for e in (near, across, far)]
+        wq_x = [qkv_columns(e, spot) for e in (across, far)]
+        send_tok = [links.to({"dp": e}, tok_i, blocks(tok, dp)) for e in (near, across)]
+        wq_near = qkv_columns(near, None)
+        wgu_x = [hidden_columns(e, spot) for e in (across, far)]
+        send_dyp = [links.to(sides[0], cot_i, blocks(dyp_o, dp))]
         get_wo = links.here(wo_i, wo)
         get_wd = links.here(wd_i, wd)
         get_dy = links.here(cot_i, blocks(dy, dp))
@@ -286,8 +297,6 @@
             for i, w_i in enumerate((wg_i, wu_i))
         ]
 
-        send_tok[1].wait_recv()
-        forward_tok = links.to({"dp": near}, blocks(tok, across), blocks(tok, across))
         get_small.wait()
         for copy in send_small:
             copy.wait_recv()
@@ -305,23 +314,25 @@
             hat, _ = normalize_rows(tok[at, :].astype(F32))
             h1[at, :] = (hat * gain(0) + gain(1)).astype(BF16)
 
+        def turn_first(b):
+            turn_block(h1[halves(b * rows, rows), :], left1, b, nd, nc)
+
         get_tok.wait()
+        wq_s = [share(wq, copies, e) for copies, e in zip(wq_x, (across, far))]
         first_norm(dp)
         send_tok[0].wait_recv()
         first_norm(near)
+        wq_c = cross(wq, wq_s[0], across)
+        send_tok[1].wait_recv()
+        forward_tok = links.to({"dp": near}, blocks(tok, across), blocks(tok, across))
+        wq_c += cross(wq, wq_s[1], far)
         first_norm(across)
         forward_tok.wait_recv()
         first_norm(far)
-        for b in range(nd):
-            turn_block(h1[b * rows : (b + 1) * rows, :], left1, b, nd, nc)
-        put_h1 = links.here(left1, h1_o)
+        wgu_d = [hidden_columns(e, 3 - spot) for e in (across, far)]
+        wgu_near = hidden_columns(near, None)
+        send_dy = [links.to({"dp": e}, cot_i, blocks(dy, dp)) for e in (near, across)]
         put_small = links.here(sm, small_o)
-
-        wq_s = [share(wq, copies, e) for copies, e in zip(wq_x, (across, far))]
-        wgu_x = [hidden_columns(e, False) for e in (across, far)]
-        wgu_near = hidden_columns(near, True)
-        send_dy = [links.to({"dp": e}, cot_i, blocks(dy, dp)) for e in (near, across)]
-        wq_c = [c for shared, e in zip(wq_s, (across, far)) for c in cross(wq, shared, e)]
         for copy in get_wq + get_turns:
             copy.wait()
         for copy in wq_near + wq_c:
@@ -375,7 +386,9 @@
         for copy in go:
             copy.wait_recv()
         put_seq = links.here(seq, seq_o)
-        wgu_s = [share(wgu, copies, e) for copies, e in zip(wgu_x, (across, far))]
+        for b in range(nd):
+            turn_first(b)
+        put_h1 = links.here(left1, h1_o)
 
         back, stay = [], []
         step = min(heads, 2)
@@ -393,6 +406,7 @@
                         back.append(links.to({"ctx": peer}, src, dst))
                     else:
                         stay.append(links.here(src, dst))
+        wgu_s = [c for copies, e in zip(wgu_x, (across, far)) for c in share(wgu, copies, e)]
         put_lse = links.here(lse, lse_o)
         get_wo.wait()
         for copy in stay:
@@ -419,9 +433,9 @@
         across_at = halves(across * rows, rows)
         part[across_at, :] = (part[across_at, :].astype(F32) + ra[:rows, :].astype(F32)).astype(BF16)
         to_across = links.to({"dp": across}, blocks(part, across), rb)
-        wgu_c = [c for shared, e in zip(wgu_s, (across, far)) for c in cross(wgu, shared, e)]
         send_dy[1].wait_recv()
         forward_dy = links.to({"dp": near}, blocks(dy, across), blocks(dy, across))
+        send_dyp.append(links.to(sides[0], blocks(dy, across), blocks(dyp_o, across)))
         to_near[1].wait_recv()
         own_at = halves(dp * rows, rows)
         r1[...] = tok[own_at, :].astype(F32) + (
@@ -443,7 +457,7 @@
         get_dy.wait()
         for copy in get_wgu:
             copy.wait()
-        for copy in wgu_near + wgu_c + [send_dy[0], forward_dy, forward_h2]:
+        for copy in wgu_near + wgu_s + wgu_d[0] + wgu_d[1] + [send_dy[0], forward_dy, forward_h2]:
             copy.wait_recv()
         turn_block(h2[halves(far * rows, rows), :], left2, far, nd, nc)
         put_h2 = links.here(left2, h2_o)
@@ -458,13 +472,20 @@
             dgu[:, here] = (dm * up * sig * (1.0 + gate * (1.0 - sig))).astype(BF16)
             dgu[:, pl.ds(hidden + at, n)] = (dm * gate * sig).astype(BF16)
 
+        if padded != share_down:
+            m[:, hidden:] = jnp.zeros((many, padded - share_down), BF16)
         over_tiles(hidden, 256, hidden_tile)
-
-        def turn_tile(at, n):
-            m_t[pl.ds(at, n), :] = m[:, pl.ds(at, n)].T
-
-        over_tiles(hidden, 128, turn_tile)
+        for c in range(nc):
+            m_t[c] = m[:, c * share_down : c * share_down + padded].T
         put_m = links.here(m_t, m_o)
+
+        send_m, forward_dyp = [], []
+        for j in range(nc // 2):
+            owner = flip_bits(flip_bit(ctx, 0), 2 * j)
+            send_m.append(links.to(sides[0], m_t.at[owner], mp_o.at[j]))
+        for copy, b in zip(send_dyp, (dp, across)):
+            copy.wait_recv()
+            forward_dyp.append(links.to({"dp": near}, blocks(dyp_o, b), blocks(dyp_o, b)))
         put_dgu = links.here(dgu, dgu_o)
 
         def dh2_tile(at, n):
@@ -477,10 +498,12 @@
 
         def result_tile(at, n):
             here = pl.ds(at, n)
-            tok[:, here] = plain(m[...], wd[:, here]).astype(BF16)
+            tok[:, here] = plain(m[:, :hidden], wd[:, here]).astype(BF16)
 
         over_tiles(width, 256, result_tile)
         put_pout = links.here(tok, pout_o)
+        for copy in send_m + forward_dyp:
+            copy.wait_recv()
 
         links.gone(*links.left)
         for copy in (
@@ -491,7 +514,7 @@
 
     anywhere = pl.BlockSpec(memory_space=pl.ANY)
     shape = jax.ShapeDtypeStruct
-    remotes = 48 + 6 * (nc - 1)
+    remotes = 64 + 7 * nc
     outs = dict(
         h1=((nc, width // nc, many), BF16),
         dy=((many, width), BF16),
@@ -501,11 +524,13 @@
         mixed=((cols, many), BF16),
         r1=((rows, width), F32),
         h2=((nc, width // nc, many), BF16),
-        m=((hidden, many), BF16),
+        m=((nc, padded, many), BF16),
         dgu=((many, 2 * hidden), BF16),
         pout=((many, width), BF16),
         pdh2=((many, width), BF16),
         small=((nd,) + small.shape, F32),
+        dyp=((many, width), BF16),
+        mp=((nc // 2, padded, many), BF16),
     )
     scratch = [
         ((many, width), BF16),
@@ -526,12 +551,12 @@
         ((many, width), BF16),
         ((width, 2 * hidden), BF16),
         ((down, width), BF16),
-        ((many, hidden), BF16),
+        ((many, hidden + padded - share_down), BF16),
         ((many, 2 * hidden), BF16),
         ((2, rows, 128), F32),
         ((nc, width // nc, many), BF16),
         ((nc, width // nc, many), BF16),
-        ((hidden, many), BF16),
+        ((nc, padded, many), BF16),
         ((cols, many), BF16),
     ]
     results = pl.pallas_call(
@@ -620,48 +645,25 @@
         self.landing = landing
         self.stage = stage.at[pl.ds(0, slots.shape[1]), pl.ds(0, slots.shape[2])]
         self.sent = {}
+        self.order = sorted(range(nc // 2), key=lambda j: (j & -j) or nc)
 
     def _landing(self, bit, j):
-        base = sum(self.nc >> (b + 1) for b in range(bit))
+        base = sum(self.nc >> (b + 1) for b in range(1, bit))
         return self.landing.at[base + (j >> bit)]
 
-    def _owner(self, e):
-        owner = self.ctx
-        bit = 0
-        while e >> bit:
-            if (e >> bit) & 1:
-                owner = flip_bit(owner, bit)
-            bit += 1
-        return owner
-
-    def give(self, j):
-        left = self.left[self._owner(2 * j + 1)]
+    def compute(self):
+        for j in self.order:
+            self.slot(j)
+
+    def slot(self, j):
+        mine, other = self.left[0][j], self.left[1][j]
 
         def step(at, n):
             here = pl.ds(at, n)
-            self.slots[j, :, here] = plain(left, self.right[:, here]).astype(BF16)
-
-        over_tiles(self.right.shape[1], 512, step)
-        self.sent[0, j] = self.links.to(
-            {"ctx": flip_bit(self.ctx, 0)}, self.slots.at[j], self._landing(0, j)
-        )
-
-    def _load(self, bit, j):
-        self.sent[bit, j if bit == 0 else j + (1 << (bit - 1))].wait_recv()
-        copy = self.links.here(self._landing(bit, j), self.stage)
-        copy.wait()
-
-    def keep(self, j):
-        left = self.left[self._owner(2 * j)]
-        self._load(0, j)
-        self.links.gone(self.sent[0, j])
-
-        def step(at, n):
-            here = pl.ds(at, n)
-            acc = plain(left, self.right[:, here]) + self.stage[:, here].astype(F32)
+            acc = plain(mine, self.right[0][:, here]) + plain(other, self.right[1][:, here])
             self.slots[j, :, here] = acc.astype(BF16)
 
-        over_tiles(self.right.shape[1], 512, step)
+        over_tiles(self.slots.shape[2], 512, step)
         self._pass(1, j)
 
     def _pass(self, bit, j):
@@ -671,22 +673,25 @@
                 {"ctx": flip_bit(self.ctx, bit)}, self.slots.at[j], self._landing(bit, j - low)
             )
 
-    def add(self, bit, j):
-        self._load(bit, j)
+    def add(self, bit):
+        for j in self.order:
+            if j % (1 << bit) == 0:
+                self.add_slot(bit, j)
+
+    def add_slot(self, bit, j):
+        self.sent[bit, j + (1 << (bit - 1))].wait_recv()
+        self.links.here(self._landing(bit, j), self.stage).wait()
 
         def step(at, n):
             here = pl.ds(at, n)
             acc = self.slots[j, :, here].astype(F32) + self.stage[:, here].astype(F32)
             self.slots[j, :, here] = acc.astype(BF16)
 
-        over_tiles(self.right.shape[1], 512, step)
+        over_tiles(self.slots.shape[2], 512, step)
         self._pass(bit + 1, j)
 
-    def order(self):
-        return sorted(range(self.nc // 2), key=lambda j: (j & -j) or self.nc)
-
-
-def backward(nd, nc, f, small, tokens, w_out, lefts):
+
+def backward(nd, nc, f, tokens, w_out):
     rows, width = tokens.shape
     half = rows // 2
     many = nd * rows
@@ -695,57 +700,62 @@
     span = heads * HDIM
     groups = nc // nd
     cols = groups * span
-    cot_rows = f["dy"]
+    hidden = f["dgu"].shape[1] // 2
+    slots = nc // 2
+    share = width // (nd * nc)
+    tall = {"gate": nd * share, "down": f["m"].shape[1], "out": cols // nc, "qkv": nd * share}
+    tall["up"] = tall["gate"]
+    flat = {"gate": hidden, "up": hidden, "down": width, "out": width, "qkv": 3 * cols}
+    names = ("down", "gate", "up", "qkv", "out")
+    bits = nc.bit_length() - 1
     keep_t, sine_t = rotary_pair_tables(length)
-    chunk = min(length, 1024)
-    names = ("gu", "down", "out", "qkv")
-    right_cols = {"gu": f["dgu"].shape[1], "down": width, "out": width, "qkv": 3 * cols}
-    left_rows = {k: lefts[k].shape[1] for k in names}
-    slots = nc // 2
-    share = left_rows["gu"] // nd
-    hidden = right_cols["gu"] // 2
+    chunk = length if length <= 1024 else 256
+    strip = 256 if length <= 1024 else 128
+    mixed_left = f["mixed"].reshape(nc, cols // nc, many)
 
     def body(
-        h2_l, m_l, mixed_l, h1_l, dy_i, dgu_i, wq_i, seq_i, lse_i, r1_i, pdh2_i, pout_i,
+        h2_l, m_l, mp_l, mixed_l, h1_l, dy_i, dyp_i, dgu_i, wq_i, seq_i, lse_i, r1_i, pdh2_i, pout_i,
         small_i, tok_i, wo_i, keep_i, sine_i,
-        out_o, tg_o, gate_o, up_o, qkv_o, down_o, out_g_o, sums_o, land_gu, land_down, land_out, land_qkv,
-        l_gu, l_down, l_out, l_qkv, dgu, dy, da, dq, s_gu, s_down, s_out, s_qkv,
-        stage,
-        part, ra, rb, ra2, rb2, r1, dr1, x, sm, wq, wo, seq, lse,
+        out_o, tg_o, gate_o, up_o, qkv_o, down_o, out_g_o, sums_o,
+        land_down, land_gate, land_up, land_qkv, land_out,
+        l_gu, l_down, l_out, l_qkv, dgu, dgup, dy, dyp, da, dq, dqp,
+        s_down, s_gate, s_up, s_qkv, s_out, stage,
+        part, ra, rb, r1, dr1, x, sm, wq, wo, seq, lse,
         dmix, dseq, dx, keep, sine, dback, sums, sums_in,
         send, recv, local,
     ):
         dp, ctx = lax.axis_index("dp"), lax.axis_index("ctx")
         near, across, far = flip_one(dp), (dp + 2) % nd, nd - 1 - dp
+        core = dp % 2
         links = Copies(send, recv, local)
         blocks = lambda ref, b: ref.at[halves(b * rows, rows)]
         own_at = halves(dp * rows, rows)
+        beside = {"ctx": flip_bit(ctx, 0)}
+
+        def get_left(left_i, left):
+            return [links.here(left_i.at[flip_bits(ctx, 2 * j)], left.at[0, j]) for j in range(slots)]
 
         get_part = links.here(pdh2_i, part)
-        get_gu = [links.here(h2_l, l_gu), links.here(dgu_i, dgu)]
-        get_first = [links.here(a, b) for a, b in ((r1_i, r1), (small_i, sm), (dy_i, dy))]
+        get_down = get_left(m_l, l_down)
+        get_down += [
+            links.here(a, b) for a, b in ((mp_l, l_down.at[1]), (dy_i, dy), (dyp_i, dyp))
+        ]
+        get_first = [links.here(a, b) for a, b in ((r1_i, r1), (small_i, sm))]
         get_wo = links.here(wo_i, wo)
-        get_down = links.here(m_l, l_down)
-        get_attn = [
-            links.here(a, b)
-            for a, b in ((seq_i, seq), (lse_i, lse))
-        ]
+        get_gu = get_left(h2_l, l_gu) + [links.here(dgu_i, dgu)]
+        get_attn = [links.here(a, b) for a, b in ((seq_i, seq), (lse_i, lse))]
+        get_late = get_left(h1_l, l_qkv) + get_left(mixed_l, l_out) + [links.here(tok_i, x)]
 
         def tables(c):
             at = pl.ds(c * chunk, chunk)
             return [links.here(a.at[at], b) for a, b in ((keep_i, keep), (sine_i, sine))]
 
         get_tables = tables(0)
-        get_out = links.here(mixed_l, l_out)
-        get_qkv = [links.here(a, b) for a, b in ((wq_i, wq), (h1_l, l_qkv), (tok_i, x))]
-
-        gu = Gradient(links, ctx, nc, l_gu, dgu, s_gu, land_gu, stage)
-        down = Gradient(links, ctx, nc, l_down, dy, s_down, land_down, stage)
-        out = Gradient(links, ctx, nc, l_out, da, s_out, land_out, stage)
-        qkv = Gradient(links, ctx, nc, l_qkv, dq, s_qkv, land_qkv, stage)
-        order = gu.order()
-        quarter = max(1, len(order) // 4)
-        turns = [order[i : i + quarter] for i in range(0, len(order), quarter)]
+
+        def strips(i):
+            return links.here(wq_i.at[pl.ds(i * strip, strip)], wq.at[i % 2])
+
+        get_wq = [strips(0), strips(1)]
 
         def gain(row):
             lines = [
@@ -755,18 +765,52 @@
             ]
             return jnp.concatenate(lines, axis=1)
 
+        def both_lefts(left_i, left):
+            n = tall["gate"] // 2
+            at = pl.ds(pl.multiple_of(core * n, 16), n)
+            return [
+                links.to(
+                    beside,
+                    left_i.at[flip_bits(flip_bit(ctx, 0), 2 * j), at],
+                    left.at[1, j, at],
+                )
+                for j in range(slots)
+            ]
+
+        def share_lefts(copies, left):
+            n = tall["gate"] // 2
+            at = pl.ds(pl.multiple_of(core * n, 16), n)
+            for copy in copies:
+                copy.wait_recv()
+            block = left.at[1, :, at]
+            return [links.to({"dp": near}, block, block)]
+
+        down = Gradient(links, ctx, nc, l_down, (dy, dyp), s_down, land_down, stage)
+        pieces = [down]
+        for i, (slot, land) in enumerate(((s_gate, land_gate), (s_up, land_up))):
+            at = pl.ds(i * hidden, hidden)
+            right = (dgu.at[:, at], dgup.at[:, at])
+            pieces.append(Gradient(links, ctx, nc, l_gu, right, slot, land, stage))
+        gate, up = pieces[1:]
+        qkv = Gradient(links, ctx, nc, l_qkv, (dq, dqp), s_qkv, land_qkv, stage)
+        out = Gradient(links, ctx, nc, l_out, (da, dyp), s_out, land_out, stage)
+
         meet((("dp", nd), ("ctx", nc)))
         get_part.wait()
         sum2 = GroupSum(links, dp, nd, rows, part, ra, rb)
-        for copy in get_gu:
+        left_gu = both_lefts(h2_l, l_gu)
+        right_gate = links.to(
+            beside, dgu_i.at[:, pl.ds(0, hidden)], dgup.at[:, pl.ds(0, hidden)]
+        )
+        for copy in get_down:
             copy.wait()
-        for j in turns[0]:
-            gu.give(j)
+        down.slot(down.order[0])
         sum2.middle()
+        for j in down.order[1:]:
+            down.slot(j)
+        left_gu2 = share_lefts(left_gu, l_gu)
         for copy in get_first:
             copy.wait()
-        for j in turns[1]:
-            gu.give(j)
 
         dh2 = sum2.total()
         hat, inverse = normalize_rows(r1[...])
@@ -775,7 +819,7 @@
         send_da = [links.to({"dp": e}, blocks(da, dp), blocks(da, dp)) for e in (near, across)]
         sums[2:3, :] = jnp.sum(dh2 * hat, axis=0, keepdims=True)
         sums[3:4, :] = jnp.sum(dh2, axis=0, keepdims=True)
-        get_down.wait()
+        dx[...] = jnp.zeros_like(dx)
         send_da[1].wait_recv()
         forward_da = links.to({"dp": near}, blocks(da, across), blocks(da, across))
         get_wo.wait()
@@ -804,15 +848,20 @@
             )
             for i, block in enumerate((ctx, mirror))
         ]
-        dx[...] = jnp.zeros_like(dx)
-        for j in turns[0]:
-            gu.keep(j)
+        right_up = links.to(
+            beside, dgu_i.at[:, pl.ds(hidden, hidden)], dgup.at[:, pl.ds(hidden, hidden)]
+        )
+        for copy in get_gu:
+            copy.wait()
+        right_gate.wait_recv()
+        left_gu2[0].wait_recv()
+        gate.compute()
+        if bits > 1:
+            down.add(1)
         for copy in get_attn + stay:
             copy.wait()
         for copy in go:
             copy.wait_recv()
-        for j in turns[2]:
-            gu.give(j)
         for head in range(heads):
             attend_back(seq, lse, dseq, dx, heads, head)
         for c in range(length // chunk):
@@ -843,13 +892,16 @@
             )
             for i, block in enumerate((ctx, mirror))
         ]
-        for j in turns[3]:
-            gu.give(j)
-        for j in turns[1]:
-            gu.keep(j)
-        for j in turns[0]:
-            down.give(j)
-        for copy in get_qkv + stay:
+        for copy in get_late:
+            copy.wait()
+        left_qkv = both_lefts(h1_l, l_qkv)
+        if bits > 1:
+            gate.add(1)
+        if bits > 2:
+            down.add(2)
+        right_up.wait_recv()
+        up.compute()
+        for copy in stay:
             copy.wait()
         for copy in back:
             copy.wait_recv()
@@ -857,27 +909,35 @@
             for j in range(3):
                 at = j * cols + g_ * span
                 dq[:, at : at + span] = dback[g_, :, j * span : (j + 1) * span]
-
-        def dh1_tile(at, n):
-            here = pl.ds(at, n)
-            part[:, here] = last_dims(dq[...], wq[here, :]).astype(BF16)
+        right_qkv = links.to(beside, dq, dqp)
+
+        n = many // 2
+        at = halves(core * n, n)
+        right_out = links.to(beside, da.at[at], dyp.at[at])
+        left_out = [
+            links.to(beside, mixed_l.at[flip_bits(flip_bit(ctx, 0), 2 * j)], l_out.at[1, j])
+            for j in range(slots)
+        ]
 
         links.gone(*sum2.a, sum2.b)
-        over_tiles(width, 256, dh1_tile)
-        sum1 = GroupSum(links, dp, nd, rows, part, ra2, rb2)
-        for j in turns[1]:
-            down.give(j)
+        for i in range(width // strip):
+            get_wq[i].wait()
+            part[:, i * strip : (i + 1) * strip] = last_dims(dq[...], wq[i % 2]).astype(BF16)
+            if i + 2 < width // strip:
+                get_wq.append(strips(i + 2))
+        sum1 = GroupSum(links, dp, nd, rows, part, ra, rb)
+        left_qkv2 = share_lefts(left_qkv, l_qkv)
         sums[4:, :] = jnp.zeros((nd, width), F32)
         sums[pl.ds(4 + dp, 1), : 3 * cols] = jnp.sum(dq[...].astype(F32), axis=0, keepdims=True)
         sum1.middle()
-        for j in turns[2] + turns[3]:
-            down.give(j)
+        if bits > 1:
+            up.add(1)
         dh1 = sum1.total()
         hat1, inverse1 = normalize_rows(x[...].astype(F32))
         sums[0:1, :] = jnp.sum(dh1 * hat1, axis=0, keepdims=True)
         sums[1:2, :] = jnp.sum(dh1, axis=0, keepdims=True)
         partners = [("dp", flip_bit(dp, b)) for b in range(nd.bit_length() - 1)]
-        partners += [("ctx", flip_bit(ctx, b)) for b in range(nc.bit_length() - 1)]
+        partners += [("ctx", flip_bit(ctx, b)) for b in range(bits)]
         sums_out = []
 
         def start_sums():
@@ -898,64 +958,55 @@
         links.gone(*sum1.a, sum1.b)
         get_pout = links.here(pout_i, part)
         get_pout.wait()
-        sum0 = GroupSum(links, dp, nd, rows, part, ra, rb)
-        for j in turns[2]:
-            gu.keep(j)
-        get_out.wait()
         end_sums()
         start_sums()
-        for j in order:
-            qkv.give(j)
-        sum0.middle()
+        sum0 = GroupSum(links, dp, nd, rows, part, ra, rb)
         end_sums()
         start_sums()
-        for j in order:
-            out.give(j)
-        for j in turns[3]:
-            gu.keep(j)
-        x[...] = (r1[...] + sum0.total()).astype(BF16)
-        put_out = links.here(x, out_o)
+        sum0.middle()
+
         arriving, put = [], []
 
-        def to_owner(slots, spans):
+        def to_owner(slots_ref, spans):
             for e in (near, across, far, dp):
                 for dst, at, to, n in spans:
-                    src = slots.at[0, pl.ds(pl.multiple_of(e * share, 16), share), pl.ds(at, n)]
+                    src = slots_ref.at[0, pl.ds(pl.multiple_of(e * share, 16), share), pl.ds(at, n)]
                     place = dst.at[:, lanes(to + dp * n, n)]
                     if e is dp:
                         put.append(links.here(src, place))
                     else:
                         arriving.append(links.to({"dp": e}, src, place))
 
-        def keep_all(piece):
-            for j in order:
-                piece.keep(j)
-
-        def add_all(piece, bit):
-            for j in sorted(range(0, nc // 2, 1 << bit), key=lambda j: (j & -j) or nc):
-                piece.add(bit, j)
-
-        gu_spans = ((gate_o, 0, 0, hidden), (up_o, hidden, 0, hidden))
         qkv_spans = tuple((qkv_o, j * cols, j * width, cols) for j in range(3))
-        closes = (
-            lambda: to_owner(s_gu, gu_spans),
-            lambda: put.append(links.here(s_down.at[0], down_o)),
-            lambda: to_owner(s_qkv, qkv_spans),
-            lambda: put.append(links.here(s_out.at[0], out_g_o)),
-        )
-        pieces = (gu, down, qkv, out)
-        bits = nc.bit_length() - 1
-        for i in range(len(pieces) + bits - 1):
-            if 0 < i < len(pieces):
-                keep_all(pieces[i])
-            if i == len(pieces) - 1:
-                end_sums()
-                start_sums()
-            for bit in range(1, bits):
-                if 0 <= i - (bit - 1) < len(pieces):
-                    add_all(pieces[i - (bit - 1)], bit)
-                    if bit == bits - 1:
-                        closes[i - (bit - 1)]()
+
+        for bit in range(3, bits):
+            down.add(bit)
+        put.append(links.here(s_down.at[0], down_o))
+        for bit in range(2, bits):
+            gate.add(bit)
+        to_owner(s_gate, ((gate_o, 0, 0, hidden),))
+        right_qkv.wait_recv()
+        left_qkv2[0].wait_recv()
+        qkv.compute()
+        right_out.wait_recv()
+        right_out2 = links.to({"dp": near}, dyp.at[at], dyp.at[at])
+        for bit in range(2, bits):
+            up.add(bit)
+        to_owner(s_up, ((up_o, 0, 0, hidden),))
+        x[...] = (r1[...] + sum0.total()).astype(BF16)
+        put_out = links.here(x, out_o)
+        right_out2.wait_recv()
+        for copy in left_out:
+            copy.wait_recv()
+        out.compute()
+        end_sums()
+        start_sums()
+        for bit in range(1, bits):
+            qkv.add(bit)
+        to_owner(s_qkv, qkv_spans)
+        for bit in range(1, bits):
+            out.add(bit)
+        put.append(links.here(s_out.at[0], out_g_o))
         while len(sums_out) < len(partners):
             end_sums()
             start_sums()
@@ -969,33 +1020,36 @@
 
     anywhere = pl.BlockSpec(memory_space=pl.ANY)
     shape = jax.ShapeDtypeStruct
-    landings = nc - 1
     outs = [
         ((rows, width), BF16),
         ((rows, width), F32),
         ((share, nd * hidden), BF16),
         ((share, nd * hidden), BF16),
         ((share, 3 * width), BF16),
-        ((left_rows["down"], width), BF16),
-        ((left_rows["out"], width), BF16),
+        ((tall["down"], width), BF16),
+        ((tall["out"], width), BF16),
         ((4 + nd, width), F32),
-        *[((landings, left_rows[k], right_cols[k]), BF16) for k in names],
+        *[((max(1, slots - 1), tall[k], flat[k]), BF16) for k in names],
     ]
     scratch = [
-        *[((nc, left_rows[k], many), BF16) for k in names],
-        ((many, right_cols["gu"]), BF16),
+        *[((2, slots, tall[k], many), BF16) for k in ("gate", "down", "out", "qkv")],
+        ((many, 2 * hidden), BF16),
+        ((many, 2 * hidden), BF16),
+        ((many, width), BF16),
         ((many, width), BF16),
         ((many, width), BF16),
         ((many, 3 * cols), BF16),
-        *[((slots, left_rows[k], right_cols[k]), BF16) for k in names],
-        ((max(left_rows.values()), max(right_cols.values())), BF16),
+        ((many, 3 * cols), BF16),
+        *[((slots, tall[k], flat[k]), BF16) for k in names],
+        ((max(tall.values()), max(flat.values())), BF16),
         ((many, width), BF16),
-        *[((2 * rows, width), BF16), ((rows, width), BF16)] * 2,
+        ((2 * rows, width), BF16),
+        ((rows, width), BF16),
         ((rows, width), F32),
         ((rows, width), F32),
         ((rows, width), BF16),
-        (small.shape, F32),
-        ((width, 3 * cols), BF16),
+        (f["small"].shape, F32),
+        ((2, strip, 3 * cols), BF16),
         ((cols, width), BF16),
         ((length, wide), BF16),
         ((heads, length), F32),
@@ -1006,27 +1060,27 @@
         ((chunk, 128), F32),
         ((groups, many, wide), BF16),
         ((4 + nd, width), F32),
-        ((nc.bit_length() + nd.bit_length() - 2, 4 + nd, width), F32),
+        ((bits + nd.bit_length() - 1, 4 + nd, width), F32),
     ]
-    remotes = 9 + 3 + 4 * (nc - 1) + 4 * (nc - 1) + nc.bit_length() + nd.bit_length() + 3 * 5 + 8
+    remotes = 64 + 4 * nc + 7 * nc
     return pl.pallas_call(
         body,
         out_shape=[shape(*o) for o in outs],
-        in_specs=[anywhere] * 17,
+        in_specs=[anywhere] * 19,
         out_specs=[anywhere] * len(outs),
         scratch_shapes=[pltpu.VMEM(*s) for s in scratch]
         + [
             pltpu.SemaphoreType.DMA((remotes,)),
             pltpu.SemaphoreType.DMA((remotes,)),
-            pltpu.SemaphoreType.DMA((40 + 4 * nc,)),
+            pltpu.SemaphoreType.DMA((64 + 7 * nc,)),
         ],
         compiler_params=pltpu.CompilerParams(
             collective_id=1, has_side_effects=True, vmem_limit_bytes=VMEM_BYTES
         ),
     )(
-        lefts["gu"], lefts["down"], lefts["out"], lefts["qkv"],
-        f["dy"], f["dgu"], f["wq"], f["seq"], f["lse"], f["r1"], f["pdh2"], f["pout"],
-        small, tokens, w_out, keep_t, sine_t,
+        f["h2"], f["m"], f["mp"], mixed_left, f["h1"],
+        f["dy"], f["dyp"], f["dgu"], f["wq"], f["seq"], f["lse"], f["r1"], f["pdh2"], f["pout"],
+        f["small"], tokens, w_out, keep_t, sine_t,
     )
 
 
@@ -1039,7 +1093,6 @@
     rows = 2 * tokens.shape[3]
     nd, nc = lax.axis_size("dp"), lax.axis_size("ctx")
     dp, ctx = lax.axis_index("dp"), lax.axis_index("ctx")
-    many = nd * rows
     x = tokens.reshape(rows, width)
 
     small = jnp.concatenate([norms.reshape(-1), b_qkv]).astype(F32)
@@ -1048,18 +1101,8 @@
         nd, nc, x, cotangent.reshape(rows, width), small, w_qkv, w_gate, w_up, w_out, w_down
     )
 
-    def by_owner(left):
-        left = left.reshape(nc, -1, many)
-        return jnp.pad(left, ((0, 0), (0, -left.shape[1] % 16), (0, 0)))
-
-    lefts = {
-        "gu": f["h2"],
-        "down": by_owner(f["m"]),
-        "out": by_owner(f["mixed"]),
-        "qkv": f["h1"],
-    }
     result, tokens_grad, g_gate, g_up, g_qkv, g_down, g_out, sums = backward(
-        nd, nc, f, f["small"], x, w_out, lefts
+        nd, nc, f, x, w_out
     )[:8]
     part_down, part_out = w_down.shape[0] // nc, w_out.shape[0] // nc
 

time: 575 us -> 474 us (0.82)
  the two profiles are of different devices: /device:TPU:20 before, /device:TPU:0 now
where the time goes in v6:
time: 474 us; the launch traced here: 469 us
  Pallas kernels  456 us (96%)
  other arithmetic  8.26 us (2%)
    pallas_call x1, Pallas kernels, backward(): pl.pallas_call(body, out_shape=[shape(*o) for o in outs], in_specs=[anywh...  289 us
    pallas_call x1, Pallas kernels, forward(): pl.pallas_call(body, out_shape=[shape(*o) for o in outs.values()], in_spe...  167 us

profile of v6, /device:TPU:0, one launch (start us, length us, event | category | flops | bytes accessed | tf_op | source)
XLA Modules:
  0.0 469.0 jit_solution(17798507163481937537)
XLA Ops:
  0.6 0.7 copy.22
  1.3 1.3 fusion.4.small_i
  2.6 167.4 %shard_map.196 = (bf16[8,256,512]{2,1,0:T(8,128)(2,1)}, bf16[512,2048]{1,0:T(8,128)(2,1)}, bf16[2048,1536]{1,0:T(8,128)(2,1)}, bf16[1024,768]{1,0:T(8,128)(2,1)}...) custom-call(bf16[128,2048]{1,0:T(8,128)(2,1)} %bitcast.17, ...), custom_call_target="tpu_custom_call" | custom-call | tf_op jit(solution)/shard_map/pallas_call | solution.py:562
  170.0 288.6 %shard_map.197 = (bf16[128,2048]{1,0:T(8,128)(2,1)}, f32[128,2048]{1,0:T(8,128)}, bf16[64,5632]{1,0:T(8,128)(2,1)}, bf16[64,5632]{1,0:T(8,128)(2,1)}, bf16[64,61...) custom-call(bf16[8,256,512]{2,1,0:T(8,128)(2,1)} %get-tuple-element., ...), custom_call_target="tpu_custom_call" | custom-call | tf_op jit(solution)/shard_map/pallas_call | solution.py:1066
  458.6 0.0 copy-start.3
  458.6 0.0 copy-start.2
  458.6 2.5 convert_element_type.18
  461.1 0.0 copy-done.3
  461.1 0.0 copy-start.1
  461.1 1.2 convert_element_type.20
  462.3 0.0 copy-done.2
  462.3 0.0 copy-start.5
  462.3 0.0 copy-start.6
  462.3 1.2 convert_element_type.21
  463.5 0.0 copy-start.4
  463.5 0.0 copy-done.1
  463.5 0.0 copy-start
  463.5 1.3 convert_element_type.22
  464.8 0.0 copy-done.5
  464.8 0.8 convert_element_type.19
  465.6 0.0 copy-done.6
  465.6 0.1 reshape.60
  465.7 0.6 constant_dynamic-slice_fusion
  466.3 0.1 reshape.59
  466.4 0.6 constant_dynamic-slice_fusion.1
  467.0 0.0 copy-done.4
  467.0 0.8 copy.25
  467.8 0.0 copy-done
  467.8 1.0 copy.26
  (2 shorter events, 0.0 us)
Async XLA Ops:
  458.6 2.5 copy-start.3
  458.6 3.7 copy-start.2
  461.1 2.4 copy-start.1
  462.3 2.5 copy-start.5
  462.3 3.3 copy-start.6
  463.5 3.5 copy-start.4
  463.5 4.3 copy-start

commit v7 on v6

--- a/solution.py
+++ b/solution.py
@@ -12,7 +12,7 @@
 MESH = pl.DeviceIdType.MESH
 F32 = jnp.float32
 BF16 = jnp.bfloat16
-VMEM_BYTES = 62 * 1024 * 1024
+VMEM_BYTES = 63 * 1024 * 1024
 
 
 def normalize_rows(field):
@@ -72,6 +72,19 @@
         if mask >> bit & 1:
             i = flip_bit(i, bit)
     return i
+
+
+def first_cut(hidden):
+    return min(1024, hidden)
+
+
+def step_orders(nc):
+    usual = list(range(nc.bit_length() - 1))
+    return usual, [1, 0] + usual[2:]
+
+
+def spread(mask, order):
+    return sum((mask >> i & 1) << bit for i, bit in enumerate(order))
 
 
 def halves(start, size):
@@ -219,9 +232,9 @@
     def body(
         tok_i, cot_i, small_i, wq_i, wg_i, wu_i, wo_i, wd_i, keep_i, sine_i,
         h1_o, dy_o, wq_o, seq_o, lse_o, mixed_o, r1_o, h2_o, m_o, dgu_o, pout_o, pdh2_o, small_o,
-        dyp_o, mp_o,
+        dyp_o, mp_o, h2p_o, gatep_o,
         tok, dy, sm, wq, h1, qkv, seq, lse, o, mixed, wo, part, ra, rb, r1, h2, wgu, wd, m, dgu,
-        turns, left1, left2, m_t, mixed_t, send, recv, local,
+        turns, left1, left2, m_t, mixed_t, dyp, h2p, send, recv, local,
     ):
         dp, ctx = lax.axis_index("dp"), lax.axis_index("ctx")
         near, across, far = flip_one(dp), (dp + 2) % nd, nd - 1 - dp
@@ -284,8 +297,8 @@
         wq_x = [qkv_columns(e, spot) for e in (across, far)]
         send_tok = [links.to({"dp": e}, tok_i, blocks(tok, dp)) for e in (near, across)]
         wq_near = qkv_columns(near, None)
-        wgu_x = [hidden_columns(e, spot) for e in (across, far)]
-        send_dyp = [links.to(sides[0], cot_i, blocks(dyp_o, dp))]
+        send_dyp = [links.to(sides[1], cot_i, blocks(dyp, dp))]
+        wgu_x = [hidden_columns(e, spot) for e in (far, across)]
         get_wo = links.here(wo_i, wo)
         get_wd = links.here(wd_i, wd)
         get_dy = links.here(cot_i, blocks(dy, dp))
@@ -329,7 +342,7 @@
         first_norm(across)
         forward_tok.wait_recv()
         first_norm(far)
-        wgu_d = [hidden_columns(e, 3 - spot) for e in (across, far)]
+        wgu_d = [c for e in (across, far) for c in hidden_columns(e, 3 - spot)]
         wgu_near = hidden_columns(near, None)
         send_dy = [links.to({"dp": e}, cot_i, blocks(dy, dp)) for e in (near, across)]
         put_small = links.here(sm, small_o)
@@ -381,15 +394,14 @@
             )
             for i, block in enumerate((ctx, mirror))
         ]
+        for b in range(nd):
+            turn_first(b)
+        put_h1 = links.here(left1, h1_o)
         for copy in stay:
             copy.wait()
         for copy in go:
             copy.wait_recv()
         put_seq = links.here(seq, seq_o)
-        for b in range(nd):
-            turn_first(b)
-        put_h1 = links.here(left1, h1_o)
-
         back, stay = [], []
         step = min(heads, 2)
         for head in range(heads):
@@ -406,7 +418,8 @@
                         back.append(links.to({"ctx": peer}, src, dst))
                     else:
                         stay.append(links.here(src, dst))
-        wgu_s = [c for copies, e in zip(wgu_x, (across, far)) for c in share(wgu, copies, e)]
+        wgu_far = share(wgu, wgu_x[0], far)
+        wgu_near2 = share(wgu, wgu_x[1], across)
         put_lse = links.here(lse, lse_o)
         get_wo.wait()
         for copy in stay:
@@ -435,7 +448,7 @@
         to_across = links.to({"dp": across}, blocks(part, across), rb)
         send_dy[1].wait_recv()
         forward_dy = links.to({"dp": near}, blocks(dy, across), blocks(dy, across))
-        send_dyp.append(links.to(sides[0], blocks(dy, across), blocks(dyp_o, across)))
+        send_dyp.append(links.to(sides[1], blocks(dy, across), blocks(dyp, across)))
         to_near[1].wait_recv()
         own_at = halves(dp * rows, rows)
         r1[...] = tok[own_at, :].astype(F32) + (
@@ -457,11 +470,19 @@
         get_dy.wait()
         for copy in get_wgu:
             copy.wait()
-        for copy in wgu_near + wgu_s + wgu_d[0] + wgu_d[1] + [send_dy[0], forward_dy, forward_h2]:
+        for copy in wgu_near + wgu_far + wgu_near2 + wgu_d + [send_dy[0], forward_dy, forward_h2]:
             copy.wait_recv()
         turn_block(h2[halves(far * rows, rows), :], left2, far, nd, nc)
         put_h2 = links.here(left2, h2_o)
         put_dy = links.here(dy, dy_o)
+
+        n = left2.shape[1] // 2
+        at = pl.ds(pl.multiple_of(dp % 2 * n, 16), n)
+        send_left = [
+            links.to(sides[0], left2.at[flip_bits(flip_bit(ctx, 0), 2 * j), at], h2p.at[j, at])
+            for j in range(nc // 2)
+        ]
+        send_gate = []
         def hidden_tile(at, n):
             here = pl.ds(at, n)
             gate = plain(h2[...], wgu[:, here])
@@ -474,18 +495,27 @@
 
         if padded != share_down:
             m[:, hidden:] = jnp.zeros((many, padded - share_down), BF16)
-        over_tiles(hidden, 256, hidden_tile)
+        for at, n in tiles(hidden, 512):
+            over_tiles(n, 256, lambda i, size, at=at: hidden_tile(at + i, size))
+            here = pl.ds(at, n)
+            if at + n <= first_cut(hidden):
+                send_gate.append(links.to(sides[0], dgu.at[:, here], gatep_o.at[:, here]))
         for c in range(nc):
             m_t[c] = m[:, c * share_down : c * share_down + padded].T
         put_m = links.here(m_t, m_o)
 
         send_m, forward_dyp = [], []
         for j in range(nc // 2):
-            owner = flip_bits(flip_bit(ctx, 0), 2 * j)
-            send_m.append(links.to(sides[0], m_t.at[owner], mp_o.at[j]))
+            owner = flip_bits(flip_bit(ctx, 1), spread(2 * j, step_orders(nc)[1]))
+            send_m.append(links.to(sides[1], m_t.at[owner], mp_o.at[j]))
         for copy, b in zip(send_dyp, (dp, across)):
             copy.wait_recv()
-            forward_dyp.append(links.to({"dp": near}, blocks(dyp_o, b), blocks(dyp_o, b)))
+            forward_dyp.append(links.to({"dp": near}, blocks(dyp, b), blocks(dyp, b)))
+        for copy in send_left:
+            copy.wait_recv()
+        n = left2.shape[1] // 2
+        at = pl.ds(pl.multiple_of(dp % 2 * n, 16), n)
+        forward_left = links.to({"dp": near}, h2p.at[:, at], h2p.at[:, at])
         put_dgu = links.here(dgu, dgu_o)
 
         def dh2_tile(at, n):
@@ -502,12 +532,15 @@
 
         over_tiles(width, 256, result_tile)
         put_pout = links.here(tok, pout_o)
-        for copy in send_m + forward_dyp:
+        for copy in forward_dyp + [forward_left]:
+            copy.wait_recv()
+        put_other = [links.here(dyp, dyp_o), links.here(h2p, h2p_o)]
+        for copy in send_m + send_gate:
             copy.wait_recv()
 
         links.gone(*links.left)
         for copy in (
-            put_small, put_h1, put_wq, put_seq, put_lse, put_mixed, put_r1, put_h2, put_dy, put_m, put_dgu,
+            *put_other, put_small, put_h1, put_wq, put_seq, put_lse, put_mixed, put_r1, put_h2, put_dy, put_m, put_dgu,
             put_pdh2, put_pout,
         ):
             copy.wait()
@@ -531,6 +564,8 @@
         small=((nd,) + small.shape, F32),
         dyp=((many, width), BF16),
         mp=((nc // 2, padded, many), BF16),
+        h2p=((nc // 2, width // nc, many), BF16),
+        gatep=((many, first_cut(hidden)), BF16),
     )
     scratch = [
         ((many, width), BF16),
@@ -558,6 +593,8 @@
         ((nc, width // nc, many), BF16),
         ((nc, padded, many), BF16),
         ((cols, many), BF16),
+        ((many, width), BF16),
+        ((nc // 2, width // nc, many), BF16),
     ]
     results = pl.pallas_call(
         body,
@@ -639,8 +676,9 @@
 
 
 class Gradient:
-    def __init__(self, links, ctx, nc, left, right, slots, landing, stage):
-        self.links, self.ctx, self.nc = links, ctx, nc
+    def __init__(self, links, ctx, bits, left, right, slots, landing, stage):
+        self.links, self.ctx, self.bits, self.nc = links, ctx, bits, 1 << len(bits)
+        nc = self.nc
         self.left, self.right, self.slots = left, right, slots
         self.landing = landing
         self.stage = stage.at[pl.ds(0, slots.shape[1]), pl.ds(0, slots.shape[2])]
@@ -651,11 +689,15 @@
         base = sum(self.nc >> (b + 1) for b in range(1, bit))
         return self.landing.at[base + (j >> bit)]
 
-    def compute(self):
+    def compute(self, send=True):
         for j in self.order:
-            self.slot(j)
-
-    def slot(self, j):
+            self.slot(j, send)
+
+    def start(self):
+        for j in self.order:
+            self._pass(1, j)
+
+    def slot(self, j, send=True):
         mine, other = self.left[0][j], self.left[1][j]
 
         def step(at, n):
@@ -664,13 +706,16 @@
             self.slots[j, :, here] = acc.astype(BF16)
 
         over_tiles(self.slots.shape[2], 512, step)
-        self._pass(1, j)
+        if send:
+            self._pass(1, j)
 
     def _pass(self, bit, j):
         low = j & -j
         if j and low == 1 << (bit - 1):
             self.sent[bit, j] = self.links.to(
-                {"ctx": flip_bit(self.ctx, bit)}, self.slots.at[j], self._landing(bit, j - low)
+                {"ctx": flip_bit(self.ctx, self.bits[bit])},
+                self.slots.at[j],
+                self._landing(bit, j - low),
             )
 
     def add(self, bit):
@@ -703,10 +748,11 @@
     hidden = f["dgu"].shape[1] // 2
     slots = nc // 2
     share = width // (nd * nc)
-    tall = {"gate": nd * share, "down": f["m"].shape[1], "out": cols // nc, "qkv": nd * share}
-    tall["up"] = tall["gate"]
-    flat = {"gate": hidden, "up": hidden, "down": width, "out": width, "qkv": 3 * cols}
-    names = ("down", "gate", "up", "qkv", "out")
+    tall = {"gu": nd * share, "down": f["m"].shape[1], "out": cols // nc, "qkv": nd * share}
+    flat = {"gu": 2 * hidden, "down": width, "out": width, "qkv": 3 * cols}
+    cut = first_cut(hidden)
+    ranges = tiles(2 * hidden, cut)
+    names = ("down", "gu", "qkv", "out")
     bits = nc.bit_length() - 1
     keep_t, sine_t = rotary_pair_tables(length)
     chunk = length if length <= 1024 else 256
@@ -714,15 +760,15 @@
     mixed_left = f["mixed"].reshape(nc, cols // nc, many)
 
     def body(
-        h2_l, m_l, mp_l, mixed_l, h1_l, dy_i, dyp_i, dgu_i, wq_i, seq_i, lse_i, r1_i, pdh2_i, pout_i,
+        h2_l, h2p_l, gatep_i, m_l, mp_l, mixed_l, h1_l, dy_i, dyp_i, dgu_i, wq_i, seq_i, lse_i, r1_i, pdh2_i, pout_i,
         small_i, tok_i, wo_i, keep_i, sine_i,
         out_o, tg_o, gate_o, up_o, qkv_o, down_o, out_g_o, sums_o,
-        land_down, land_gate, land_up, land_qkv, land_out,
+        land_down, land_gu, land_qkv, land_out,
         l_gu, l_down, l_out, l_qkv, dgu, dgup, dy, dyp, da, dq, dqp,
-        s_down, s_gate, s_up, s_qkv, s_out, stage,
+        s_down, s_gu, s_qkv, s_out, stage,
         part, ra, rb, r1, dr1, x, sm, wq, wo, seq, lse,
         dmix, dseq, dx, keep, sine, dback, sums, sums_in,
-        send, recv, local,
+        send, recv, local, free,
     ):
         dp, ctx = lax.axis_index("dp"), lax.axis_index("ctx")
         near, across, far = flip_one(dp), (dp + 2) % nd, nd - 1 - dp
@@ -732,17 +778,26 @@
         own_at = halves(dp * rows, rows)
         beside = {"ctx": flip_bit(ctx, 0)}
 
-        def get_left(left_i, left):
-            return [links.here(left_i.at[flip_bits(ctx, 2 * j)], left.at[0, j]) for j in range(slots)]
+        usual, swapped = step_orders(nc)
+
+        def get_left(left_i, left, order=usual):
+            return [
+                links.here(left_i.at[flip_bits(ctx, spread(2 * j, order))], left.at[0, j])
+                for j in range(slots)
+            ]
 
         get_part = links.here(pdh2_i, part)
-        get_down = get_left(m_l, l_down)
+        get_gu = get_left(h2_l, l_gu)
+        get_gu += [
+            links.here(a, b)
+            for a, b in ((h2p_l, l_gu.at[1]), (dgu_i, dgu), (gatep_i, dgup.at[:, pl.ds(0, cut)]))
+        ]
+        get_down = get_left(m_l, l_down, swapped)
         get_down += [
             links.here(a, b) for a, b in ((mp_l, l_down.at[1]), (dy_i, dy), (dyp_i, dyp))
         ]
         get_first = [links.here(a, b) for a, b in ((r1_i, r1), (small_i, sm))]
         get_wo = links.here(wo_i, wo)
-        get_gu = get_left(h2_l, l_gu) + [links.here(dgu_i, dgu)]
         get_attn = [links.here(a, b) for a, b in ((seq_i, seq), (lse_i, lse))]
         get_late = get_left(h1_l, l_qkv) + get_left(mixed_l, l_out) + [links.here(tok_i, x)]
 
@@ -766,7 +821,7 @@
             return jnp.concatenate(lines, axis=1)
 
         def both_lefts(left_i, left):
-            n = tall["gate"] // 2
+            n = tall["gu"] // 2
             at = pl.ds(pl.multiple_of(core * n, 16), n)
             return [
                 links.to(
@@ -778,38 +833,50 @@
             ]
 
         def share_lefts(copies, left):
-            n = tall["gate"] // 2
+            n = tall["gu"] // 2
             at = pl.ds(pl.multiple_of(core * n, 16), n)
             for copy in copies:
                 copy.wait_recv()
             block = left.at[1, :, at]
             return [links.to({"dp": near}, block, block)]
 
-        down = Gradient(links, ctx, nc, l_down, (dy, dyp), s_down, land_down, stage)
-        pieces = [down]
-        for i, (slot, land) in enumerate(((s_gate, land_gate), (s_up, land_up))):
-            at = pl.ds(i * hidden, hidden)
-            right = (dgu.at[:, at], dgup.at[:, at])
-            pieces.append(Gradient(links, ctx, nc, l_gu, right, slot, land, stage))
-        gate, up = pieces[1:]
-        qkv = Gradient(links, ctx, nc, l_qkv, (dq, dqp), s_qkv, land_qkv, stage)
-        out = Gradient(links, ctx, nc, l_out, (da, dyp), s_out, land_out, stage)
+        down = Gradient(links, ctx, swapped, l_down, (dy, dyp), s_down, land_down, stage)
+        gu = []
+        for at, n in ranges:
+            here = pl.ds(at, n)
+            gu.append(
+                Gradient(
+                    links, ctx, usual, l_gu, (dgu.at[:, here], dgup.at[:, here]),
+                    s_gu.at[:, :, here], land_gu.at[:, :, here], stage,
+                )
+            )
+        qkv = []
+        for j in range(3):
+            at = pl.ds(j * cols, cols)
+            qkv.append(
+                Gradient(
+                    links, ctx, usual, l_qkv, (dq.at[:, at], dqp.at[:, at]),
+                    s_qkv.at[:, :, at], land_qkv.at[:, :, at], stage,
+                )
+            )
+        out = Gradient(links, ctx, usual, l_out, (da, dyp), s_out, land_out, stage)
 
         meet((("dp", nd), ("ctx", nc)))
         get_part.wait()
         sum2 = GroupSum(links, dp, nd, rows, part, ra, rb)
-        left_gu = both_lefts(h2_l, l_gu)
-        right_gate = links.to(
-            beside, dgu_i.at[:, pl.ds(0, hidden)], dgup.at[:, pl.ds(0, hidden)]
-        )
-        for copy in get_down:
+
+        def send_right(i):
+            here = pl.ds(*ranges[i])
+            return links.to(beside, dgu_i.at[:, here], dgup.at[:, here])
+
+        right_gu = [None, send_right(1)]
+        for copy in get_gu:
             copy.wait()
-        down.slot(down.order[0])
+        gu[0].slot(gu[0].order[0])
         sum2.middle()
-        for j in down.order[1:]:
-            down.slot(j)
-        left_gu2 = share_lefts(left_gu, l_gu)
-        for copy in get_first:
+        for j in gu[0].order[1:]:
+            gu[0].slot(j)
+        for copy in get_first + get_down:
             copy.wait()
 
         dh2 = sum2.total()
@@ -848,16 +915,12 @@
             )
             for i, block in enumerate((ctx, mirror))
         ]
-        right_up = links.to(
-            beside, dgu_i.at[:, pl.ds(hidden, hidden)], dgup.at[:, pl.ds(hidden, hidden)]
-        )
-        for copy in get_gu:
-            copy.wait()
-        right_gate.wait_recv()
-        left_gu2[0].wait_recv()
-        gate.compute()
+        right_gu += [send_right(i) for i in range(2, len(ranges))]
+        left_qkv = both_lefts(h1_l, l_qkv)
+        right_gu[1].wait_recv()
+        gu[1].compute()
         if bits > 1:
-            down.add(1)
+            gu[0].add(1)
         for copy in get_attn + stay:
             copy.wait()
         for copy in go:
@@ -894,13 +957,12 @@
         ]
         for copy in get_late:
             copy.wait()
-        left_qkv = both_lefts(h1_l, l_qkv)
-        if bits > 1:
-            gate.add(1)
-        if bits > 2:
-            down.add(2)
-        right_up.wait_recv()
-        up.compute()
+        down.compute()
+        for i, device in enumerate((beside, {"dp": near})):
+            pl.semaphore_signal(free.at[i], inc=1, device_id=device, device_id_type=MESH)
+        for i in range(2, len(ranges)):
+            right_gu[i].wait_recv()
+            gu[i].compute()
         for copy in stay:
             copy.wait()
         for copy in back:
@@ -909,16 +971,22 @@
             for j in range(3):
                 at = j * cols + g_ * span
                 dq[:, at : at + span] = dback[g_, :, j * span : (j + 1) * span]
-        right_qkv = links.to(beside, dq, dqp)
+        right_qkv = [
+            links.to(beside, dq.at[:, pl.ds(j * cols, cols)], dqp.at[:, pl.ds(j * cols, cols)])
+            for j in range(3)
+        ]
 
         n = many // 2
         at = halves(core * n, n)
+        pl.semaphore_wait(free.at[0], 1)
         right_out = links.to(beside, da.at[at], dyp.at[at])
         left_out = [
             links.to(beside, mixed_l.at[flip_bits(flip_bit(ctx, 0), 2 * j)], l_out.at[1, j])
             for j in range(slots)
         ]
 
+        if bits > 1:
+            gu[1].add(1)
         links.gone(*sum2.a, sum2.b)
         for i in range(width // strip):
             get_wq[i].wait()
@@ -930,8 +998,18 @@
         sums[4:, :] = jnp.zeros((nd, width), F32)
         sums[pl.ds(4 + dp, 1), : 3 * cols] = jnp.sum(dq[...].astype(F32), axis=0, keepdims=True)
         sum1.middle()
+
+        def compute_qkv(j):
+            right_qkv[j].wait_recv()
+            qkv[j].compute()
+
+        left_qkv2[0].wait_recv()
+        compute_qkv(0)
         if bits > 1:
-            up.add(1)
+            for i in range(2, len(ranges)):
+                gu[i].add(1)
+            down.add(1)
+        compute_qkv(1)
         dh1 = sum1.total()
         hat1, inverse1 = normalize_rows(x[...].astype(F32))
         sums[0:1, :] = jnp.sum(dh1 * hat1, axis=0, keepdims=True)
@@ -955,62 +1033,83 @@
         start_sums()
         dr1[...] += norm_reverse(dh1, gain(0), hat1, inverse1)
         put_tg = links.here(dr1, tg_o)
-        links.gone(*sum1.a, sum1.b)
-        get_pout = links.here(pout_i, part)
-        get_pout.wait()
-        end_sums()
-        start_sums()
-        sum0 = GroupSum(links, dp, nd, rows, part, ra, rb)
-        end_sums()
-        start_sums()
-        sum0.middle()
-
         arriving, put = [], []
 
         def to_owner(slots_ref, spans):
             for e in (near, across, far, dp):
-                for dst, at, to, n in spans:
+                for dst, at, to, n, every in spans:
                     src = slots_ref.at[0, pl.ds(pl.multiple_of(e * share, 16), share), pl.ds(at, n)]
-                    place = dst.at[:, lanes(to + dp * n, n)]
+                    place = dst.at[:, lanes(to + dp * every, n)]
                     if e is dp:
                         put.append(links.here(src, place))
                     else:
                         arriving.append(links.to({"dp": e}, src, place))
 
-        qkv_spans = tuple((qkv_o, j * cols, j * width, cols) for j in range(3))
-
-        for bit in range(3, bits):
+        qkv_spans = tuple((qkv_o, j * cols, j * width, cols, cols) for j in range(3))
+
+        def close_gu(i):
+            for bit in range(2, bits):
+                gu[i].add(bit)
+            at, n = ranges[i]
+            for dst, base in ((gate_o, 0), (up_o, hidden)):
+                first, last = max(at, base), min(at + n, base + hidden)
+                if first < last:
+                    to_owner(s_gu, ((dst, first, first - base, last - first, hidden),))
+
+        def next_sums():
+            end_sums()
+            start_sums()
+
+        links.gone(*sum1.a, sum1.b)
+        get_pout = links.here(pout_i, part)
+        compute_qkv(2)
+        next_sums()
+        get_pout.wait()
+        sum0 = GroupSum(links, dp, nd, rows, part, ra, rb)
+        close_gu(0)
+        next_sums()
+        sum0.middle()
+        for bit in range(2, bits):
             down.add(bit)
         put.append(links.here(s_down.at[0], down_o))
-        for bit in range(2, bits):
-            gate.add(bit)
-        to_owner(s_gate, ((gate_o, 0, 0, hidden),))
-        right_qkv.wait_recv()
-        left_qkv2[0].wait_recv()
-        qkv.compute()
         right_out.wait_recv()
+        pl.semaphore_wait(free.at[1], 1)
         right_out2 = links.to({"dp": near}, dyp.at[at], dyp.at[at])
-        for bit in range(2, bits):
-            up.add(bit)
-        to_owner(s_up, ((up_o, 0, 0, hidden),))
-        x[...] = (r1[...] + sum0.total()).astype(BF16)
-        put_out = links.here(x, out_o)
+        if bits > 1:
+            qkv[0].add(1)
+        next_sums()
         right_out2.wait_recv()
         for copy in left_out:
             copy.wait_recv()
-        out.compute()
+        out.compute(send=False)
+        x[...] = (r1[...] + sum0.total()).astype(BF16)
+        put_out = links.here(x, out_o)
+        close_gu(1)
+        if bits > 1:
+            qkv[1].add(1)
+        out.start()
+        next_sums()
+        for i in range(2, len(ranges)):
+            close_gu(i)
+        if bits > 1:
+            qkv[2].add(1)
+
+        def close_qkv(j):
+            for bit in range(2, bits):
+                qkv[j].add(bit)
+            to_owner(s_qkv, (qkv_spans[j],))
+
+        close_qkv(0)
+        if bits > 1:
+            out.add(1)
+        close_qkv(1)
+        close_qkv(2)
+        while len(sums_out) < len(partners):
+            next_sums()
         end_sums()
-        start_sums()
-        for bit in range(1, bits):
-            qkv.add(bit)
-        to_owner(s_qkv, qkv_spans)
-        for bit in range(1, bits):
+        for bit in range(2, bits):
             out.add(bit)
         put.append(links.here(s_out.at[0], out_g_o))
-        while len(sums_out) < len(partners):
-            end_sums()
-            start_sums()
-        end_sums()
         put_sums = [links.here(sums, sums_o), put_tg, put_out]
         for copy in arriving:
             copy.wait_recv()
@@ -1032,7 +1131,7 @@
         *[((max(1, slots - 1), tall[k], flat[k]), BF16) for k in names],
     ]
     scratch = [
-        *[((2, slots, tall[k], many), BF16) for k in ("gate", "down", "out", "qkv")],
+        *[((2, slots, tall[k], many), BF16) for k in ("gu", "down", "out", "qkv")],
         ((many, 2 * hidden), BF16),
         ((many, 2 * hidden), BF16),
         ((many, width), BF16),
@@ -1041,7 +1140,7 @@
         ((many, 3 * cols), BF16),
         ((many, 3 * cols), BF16),
         *[((slots, tall[k], flat[k]), BF16) for k in names],
-        ((max(tall.values()), max(flat.values())), BF16),
+        ((max(tall.values()), width), BF16),
         ((many, width), BF16),
         ((2 * rows, width), BF16),
         ((rows, width), BF16),
@@ -1066,22 +1165,55 @@
     return pl.pallas_call(
         body,
         out_shape=[shape(*o) for o in outs],
-        in_specs=[anywhere] * 19,
+        in_specs=[anywhere] * 21,
         out_specs=[anywhere] * len(outs),
         scratch_shapes=[pltpu.VMEM(*s) for s in scratch]
         + [
             pltpu.SemaphoreType.DMA((remotes,)),
             pltpu.SemaphoreType.DMA((remotes,)),
             pltpu.SemaphoreType.DMA((64 + 7 * nc,)),
+            pltpu.SemaphoreType.REGULAR((2,)),
         ],
         compiler_params=pltpu.CompilerParams(
             collective_id=1, has_side_effects=True, vmem_limit_bytes=VMEM_BYTES
         ),
     )(
-        f["h2"], f["m"], f["mp"], mixed_left, f["h1"],
+        f["h2"], f["h2p"], f["gatep"], f["m"], f["mp"], mixed_left, f["h1"],
         f["dy"], f["dyp"], f["dgu"], f["wq"], f["seq"], f["lse"], f["r1"], f["pdh2"], f["pout"],
         f["small"], tokens, w_out, keep_t, sine_t,
     )
+
+
+def widen(arrays):
+    def body(*refs):
+        n = len(arrays)
+        ins, outs, held, wide = (refs[i * n : (i + 1) * n] for i in range(4))
+        load, store = refs[4 * n :]
+        loads = [pltpu.make_async_copy(ins[i], held[i], load.at[i]) for i in range(n)]
+        for copy in loads:
+            copy.start()
+        stores = []
+        for i in range(n):
+            loads[i].wait()
+            wide[i][...] = held[i][: wide[i].shape[0], :].astype(wide[i].dtype)
+            stores.append(pltpu.make_async_copy(wide[i], outs[i], store.at[i]))
+            stores[-1].start()
+        for copy in stores:
+            copy.wait()
+
+    anywhere = pl.BlockSpec(memory_space=pl.ANY)
+    n = len(arrays)
+    shapes = [(rows, x.shape[1]) for x, rows, _ in arrays]
+    return pl.pallas_call(
+        body,
+        out_shape=[jax.ShapeDtypeStruct(k, kind) for k, (_, _, kind) in zip(shapes, arrays)],
+        in_specs=[anywhere] * n,
+        out_specs=[anywhere] * n,
+        scratch_shapes=[pltpu.VMEM(x.shape, x.dtype) for x, _, _ in arrays]
+        + [pltpu.VMEM(k, kind) for k, (_, _, kind) in zip(shapes, arrays)]
+        + [pltpu.SemaphoreType.DMA((n,)), pltpu.SemaphoreType.DMA((n,))],
+        compiler_params=pltpu.CompilerParams(vmem_limit_bytes=VMEM_BYTES),
+    )(*[x for x, _, _ in arrays])
 
 
 def take(x, index):
@@ -1104,21 +1236,29 @@
     result, tokens_grad, g_gate, g_up, g_qkv, g_down, g_out, sums = backward(
         nd, nc, f, x, w_out
     )[:8]
-    part_down, part_out = w_down.shape[0] // nc, w_out.shape[0] // nc
-
     place = dp * nc + ctx
     norms_grad = lax.dynamic_index_in_dim(sums[:4].reshape(4, nd * nc, -1), place, 1, keepdims=False)
     bias = sums[4:, : 3 * width // nd].reshape(nd, 3, -1).transpose(1, 0, 2)
 
+    result, tokens_grad, *grads = widen(
+        [
+            (result, rows, BF16),
+            (tokens_grad, rows, F32),
+            *[(g, g.shape[0], F32) for g in (g_qkv, g_gate, g_up)],
+            (g_down, w_down.shape[0] // nc, F32),
+            (g_out, w_out.shape[0] // nc, F32),
+        ]
+    )
+    grad_qkv, grad_gate, grad_up, grad_down, grad_out = grads
     return (
         result.reshape(tokens.shape),
         tokens_grad.reshape(tokens.shape),
-        g_qkv.astype(F32),
+        grad_qkv,
         take(bias.reshape(nd * nc, -1), place),
-        g_out[:part_out].astype(F32),
-        g_gate.astype(F32),
-        g_up.astype(F32),
-        g_down[:part_down].astype(F32),
+        grad_out,
+        grad_gate,
+        grad_up,
+        grad_down,
         norms_grad,
     )
 

time: 474 us -> 427 us (0.901)
  Pallas kernels: 456 us -> 418 us
  other arithmetic: 8.26 us -> 1.3 us
    pallas_call x1, Pallas kernels: 289 us -> 239 us  [backward(): pl.pallas_call(body, out_shape=[shape(*o) for o in outs], in_specs=[anywh...]
    convert_element_type x5 -> x0, other arithmetic: 6.96 us -> none  [the longest x1 2.49 us: shards(): g_qkv.astype(F32)]
    pallas_call x1, Pallas kernels: 167 us -> 174 us  [forward(): pl.pallas_call(body, out_shape=[shape(*o) for o in outs.values()], in_spe...]
where the time goes in v7:
time: 427 us; the launch traced here: 422 us
  Pallas kernels  418 us (98%)
    pallas_call x1, Pallas kernels, backward(): pl.pallas_call(body, out_shape=[shape(*o) for o in outs], in_specs=[anywh...  239 us
    pallas_call x1, Pallas kernels, forward(): pl.pallas_call(body, out_shape=[shape(*o) for o in outs.values()], in_spe...  174 us

profile of v7, /device:TPU:0, one launch (start us, length us, event | category | flops | bytes accessed | tf_op | source)
XLA Modules:
  0.0 422.1 jit_solution(9610776513396707275)
XLA Ops:
  0.6 0.7 copy.22
  1.3 1.3 fusion.4.small_i
  2.6 173.6 %shard_map.196 = (bf16[8,256,512]{2,1,0:T(8,128)(2,1)}, bf16[512,2048]{1,0:T(8,128)(2,1)}, bf16[2048,1536]{1,0:T(8,128)(2,1)}, bf16[1024,768]{1,0:T(8,128)(2,1)}...) custom-call(bf16[128,2048]{1,0:T(8,128)(2,1)} %bitcast.17, ...), custom_call_target="tpu_custom_call" | custom-call | tf_op jit(solution)/shard_map/pallas_call | solution.py:599
  176.2 239.5 %shard_map.197 = (bf16[128,2048]{1,0:T(8,128)(2,1)}, f32[128,2048]{1,0:T(8,128)}, bf16[64,5632]{1,0:T(8,128)(2,1)}, bf16[64,5632]{1,0:T(8,128)(2,1)}, bf16[64,61...) custom-call(bf16[8,256,512]{2,1,0:T(8,128)(2,1)} %get-tuple-element., ...), custom_call_target="tpu_custom_call" | custom-call | tf_op jit(solution)/shard_map/pallas_call | solution.py:1165
  415.7 0.0 copy-start
  415.7 4.6 %shard_map.198 = (bf16[128,2048]{1,0:T(8,128)(2,1)}, f32[128,2048]{1,0:T(8,128)}, f32[64,6144]{1,0:T(8,128)}, f32[64,5632]{1,0:T(8,128)}, f32[64,5632]{1,0:T(8,1...) custom-call(bf16[128,2048]{1,0:T(8,128)(2,1)} %get-tuple-element.58.refs_0_, f32[128,2048]{1,0:T(8,128)} %get-tuple-element.59.refs_1_, ...), custom_call_target="tpu_custom_call" | custom-call | tf_op jit(solution)/shard_map/pallas_call | solution.py:1207
  420.3 0.0 copy-done
  420.3 0.1 reshape.60
  420.4 0.6 constant_dynamic-slice_fusion
  421.0 0.1 reshape.59
  421.1 0.6 constant_dynamic-slice_fusion.1
  (2 shorter events, 0.0 us)
Async XLA Ops:
  415.7 4.6 %copy-start = (f32[8,2048]{1,0:T(8,128)S(1)}, f32[8,2048]{1,0:T(8,128)}, u32[]{:S(2)}) copy-start(f32[8,2048]{1,0:T(8,128)} %get-tuple-element.68) | copy-start | bytes 196612

commit v8 on v7

--- a/solution.py
+++ b/solution.py
@@ -74,8 +74,17 @@
     return i
 
 
+def quarter_of(left, device, parts=4):
+    n = left.shape[-2] // parts
+    return pl.ds(pl.multiple_of(device * n, 16), n)
+
+
 def first_cut(hidden):
     return min(1024, hidden)
+
+
+def swapped_cut(hidden):
+    return min(512, hidden)
 
 
 def step_orders(nc):
@@ -232,9 +241,9 @@
     def body(
         tok_i, cot_i, small_i, wq_i, wg_i, wu_i, wo_i, wd_i, keep_i, sine_i,
         h1_o, dy_o, wq_o, seq_o, lse_o, mixed_o, r1_o, h2_o, m_o, dgu_o, pout_o, pdh2_o, small_o,
-        dyp_o, mp_o, h2p_o, gatep_o,
+        dyp_o, mp_o, h2p_o, gatep_o, upz_o,
         tok, dy, sm, wq, h1, qkv, seq, lse, o, mixed, wo, part, ra, rb, r1, h2, wgu, wd, m, dgu,
-        turns, left1, left2, m_t, mixed_t, dyp, h2p, send, recv, local,
+        turns, left1, left2, m_t, mixed_t, dyp, send, recv, local,
     ):
         dp, ctx = lax.axis_index("dp"), lax.axis_index("ctx")
         near, across, far = flip_one(dp), (dp + 2) % nd, nd - 1 - dp
@@ -402,6 +411,7 @@
         for copy in go:
             copy.wait_recv()
         put_seq = links.here(seq, seq_o)
+        put_h1.wait()
         back, stay = [], []
         step = min(heads, 2)
         for head in range(heads):
@@ -448,7 +458,6 @@
         to_across = links.to({"dp": across}, blocks(part, across), rb)
         send_dy[1].wait_recv()
         forward_dy = links.to({"dp": near}, blocks(dy, across), blocks(dy, across))
-        send_dyp.append(links.to(sides[1], blocks(dy, across), blocks(dyp, across)))
         to_near[1].wait_recv()
         own_at = halves(dp * rows, rows)
         r1[...] = tok[own_at, :].astype(F32) + (
@@ -460,6 +469,8 @@
         hat, _ = normalize_rows(r1[...])
         h2[own_at, :] = (hat * gain(2) + gain(3)).astype(BF16)
         send_h2 = [links.to({"dp": e}, blocks(h2, dp), blocks(h2, dp)) for e in (near, across)]
+        send_dyp[0].wait_recv()
+        share_dyp = [links.to({"dp": e}, blocks(dyp, dp), blocks(dyp, dp)) for e in (near, across)]
         turn_block(h2[own_at, :], left2, dp, nd, nc)
         send_h2[0].wait_recv()
         turn_block(h2[halves(near * rows, rows), :], left2, near, nd, nc)
@@ -476,11 +487,18 @@
         put_h2 = links.here(left2, h2_o)
         put_dy = links.here(dy, dy_o)
 
-        n = left2.shape[1] // 2
-        at = pl.ds(pl.multiple_of(dp % 2 * n, 16), n)
+        spare = nc // 2
         send_left = [
-            links.to(sides[0], left2.at[flip_bits(flip_bit(ctx, 0), 2 * j), at], h2p.at[j, at])
-            for j in range(nc // 2)
+            links.to(
+                sides[bit],
+                left2.at[
+                    flip_bits(flip_bit(ctx, bit), spread(2 * j, step_orders(nc)[bit])),
+                    quarter_of(left2, dp),
+                ],
+                left1.at[bit * spare + j, quarter_of(left2, dp)],
+            )
+            for bit in range(2)
+            for j in range(spare)
         ]
         send_gate = []
         def hidden_tile(at, n):
@@ -500,23 +518,24 @@
             here = pl.ds(at, n)
             if at + n <= first_cut(hidden):
                 send_gate.append(links.to(sides[0], dgu.at[:, here], gatep_o.at[:, here]))
+            if at + n <= swapped_cut(hidden):
+                there = pl.ds(hidden + at, n)
+                send_gate.append(links.to(sides[1], dgu.at[:, there], upz_o.at[:, here]))
         for c in range(nc):
             m_t[c] = m[:, c * share_down : c * share_down + padded].T
         put_m = links.here(m_t, m_o)
 
-        send_m, forward_dyp = [], []
+        put_dgu = links.here(dgu, dgu_o)
+        send_m = []
         for j in range(nc // 2):
             owner = flip_bits(flip_bit(ctx, 1), spread(2 * j, step_orders(nc)[1]))
             send_m.append(links.to(sides[1], m_t.at[owner], mp_o.at[j]))
-        for copy, b in zip(send_dyp, (dp, across)):
-            copy.wait_recv()
-            forward_dyp.append(links.to({"dp": near}, blocks(dyp, b), blocks(dyp, b)))
+        share_dyp[1].wait_recv()
+        forward_dyp = links.to({"dp": near}, blocks(dyp, across), blocks(dyp, across))
         for copy in send_left:
             copy.wait_recv()
-        n = left2.shape[1] // 2
-        at = pl.ds(pl.multiple_of(dp % 2 * n, 16), n)
-        forward_left = links.to({"dp": near}, h2p.at[:, at], h2p.at[:, at])
-        put_dgu = links.here(dgu, dgu_o)
+        own_left = left1.at[:, quarter_of(left2, dp)]
+        share_left = [links.to({"dp": e}, own_left, own_left) for e in (near, across)]
 
         def dh2_tile(at, n):
             here = pl.ds(at, n)
@@ -530,17 +549,20 @@
             here = pl.ds(at, n)
             tok[:, here] = plain(m[:, :hidden], wd[:, here]).astype(BF16)
 
+        share_left[1].wait_recv()
+        other_left = left1.at[:, quarter_of(left2, across)]
+        forward_left = links.to({"dp": near}, other_left, other_left)
         over_tiles(width, 256, result_tile)
         put_pout = links.here(tok, pout_o)
-        for copy in forward_dyp + [forward_left]:
+        for copy in (share_dyp[0], forward_dyp, share_left[0], forward_left):
             copy.wait_recv()
-        put_other = [links.here(dyp, dyp_o), links.here(h2p, h2p_o)]
+        put_other = [links.here(dyp, dyp_o), links.here(left1, h2p_o)]
         for copy in send_m + send_gate:
             copy.wait_recv()
 
         links.gone(*links.left)
         for copy in (
-            *put_other, put_small, put_h1, put_wq, put_seq, put_lse, put_mixed, put_r1, put_h2, put_dy, put_m, put_dgu,
+            *put_other, put_small, put_wq, put_seq, put_lse, put_mixed, put_r1, put_h2, put_dy, put_m, put_dgu,
             put_pdh2, put_pout,
         ):
             copy.wait()
@@ -564,8 +586,9 @@
         small=((nd,) + small.shape, F32),
         dyp=((many, width), BF16),
         mp=((nc // 2, padded, many), BF16),
-        h2p=((nc // 2, width // nc, many), BF16),
+        h2p=((nc, width // nc, many), BF16),
         gatep=((many, first_cut(hidden)), BF16),
+        upz=((many, swapped_cut(hidden)), BF16),
     )
     scratch = [
         ((many, width), BF16),
@@ -594,7 +617,6 @@
         ((nc, padded, many), BF16),
         ((cols, many), BF16),
         ((many, width), BF16),
-        ((nc // 2, width // nc, many), BF16),
     ]
     results = pl.pallas_call(
         body,
@@ -693,8 +715,9 @@
         for j in self.order:
             self.slot(j, send)
 
-    def start(self):
-        for j in self.order:
+    def start(self, part):
+        odd = [j for j in self.order if j % 2]
+        for j in odd[part * len(odd) // 2 : (part + 1) * len(odd) // 2]:
             self._pass(1, j)
 
     def slot(self, j, send=True):
@@ -751,7 +774,10 @@
     tall = {"gu": nd * share, "down": f["m"].shape[1], "out": cols // nc, "qkv": nd * share}
     flat = {"gu": 2 * hidden, "down": width, "out": width, "qkv": 3 * cols}
     cut = first_cut(hidden)
-    ranges = tiles(2 * hidden, cut)
+    cut_z = swapped_cut(hidden)
+    ranges = [(0, cut // 2), (cut // 2, cut - cut // 2)]
+    ranges += [(hidden + cut_z, hidden - cut_z), (cut, hidden - cut)]
+    range_z = (hidden, cut_z)
     names = ("down", "gu", "qkv", "out")
     bits = nc.bit_length() - 1
     keep_t, sine_t = rotary_pair_tables(length)
@@ -760,11 +786,11 @@
     mixed_left = f["mixed"].reshape(nc, cols // nc, many)
 
     def body(
-        h2_l, h2p_l, gatep_i, m_l, mp_l, mixed_l, h1_l, dy_i, dyp_i, dgu_i, wq_i, seq_i, lse_i, r1_i, pdh2_i, pout_i,
+        h2_l, h2p_l, gatep_i, upz_i, m_l, mp_l, mixed_l, h1_l, dy_i, dyp_i, dgu_i, wq_i, seq_i, lse_i, r1_i, pdh2_i, pout_i,
         small_i, tok_i, wo_i, keep_i, sine_i,
         out_o, tg_o, gate_o, up_o, qkv_o, down_o, out_g_o, sums_o,
         land_down, land_gu, land_qkv, land_out,
-        l_gu, l_down, l_out, l_qkv, dgu, dgup, dy, dyp, da, dq, dqp,
+        l_gu, l_up, l_down, l_out, l_qkv, dgu, dgup, dy, dyp, da, dq, dqp,
         s_down, s_gu, s_qkv, s_out, stage,
         part, ra, rb, r1, dr1, x, sm, wq, wo, seq, lse,
         dmix, dseq, dx, keep, sine, dback, sums, sums_in,
@@ -772,7 +798,6 @@
     ):
         dp, ctx = lax.axis_index("dp"), lax.axis_index("ctx")
         near, across, far = flip_one(dp), (dp + 2) % nd, nd - 1 - dp
-        core = dp % 2
         links = Copies(send, recv, local)
         blocks = lambda ref, b: ref.at[halves(b * rows, rows)]
         own_at = halves(dp * rows, rows)
@@ -790,7 +815,16 @@
         get_gu = get_left(h2_l, l_gu)
         get_gu += [
             links.here(a, b)
-            for a, b in ((h2p_l, l_gu.at[1]), (dgu_i, dgu), (gatep_i, dgup.at[:, pl.ds(0, cut)]))
+            for a, b in (
+                (h2p_l.at[pl.ds(0, slots)], l_gu.at[1]),
+                (dgu_i, dgu),
+                (gatep_i, dgup.at[:, pl.ds(0, cut)]),
+            )
+        ]
+        get_up = get_left(h2_l, l_up, swapped)
+        get_up += [
+            links.here(a, b)
+            for a, b in ((h2p_l.at[pl.ds(slots, slots)], l_up.at[1]), (upz_i, dgup.at[:, pl.ds(*range_z)]))
         ]
         get_down = get_left(m_l, l_down, swapped)
         get_down += [
@@ -820,36 +854,18 @@
             ]
             return jnp.concatenate(lines, axis=1)
 
-        def both_lefts(left_i, left):
-            n = tall["gu"] // 2
-            at = pl.ds(pl.multiple_of(core * n, 16), n)
-            return [
-                links.to(
-                    beside,
-                    left_i.at[flip_bits(flip_bit(ctx, 0), 2 * j), at],
-                    left.at[1, j, at],
-                )
-                for j in range(slots)
-            ]
-
-        def share_lefts(copies, left):
-            n = tall["gu"] // 2
-            at = pl.ds(pl.multiple_of(core * n, 16), n)
-            for copy in copies:
-                copy.wait_recv()
-            block = left.at[1, :, at]
-            return [links.to({"dp": near}, block, block)]
-
         down = Gradient(links, ctx, swapped, l_down, (dy, dyp), s_down, land_down, stage)
         gu = []
-        for at, n in ranges:
+        for at, n in ranges + [range_z]:
             here = pl.ds(at, n)
+            order, left = (swapped, l_up) if at == hidden else (usual, l_gu)
             gu.append(
                 Gradient(
-                    links, ctx, usual, l_gu, (dgu.at[:, here], dgup.at[:, here]),
+                    links, ctx, order, left, (dgu.at[:, here], dgup.at[:, here]),
                     s_gu.at[:, :, here], land_gu.at[:, :, here], stage,
                 )
             )
+        up = gu.pop()
         qkv = []
         for j in range(3):
             at = pl.ds(j * cols, cols)
@@ -869,24 +885,33 @@
             here = pl.ds(*ranges[i])
             return links.to(beside, dgu_i.at[:, here], dgup.at[:, here])
 
-        right_gu = [None, send_right(1)]
+        right_gu = [None, None, send_right(2)]
         for copy in get_gu:
             copy.wait()
         gu[0].slot(gu[0].order[0])
         sum2.middle()
         for j in gu[0].order[1:]:
             gu[0].slot(j)
-        for copy in get_first + get_down:
+        for copy in get_first + get_down + get_up:
             copy.wait()
+        up.compute()
+        gu[1].compute()
+        down.compute(send=False)
+        for i, device in enumerate((beside, {"dp": near}, {"dp": across})):
+            pl.semaphore_signal(free.at[i], inc=1, device_id=device, device_id_type=MESH)
 
         dh2 = sum2.total()
         hat, inverse = normalize_rows(r1[...])
         dr1[...] = dy[own_at, :].astype(F32) + norm_reverse(dh2, gain(2), hat, inverse)
         da[own_at, :] = dr1[...].astype(BF16)
         send_da = [links.to({"dp": e}, blocks(da, dp), blocks(da, dp)) for e in (near, across)]
+        pl.semaphore_wait(free.at[0], 1)
+        right_out = links.to(beside, blocks(da, dp), blocks(dyp, dp))
         sums[2:3, :] = jnp.sum(dh2 * hat, axis=0, keepdims=True)
         sums[3:4, :] = jnp.sum(dh2, axis=0, keepdims=True)
         dx[...] = jnp.zeros_like(dx)
+        if bits > 1:
+            gu[0].add(1)
         send_da[1].wait_recv()
         forward_da = links.to({"dp": near}, blocks(da, across), blocks(da, across))
         get_wo.wait()
@@ -915,16 +940,45 @@
             )
             for i, block in enumerate((ctx, mirror))
         ]
-        right_gu += [send_right(i) for i in range(2, len(ranges))]
-        left_qkv = both_lefts(h1_l, l_qkv)
-        right_gu[1].wait_recv()
-        gu[1].compute()
+        right_gu.append(send_right(3))
+
+        left_qkv = [
+            links.to(
+                beside,
+                h1_l.at[flip_bits(flip_bit(ctx, 0), 2 * j), quarter_of(l_qkv, dp)],
+                l_qkv.at[1, j, quarter_of(l_qkv, dp)],
+            )
+            for j in range(slots)
+        ]
+        left_out = [
+            links.to(beside, mixed_l.at[flip_bits(flip_bit(ctx, 0), 2 * j)], l_out.at[1, j])
+            for j in range(slots)
+        ]
+        right_gu[2].wait_recv()
+        gu[2].compute()
         if bits > 1:
-            gu[0].add(1)
+            up.add(1)
+            gu[1].add(1)
+
+        def share_right():
+            right_out.wait_recv()
+            for i in (1, 2):
+                pl.semaphore_wait(free.at[i], 1)
+            block = blocks(dyp, dp)
+            return [links.to({"dp": e}, block, block) for e in (near, across)]
+
+        def share_left():
+            for copy in left_qkv:
+                copy.wait_recv()
+            block = l_qkv.at[1, :, quarter_of(l_qkv, dp)]
+            return [links.to({"dp": e}, block, block) for e in (near, across)]
+
         for copy in get_attn + stay:
             copy.wait()
         for copy in go:
             copy.wait_recv()
+        down.start(0)
+        shared_right = share_right()
         for head in range(heads):
             attend_back(seq, lse, dseq, dx, heads, head)
         for c in range(length // chunk):
@@ -955,14 +1009,19 @@
             )
             for i, block in enumerate((ctx, mirror))
         ]
+        shared_left = share_left()
+        shared_right[1].wait_recv()
+        forward_right = links.to({"dp": near}, blocks(dyp, across), blocks(dyp, across))
         for copy in get_late:
             copy.wait()
-        down.compute()
-        for i, device in enumerate((beside, {"dp": near})):
-            pl.semaphore_signal(free.at[i], inc=1, device_id=device, device_id_type=MESH)
-        for i in range(2, len(ranges)):
-            right_gu[i].wait_recv()
-            gu[i].compute()
+        right_gu[3].wait_recv()
+        gu[3].compute()
+        shared_left[1].wait_recv()
+        block = l_qkv.at[1, :, quarter_of(l_qkv, across)]
+        forward_left = links.to({"dp": near}, block, block)
+        for copy in left_out + [shared_right[0], forward_right]:
+            copy.wait_recv()
+        out.compute()
         for copy in stay:
             copy.wait()
         for copy in back:
@@ -971,22 +1030,17 @@
             for j in range(3):
                 at = j * cols + g_ * span
                 dq[:, at : at + span] = dback[g_, :, j * span : (j + 1) * span]
-        right_qkv = [
-            links.to(beside, dq.at[:, pl.ds(j * cols, cols)], dqp.at[:, pl.ds(j * cols, cols)])
-            for j in range(3)
-        ]
-
-        n = many // 2
-        at = halves(core * n, n)
-        pl.semaphore_wait(free.at[0], 1)
-        right_out = links.to(beside, da.at[at], dyp.at[at])
-        left_out = [
-            links.to(beside, mixed_l.at[flip_bits(flip_bit(ctx, 0), 2 * j)], l_out.at[1, j])
-            for j in range(slots)
-        ]
-
+        right_qkv = []
+
+        def send_qkv():
+            here = pl.ds(len(right_qkv) * cols, cols)
+            right_qkv.append(links.to(beside, dq.at[:, here], dqp.at[:, here]))
+
+        send_qkv()
         if bits > 1:
-            gu[1].add(1)
+            gu[2].add(1)
+        send_qkv()
+        down.start(1)
         links.gone(*sum2.a, sum2.b)
         for i in range(width // strip):
             get_wq[i].wait()
@@ -994,45 +1048,21 @@
             if i + 2 < width // strip:
                 get_wq.append(strips(i + 2))
         sum1 = GroupSum(links, dp, nd, rows, part, ra, rb)
-        left_qkv2 = share_lefts(left_qkv, l_qkv)
-        sums[4:, :] = jnp.zeros((nd, width), F32)
-        sums[pl.ds(4 + dp, 1), : 3 * cols] = jnp.sum(dq[...].astype(F32), axis=0, keepdims=True)
-        sum1.middle()
+        send_qkv()
+        for copy in (shared_left[0], forward_left):
+            copy.wait_recv()
 
         def compute_qkv(j):
             right_qkv[j].wait_recv()
             qkv[j].compute()
 
-        left_qkv2[0].wait_recv()
         compute_qkv(0)
+        sum1.middle()
         if bits > 1:
-            for i in range(2, len(ranges)):
-                gu[i].add(1)
-            down.add(1)
-        compute_qkv(1)
-        dh1 = sum1.total()
-        hat1, inverse1 = normalize_rows(x[...].astype(F32))
-        sums[0:1, :] = jnp.sum(dh1 * hat1, axis=0, keepdims=True)
-        sums[1:2, :] = jnp.sum(dh1, axis=0, keepdims=True)
-        partners = [("dp", flip_bit(dp, b)) for b in range(nd.bit_length() - 1)]
-        partners += [("ctx", flip_bit(ctx, b)) for b in range(bits)]
-        sums_out = []
-
-        def start_sums():
-            i = len(sums_out)
-            if i < len(partners):
-                axis, device = partners[i]
-                sums_out.append(links.to({axis: device}, sums, sums_in.at[i]))
-
-        def end_sums():
-            i = len(sums_out) - 1
-            sums_out[i].wait_recv()
-            links.gone(sums_out[i])
-            sums[...] += sums_in[i]
-
-        start_sums()
-        dr1[...] += norm_reverse(dh1, gain(0), hat1, inverse1)
-        put_tg = links.here(dr1, tg_o)
+            gu[3].add(1)
+        sums[4:, :] = jnp.zeros((nd, width), F32)
+        sums[pl.ds(4 + dp, 1), : 3 * cols] = jnp.sum(dq[...].astype(F32), axis=0, keepdims=True)
+
         arriving, put = [], []
 
         def to_owner(slots_ref, spans):
@@ -1045,71 +1075,87 @@
                     else:
                         arriving.append(links.to({"dp": e}, src, place))
 
-        qkv_spans = tuple((qkv_o, j * cols, j * width, cols, cols) for j in range(3))
-
-        def close_gu(i):
+        def close_gu(piece, span_of):
             for bit in range(2, bits):
-                gu[i].add(bit)
-            at, n = ranges[i]
+                piece.add(bit)
+            at, n = span_of
             for dst, base in ((gate_o, 0), (up_o, hidden)):
                 first, last = max(at, base), min(at + n, base + hidden)
                 if first < last:
                     to_owner(s_gu, ((dst, first, first - base, last - first, hidden),))
 
+        def close_qkv(j):
+            for bit in range(2, bits):
+                qkv[j].add(bit)
+            to_owner(s_qkv, ((qkv_o, j * cols, j * width, cols, cols),))
+
+        compute_qkv(1)
+        close_gu(gu[0], ranges[0])
+        close_gu(up, range_z)
+        if bits > 1:
+            out.add(1)
+            down.add(1)
+
+        dh1 = sum1.total()
+        hat1, inverse1 = normalize_rows(x[...].astype(F32))
+        sums[0:1, :] = jnp.sum(dh1 * hat1, axis=0, keepdims=True)
+        sums[1:2, :] = jnp.sum(dh1, axis=0, keepdims=True)
+        partners = [("dp", flip_bit(dp, b)) for b in range(nd.bit_length() - 1)]
+        partners += [("ctx", flip_bit(ctx, b)) for b in range(bits)]
+        sums_out = []
+
+        def start_sums():
+            i = len(sums_out)
+            if i < len(partners):
+                axis, device = partners[i]
+                sums_out.append(links.to({axis: device}, sums, sums_in.at[i]))
+
+        def end_sums():
+            i = len(sums_out) - 1
+            sums_out[i].wait_recv()
+            links.gone(sums_out[i])
+            sums[...] += sums_in[i]
+
         def next_sums():
             end_sums()
             start_sums()
 
+        start_sums()
+        dr1[...] += norm_reverse(dh1, gain(0), hat1, inverse1)
+        put_tg = links.here(dr1, tg_o)
         links.gone(*sum1.a, sum1.b)
         get_pout = links.here(pout_i, part)
         compute_qkv(2)
         next_sums()
         get_pout.wait()
         sum0 = GroupSum(links, dp, nd, rows, part, ra, rb)
-        close_gu(0)
+        if bits > 1:
+            qkv[0].add(1)
+        close_gu(gu[1], ranges[1])
         next_sums()
         sum0.middle()
+        next_sums()
+        if bits > 1:
+            qkv[1].add(1)
+        x[...] = (r1[...] + sum0.total()).astype(BF16)
+        put_out = links.here(x, out_o)
+        for i in range(2, len(ranges)):
+            close_gu(gu[i], ranges[i])
+        if bits > 1:
+            qkv[2].add(1)
+        next_sums()
         for bit in range(2, bits):
             down.add(bit)
         put.append(links.here(s_down.at[0], down_o))
-        right_out.wait_recv()
-        pl.semaphore_wait(free.at[1], 1)
-        right_out2 = links.to({"dp": near}, dyp.at[at], dyp.at[at])
-        if bits > 1:
-            qkv[0].add(1)
-        next_sums()
-        right_out2.wait_recv()
-        for copy in left_out:
-            copy.wait_recv()
-        out.compute(send=False)
-        x[...] = (r1[...] + sum0.total()).astype(BF16)
-        put_out = links.here(x, out_o)
-        close_gu(1)
-        if bits > 1:
-            qkv[1].add(1)
-        out.start()
-        next_sums()
-        for i in range(2, len(ranges)):
-            close_gu(i)
-        if bits > 1:
-            qkv[2].add(1)
-
-        def close_qkv(j):
-            for bit in range(2, bits):
-                qkv[j].add(bit)
-            to_owner(s_qkv, (qkv_spans[j],))
-
-        close_qkv(0)
-        if bits > 1:
-            out.add(1)
-        close_qkv(1)
-        close_qkv(2)
-        while len(sums_out) < len(partners):
-            next_sums()
-        end_sums()
         for bit in range(2, bits):
             out.add(bit)
         put.append(links.here(s_out.at[0], out_g_o))
+        close_qkv(0)
+        close_qkv(1)
+        while len(sums_out) < len(partners):
+            next_sums()
+        close_qkv(2)
+        end_sums()
         put_sums = [links.here(sums, sums_o), put_tg, put_out]
         for copy in arriving:
             copy.wait_recv()
@@ -1131,7 +1177,7 @@
         *[((max(1, slots - 1), tall[k], flat[k]), BF16) for k in names],
     ]
     scratch = [
-        *[((2, slots, tall[k], many), BF16) for k in ("gu", "down", "out", "qkv")],
+        *[((2, slots, tall[k], many), BF16) for k in ("gu", "gu", "down", "out", "qkv")],
         ((many, 2 * hidden), BF16),
         ((many, 2 * hidden), BF16),
         ((many, width), BF16),
@@ -1165,20 +1211,20 @@
     return pl.pallas_call(
         body,
         out_shape=[shape(*o) for o in outs],
-        in_specs=[anywhere] * 21,
+        in_specs=[anywhere] * 22,
         out_specs=[anywhere] * len(outs),
         scratch_shapes=[pltpu.VMEM(*s) for s in scratch]
         + [
             pltpu.SemaphoreType.DMA((remotes,)),
             pltpu.SemaphoreType.DMA((remotes,)),
             pltpu.SemaphoreType.DMA((64 + 7 * nc,)),
-            pltpu.SemaphoreType.REGULAR((2,)),
+            pltpu.SemaphoreType.REGULAR((3,)),
         ],
         compiler_params=pltpu.CompilerParams(
             collective_id=1, has_side_effects=True, vmem_limit_bytes=VMEM_BYTES
         ),
     )(
-        f["h2"], f["h2p"], f["gatep"], f["m"], f["mp"], mixed_left, f["h1"],
+        f["h2"], f["h2p"], f["gatep"], f["upz"], f["m"], f["mp"], mixed_left, f["h1"],
         f["dy"], f["dyp"], f["dgu"], f["wq"], f["seq"], f["lse"], f["r1"], f["pdh2"], f["pout"],
         f["small"], tokens, w_out, keep_t, sine_t,
     )

time: 427 us -> 416 us (0.974)
  Pallas kernels: 418 us -> 406 us
    pallas_call x1, Pallas kernels: 239 us -> 229 us  [backward(): pl.pallas_call(body, out_shape=[shape(*o) for o in outs], in_specs=[anywh...]
where the time goes in v8:
time: 416 us; the launch traced here: 411 us
  Pallas kernels  406 us (98%)
    pallas_call x1, Pallas kernels, backward(): pl.pallas_call(body, out_shape=[shape(*o) for o in outs], in_specs=[anywh...  229 us
    pallas_call x1, Pallas kernels, forward(): pl.pallas_call(body, out_shape=[shape(*o) for o in outs.values()], in_spe...  173 us

profile of v8, /device:TPU:0, one launch (start us, length us, event | category | flops | bytes accessed | tf_op | source)
XLA Modules:
  0.0 410.6 jit_solution(3060257310867265339)
XLA Ops:
  0.6 0.7 copy.22
  1.3 1.3 fusion.4.small_i
  2.6 172.9 %shard_map.196 = (bf16[8,256,512]{2,1,0:T(8,128)(2,1)}, bf16[512,2048]{1,0:T(8,128)(2,1)}, bf16[2048,1536]{1,0:T(8,128)(2,1)}, bf16[1024,768]{1,0:T(8,128)(2,1)}...) custom-call(bf16[128,2048]{1,0:T(8,128)(2,1)} %bitcast.17, ...), custom_call_target="tpu_custom_call" | custom-call | tf_op jit(solution)/shard_map/pallas_call | solution.py:621
  175.5 228.9 %shard_map.197 = (bf16[128,2048]{1,0:T(8,128)(2,1)}, f32[128,2048]{1,0:T(8,128)}, bf16[64,5632]{1,0:T(8,128)(2,1)}, bf16[64,5632]{1,0:T(8,128)(2,1)}, bf16[64,61...) custom-call(bf16[8,256,512]{2,1,0:T(8,128)(2,1)} %get-tuple-element., ...), custom_call_target="tpu_custom_call" | custom-call | tf_op jit(solution)/shard_map/pallas_call | solution.py:1211
  404.4 0.0 copy-start
  404.4 4.6 %shard_map.198 = (bf16[128,2048]{1,0:T(8,128)(2,1)}, f32[128,2048]{1,0:T(8,128)}, f32[64,6144]{1,0:T(8,128)}, f32[64,5632]{1,0:T(8,128)}, f32[64,5632]{1,0:T(8,1...) custom-call(bf16[128,2048]{1,0:T(8,128)(2,1)} %get-tuple-element.60.refs_0_, f32[128,2048]{1,0:T(8,128)} %get-tuple-element.61.refs_1_, ...), custom_call_target="tpu_custom_call" | custom-call | tf_op jit(solution)/shard_map/pallas_call | solution.py:1253
  409.0 0.0 copy-done
  409.0 0.1 reshape.60
  409.1 0.6 constant_dynamic-slice_fusion
  409.7 0.1 reshape.59
  409.8 0.6 constant_dynamic-slice_fusion.1
  (2 shorter events, 0.0 us)
Async XLA Ops:
  404.4 4.6 %copy-start = (f32[8,2048]{1,0:T(8,128)S(1)}, f32[8,2048]{1,0:T(8,128)}, u32[]{:S(2)}) copy-start(f32[8,2048]{1,0:T(8,128)} %get-tuple-element.70) | copy-start | bytes 196612

commit v9 on v8

--- a/solution.py
+++ b/solution.py
@@ -705,7 +705,8 @@
         self.landing = landing
         self.stage = stage.at[pl.ds(0, slots.shape[1]), pl.ds(0, slots.shape[2])]
         self.sent = {}
-        self.order = sorted(range(nc // 2), key=lambda j: (j & -j) or nc)
+        low = lambda j: (j & -j) or nc
+        self.order = sorted(range(nc // 2), key=lambda j: (low(j), low(j & (j - 1))))
 
     def _landing(self, bit, j):
         base = sum(self.nc >> (b + 1) for b in range(1, bit))
@@ -716,9 +717,16 @@
             self.slot(j, send)
 
     def start(self, part):
+        for j in self.half(part):
+            self._pass(1, j)
+
+    def half(self, part):
         odd = [j for j in self.order if j % 2]
-        for j in odd[part * len(odd) // 2 : (part + 1) * len(odd) // 2]:
-            self._pass(1, j)
+        return odd[part * len(odd) // 2 : (part + 1) * len(odd) // 2]
+
+    def add_half(self, part):
+        for j in self.half(part):
+            self.add_slot(1, j - 1)
 
     def slot(self, j, send=True):
         mine, other = self.left[0][j], self.left[1][j]
@@ -1040,7 +1048,7 @@
         if bits > 1:
             gu[2].add(1)
         send_qkv()
-        down.start(1)
+        down.add_half(0)
         links.gone(*sum2.a, sum2.b)
         for i in range(width // strip):
             get_wq[i].wait()
@@ -1049,6 +1057,7 @@
                 get_wq.append(strips(i + 2))
         sum1 = GroupSum(links, dp, nd, rows, part, ra, rb)
         send_qkv()
+        down.start(1)
         for copy in (shared_left[0], forward_left):
             copy.wait_recv()
 
@@ -1094,7 +1103,7 @@
         close_gu(up, range_z)
         if bits > 1:
             out.add(1)
-            down.add(1)
+        compute_qkv(2)
 
         dh1 = sum1.total()
         hat1, inverse1 = normalize_rows(x[...].astype(F32))
@@ -1125,7 +1134,6 @@
         put_tg = links.here(dr1, tg_o)
         links.gone(*sum1.a, sum1.b)
         get_pout = links.here(pout_i, part)
-        compute_qkv(2)
         next_sums()
         get_pout.wait()
         sum0 = GroupSum(links, dp, nd, rows, part, ra, rb)
@@ -1144,6 +1152,7 @@
         if bits > 1:
             qkv[2].add(1)
         next_sums()
+        down.add_half(1)
         for bit in range(2, bits):
             down.add(bit)
         put.append(links.here(s_down.at[0], down_o))
@@ -1217,7 +1226,7 @@
         + [
             pltpu.SemaphoreType.DMA((remotes,)),
             pltpu.SemaphoreType.DMA((remotes,)),
-            pltpu.SemaphoreType.DMA((64 + 7 * nc,)),
+            pltpu.SemaphoreType.DMA((64 + 10 * nc,)),
             pltpu.SemaphoreType.REGULAR((3,)),
         ],
         compiler_params=pltpu.CompilerParams(

time: 416 us -> 412 us (level)
  no operation moved by 1% of the time
where the time goes in v9:
time: 412 us; the launch traced here: 406 us
  Pallas kernels  402 us (98%)
    pallas_call x1, Pallas kernels, backward(): pl.pallas_call(body, out_shape=[shape(*o) for o in outs], in_specs=[anywh...  225 us
    pallas_call x1, Pallas kernels, forward(): pl.pallas_call(body, out_shape=[shape(*o) for o in outs.values()], in_spe...  173 us

profile of v9, /device:TPU:0, one launch (start us, length us, event | category | flops | bytes accessed | tf_op | source)
XLA Modules:
  0.0 406.5 jit_solution(14414706889683437995)
XLA Ops:
  0.6 0.7 copy.22
  1.3 1.3 fusion.4.small_i
  2.6 172.9 %shard_map.196 = (bf16[8,256,512]{2,1,0:T(8,128)(2,1)}, bf16[512,2048]{1,0:T(8,128)(2,1)}, bf16[2048,1536]{1,0:T(8,128)(2,1)}, bf16[1024,768]{1,0:T(8,128)(2,1)}...) custom-call(bf16[128,2048]{1,0:T(8,128)(2,1)} %bitcast.17, ...), custom_call_target="tpu_custom_call" | custom-call | tf_op jit(solution)/shard_map/pallas_call | solution.py:621
  175.5 224.8 %shard_map.197 = (bf16[128,2048]{1,0:T(8,128)(2,1)}, f32[128,2048]{1,0:T(8,128)}, bf16[64,5632]{1,0:T(8,128)(2,1)}, bf16[64,5632]{1,0:T(8,128)(2,1)}, bf16[64,61...) custom-call(bf16[8,256,512]{2,1,0:T(8,128)(2,1)} %get-tuple-element., ...), custom_call_target="tpu_custom_call" | custom-call | tf_op jit(solution)/shard_map/pallas_call | solution.py:1220
  400.3 0.0 copy-start
  400.3 4.6 %shard_map.198 = (bf16[128,2048]{1,0:T(8,128)(2,1)}, f32[128,2048]{1,0:T(8,128)}, f32[64,6144]{1,0:T(8,128)}, f32[64,5632]{1,0:T(8,128)}, f32[64,5632]{1,0:T(8,1...) custom-call(bf16[128,2048]{1,0:T(8,128)(2,1)} %get-tuple-element.60.refs_0_, f32[128,2048]{1,0:T(8,128)} %get-tuple-element.61.refs_1_, ...), custom_call_target="tpu_custom_call" | custom-call | tf_op jit(solution)/shard_map/pallas_call | solution.py:1262
  404.9 0.0 copy-done
  404.9 0.1 reshape.60
  405.0 0.6 constant_dynamic-slice_fusion
  405.6 0.1 reshape.59
  405.7 0.6 constant_dynamic-slice_fusion.1
  (2 shorter events, 0.0 us)
Async XLA Ops:
  400.3 4.6 %copy-start = (f32[8,2048]{1,0:T(8,128)S(1)}, f32[8,2048]{1,0:T(8,128)}, u32[]{:S(2)}) copy-start(f32[8,2048]{1,0:T(8,128)} %get-tuple-element.70) | copy-start | bytes 196612

commit v10 on v9

--- a/solution.py
+++ b/solution.py
@@ -549,10 +549,10 @@
             here = pl.ds(at, n)
             tok[:, here] = plain(m[:, :hidden], wd[:, here]).astype(BF16)
 
+        over_tiles(width, 256, result_tile)
         share_left[1].wait_recv()
         other_left = left1.at[:, quarter_of(left2, across)]
         forward_left = links.to({"dp": near}, other_left, other_left)
-        over_tiles(width, 256, result_tile)
         put_pout = links.here(tok, pout_o)
         for copy in (share_dyp[0], forward_dyp, share_left[0], forward_left):
             copy.wait_recv()
@@ -1057,7 +1057,6 @@
                 get_wq.append(strips(i + 2))
         sum1 = GroupSum(links, dp, nd, rows, part, ra, rb)
         send_qkv()
-        down.start(1)
         for copy in (shared_left[0], forward_left):
             copy.wait_recv()
 
@@ -1099,6 +1098,7 @@
             to_owner(s_qkv, ((qkv_o, j * cols, j * width, cols, cols),))
 
         compute_qkv(1)
+        down.start(1)
         close_gu(gu[0], ranges[0])
         close_gu(up, range_z)
         if bits > 1:

time: 412 us -> 412 us (level)
  no operation moved by 1% of the time
where the time goes in v10:
time: 412 us; the launch traced here: 406 us
  Pallas kernels  402 us (98%)
    pallas_call x1, Pallas kernels, backward(): pl.pallas_call(body, out_shape=[shape(*o) for o in outs], in_specs=[anywh...  225 us
    pallas_call x1, Pallas kernels, forward(): pl.pallas_call(body, out_shape=[shape(*o) for o in outs.values()], in_spe...  173 us

profile of v10, /device:TPU:0, one launch (start us, length us, event | category | flops | bytes accessed | tf_op | source)
XLA Modules:
  0.0 406.5 jit_solution(18262814630387670490)
XLA Ops:
  0.6 0.7 copy.22
  1.3 1.3 fusion.4.small_i
  2.6 172.9 %shard_map.196 = (bf16[8,256,512]{2,1,0:T(8,128)(2,1)}, bf16[512,2048]{1,0:T(8,128)(2,1)}, bf16[2048,1536]{1,0:T(8,128)(2,1)}, bf16[1024,768]{1,0:T(8,128)(2,1)}...) custom-call(bf16[128,2048]{1,0:T(8,128)(2,1)} %bitcast.17, ...), custom_call_target="tpu_custom_call" | custom-call | tf_op jit(solution)/shard_map/pallas_call | solution.py:621
  175.5 224.8 %shard_map.197 = (bf16[128,2048]{1,0:T(8,128)(2,1)}, f32[128,2048]{1,0:T(8,128)}, bf16[64,5632]{1,0:T(8,128)(2,1)}, bf16[64,5632]{1,0:T(8,128)(2,1)}, bf16[64,61...) custom-call(bf16[8,256,512]{2,1,0:T(8,128)(2,1)} %get-tuple-element., ...), custom_call_target="tpu_custom_call" | custom-call | tf_op jit(solution)/shard_map/pallas_call | solution.py:1220
  400.3 0.0 copy-start
  400.3 4.6 %shard_map.198 = (bf16[128,2048]{1,0:T(8,128)(2,1)}, f32[128,2048]{1,0:T(8,128)}, f32[64,6144]{1,0:T(8,128)}, f32[64,5632]{1,0:T(8,128)}, f32[64,5632]{1,0:T(8,1...) custom-call(bf16[128,2048]{1,0:T(8,128)(2,1)} %get-tuple-element.60.refs_0_, f32[128,2048]{1,0:T(8,128)} %get-tuple-element.61.refs_1_, ...), custom_call_target="tpu_custom_call" | custom-call | tf_op jit(solution)/shard_map/pallas_call | solution.py:1262
  404.9 0.0 copy-done
  404.9 0.1 reshape.60
  405.0 0.6 constant_dynamic-slice_fusion
  405.6 0.1 reshape.59
  405.7 0.6 constant_dynamic-slice_fusion.1
  (2 shorter events, 0.0 us)
Async XLA Ops:
  400.3 4.6 %copy-start = (f32[8,2048]{1,0:T(8,128)S(1)}, f32[8,2048]{1,0:T(8,128)}, u32[]{:S(2)}) copy-start(f32[8,2048]{1,0:T(8,128)} %get-tuple-element.70) | copy-start | bytes 196612
